TPU v7x, 512 devices: a whole 4x8x8 slice. The times are simulated.
512 devices in a mesh: band: 64 (over y, z), fld: 8 (over x, core).
Axes of the slice: x: 4, y: 8, z: 8, core: 2. Of those that a mesh axis runs over, the one named last changes fastest.
Arguments:
- grid: bfloat16 [8, 64, 256, 2596], P('fld', 'band'), may hold values from -6 to 6
- pair_ids: int32 [8, 64], P('fld', 'band'), may hold values from 0 to 319, as said below
- trims: int32 [8, 64, 2], P('fld', 'band'), may hold values from 0 to 79
- weights: float32 [8, 64, 2], P('fld', 'band'), may hold values from 100 to 1000
- wavenumbers: int32 [640], replicated, may hold values from 0 to 639, as said below
- legendre: bfloat16 [320, 1024, 641], P('band', 'fld'), may hold values from -0.03125 to 0.03125
- damping: float32 [640], replicated, may hold values from 0.1 to 1
Outputs:
- spectrum: bfloat16 [320, 2, 256, 641], P('band', None, 'fld')
- restored: bfloat16 [8, 64, 256, 2596], P('fld', 'band')
Inputs may be any that keep to these rules, and one draw needn't show every extreme that they name: `pair_ids`: pair index i of each slot; its cycles have 20 + 4 i and 20 + 4 (639 - i) points. `wavenumbers`: entries 2 q and 2 q + 1 sum to 639; each wavenumber appears once.
All inputs are finite; a program needn't handle non-finite values.
Results may differ from a plain program's by a relative error of at most 0.02.
Values may be sent and summed in bfloat16 or wider, within the bound.
No kernel may reach another device: no remote copies, remote signals or barrier semaphores. Data moves between devices by JAX's collectives and lax.ppermute only.
A program may use at most 64 MiB of HBM per device.

v0:
```python
import jax
import jax.numpy as jnp
from jax import lax
from jax.sharding import PartitionSpec as P

TWO_PI = 6.283185307179586
BLOCK_ROWS = 128


def padded_table(first_count, limit_pair, wavenumbers, length, padded_length):
    row_index = jnp.arange(padded_length, dtype=jnp.int32)
    in_second = row_index >= first_count
    local_index = jnp.where(in_second, row_index - first_count, row_index)
    cycle_count = jnp.where(in_second, length - first_count, first_count)
    cycle_limit = jnp.where(in_second, limit_pair[1], limit_pair[0])
    residue = local_index[:, None] * wavenumbers[None, :] % cycle_count[:, None]
    angles = TWO_PI * (residue.astype(jnp.float32) / cycle_count[:, None].astype(jnp.float32))
    kept_mask = (wavenumbers[None, :] <= cycle_limit[:, None]) & (row_index < length)[:, None]
    cosine = jnp.where(kept_mask, jnp.cos(angles), 0.0)
    minus_sine = jnp.where(kept_mask, -jnp.sin(angles), 0.0)
    return jnp.concatenate([cosine, minus_sine], axis=1).astype(jnp.bfloat16)


def slot_layout(slot, full_blocks, straddle, has_split, first_count):
    is_extra = slot >= full_blocks
    block_index = jnp.where(is_extra, straddle, slot)
    row_start = block_index * BLOCK_ROWS
    owner_cycle = jnp.where(is_extra, 1, (row_start >= first_count).astype(jnp.int32))
    positions = row_start + jnp.arange(BLOCK_ROWS, dtype=jnp.int32)
    row_mask = ((positions >= first_count).astype(jnp.int32) == owner_cycle) & (
        jnp.logical_not(is_extra) | has_split
    )
    return (row_start, owner_cycle, row_mask)


def on_device(grid, pair_ids, trims, weights, wavenumbers, legendre, damping):
    fields = grid.shape[2]
    length = grid.shape[3]
    columns = wavenumbers.shape[0]
    highest = columns - 1
    local_pairs = legendre.shape[0]
    packed = legendre.shape[2]
    full_blocks = -(-length // BLOCK_ROWS)
    padded_length = full_blocks * BLOCK_ROWS
    cycle_block = grid[0, 0]
    first_count = 20 + 4 * pair_ids[0, 0]
    degree_counts = jnp.stack([first_count, length - first_count])
    degree_limits = jnp.maximum(jnp.minimum(highest, degree_counts // 2 - 1) - trims[0, 0], 0)
    twiddles = padded_table(first_count, degree_limits, wavenumbers, length, padded_length)
    grid_rows = jnp.pad(cycle_block, ((0, 0), (0, padded_length - length)))
    straddle = first_count // BLOCK_ROWS
    has_split = first_count % BLOCK_ROWS != 0
    slot_order = jnp.arange(full_blocks + 1, dtype=jnp.int32)

    def forward_slot(totals, slot):
        row_start, owner_cycle, row_mask = slot_layout(
            slot, full_blocks, straddle, has_split, first_count
        )
        table_rows = lax.dynamic_slice_in_dim(twiddles, row_start, BLOCK_ROWS, 0)
        data_rows = lax.dynamic_slice_in_dim(grid_rows, row_start, BLOCK_ROWS, 1)
        data_rows = jnp.where(row_mask[None, :], data_rows, jnp.zeros_like(data_rows))
        product = lax.dot_general(
            table_rows, data_rows, (((0,), (1,)), ((), ())), preferred_element_type=jnp.float32
        )
        second_share = owner_cycle.astype(jnp.float32)
        return (totals + jnp.stack([product * (1.0 - second_share), product * second_share]), None)

    totals_init = jnp.zeros((2, 2 * columns, fields), jnp.float32)
    cycle_totals, _ = lax.scan(forward_slot, totals_init, slot_order)
    raw_sums = cycle_totals.transpose(1, 0, 2).reshape(2, columns, 2, fields)
    scaling = weights[0, 0] / degree_counts.astype(jnp.float32)
    coefficients = (raw_sums * scaling[None, None, :, None]).astype(jnp.bfloat16)
    coefficients = coefficients.reshape(2, columns // 2, 2, 2, fields)
    band_index = lax.axis_index("band")
    own_waves = lax.dynamic_slice_in_dim(wavenumbers, band_index * 2 * local_pairs, 2 * local_pairs)
    opening = own_waves.reshape(local_pairs, 2)[:, 0]
    packed_index = jnp.arange(packed, dtype=jnp.int32)
    first_part = packed_index[None, :] < (highest + 1 - opening)[:, None]
    padded = jnp.concatenate([damping, jnp.zeros((packed,), damping.dtype)])
    upper_rows = jax.vmap(lambda offset: lax.dynamic_slice_in_dim(padded, offset, packed))(opening)
    shifted = jnp.concatenate([damping[:1], damping])
    factors = jnp.where(first_part, upper_rows, shifted[None, :])
    products = jnp.einsum(
        "pqhgf,qgk->qhpfk",
        lax.all_to_all(coefficients, "band", split_axis=1, concat_axis=3, tiled=True),
        legendre,
        preferred_element_type=jnp.float32,
    )
    summed_local = jnp.where(first_part[:, None, None, :], products[:, 0], products[:, 1])
    totals = lax.psum(summed_local.astype(jnp.bfloat16), "fld").astype(jnp.float32)
    filtered = (totals * factors[:, None, None, :]).astype(jnp.bfloat16)
    field_share = fields // lax.axis_size("fld")
    spectrum = lax.dynamic_slice_in_dim(
        filtered, lax.axis_index("fld") * field_share, field_share, 2
    )
    nothing = jnp.zeros_like(filtered)
    head_mask = first_part[:, None, None, :]
    split_parts = jnp.stack(
        [jnp.where(head_mask, filtered, nothing), jnp.where(head_mask, nothing, filtered)], axis=1
    )
    products = jnp.einsum(
        "qhpfk,qgk->pqhgf", split_parts, legendre, preferred_element_type=jnp.float32
    )
    rebuilt = products.astype(jnp.bfloat16)
    returned = lax.all_to_all(rebuilt, "band", split_axis=3, concat_axis=1, tiled=True)
    doubling = jnp.where(wavenumbers == 0, 1.0, 2.0).astype(jnp.bfloat16)
    scaled = (returned.reshape(2, columns, 2, fields) * doubling[None, :, None, None]).reshape(
        2 * columns, 2, fields
    )

    def inverse_slot(rows_total, slot):
        row_start, owner_cycle, row_mask = slot_layout(
            slot, full_blocks, straddle, has_split, first_count
        )
        table_rows = lax.dynamic_slice_in_dim(twiddles, row_start, BLOCK_ROWS, 0)
        coefficient = jnp.where(owner_cycle == 1, scaled[:, 1], scaled[:, 0])
        product = lax.dot_general(
            coefficient, table_rows, (((0,), (1,)), ((), ())), preferred_element_type=jnp.float32
        )
        product = jnp.where(row_mask[None, :], product, 0.0)
        current = lax.dynamic_slice_in_dim(rows_total, row_start, BLOCK_ROWS, 1)
        return (lax.dynamic_update_slice_in_dim(rows_total, current + product, row_start, 1), None)

    rows_init = jnp.zeros((fields, padded_length), jnp.float32)
    rows_total, _ = lax.scan(inverse_slot, rows_init, slot_order)
    restored = rows_total[:, :length].astype(jnp.bfloat16)
    return (spectrum, restored.reshape(1, 1, fields, length))


def solution(mesh):
    placed = (
        P("fld", "band", None, None),
        P("fld", "band"),
        P("fld", "band", None),
        P("fld", "band", None),
        P(),
        P("band", "fld", None),
        P(),
    )
    return jax.shard_map(
        on_device,
        mesh=mesh,
        in_specs=placed,
        out_specs=(P("band", None, "fld", None), P("fld", "band", None, None)),
        check_vma=False,
    )
```

profile of v0, /device:TPU:1, one launch (start us, length us, event | category | flops | bytes accessed | tf_op | source)
XLA Modules:
  0.0 599.5 jit_solution(13791072665065535483)
XLA Ops:
  13.3 98.6 %select_convert_fusion.1 = (bf16[2688,640]{1,0:T(8,128)(2,1)S(1)}, bf16[2688,640]{1,0:T(8,128)(2,1)S(1)}) fusion(s32[640]{0:T(1024)S(1)} %copy-done.2, s32[2688]{0:T(1024)S(1)} %get-tuple-element.244, f32[2688]{0:T(1024)S(1)} %get-tuple-element.242, pred[2688]{0:T(1024)(128)(4,1)S(1)} %get-tuple-element.246, s32[2688]{0:T(1024)S(1)} %get-tuple-element.241, ...), kind=kLoop, calls=%fused_computation.34 | loop fusion | flops 30965760 | bytes 6932224 | tf_op jit(solution)/shard_map/convert.1
  117.7 151.0 %while.24 = (s32[]{:T(128)}, f32[2,1280,256]{2,1,0:T(8,128)}, s32[22]{0:T(128)S(1)}, s32[]{:T(128)}, bf16[2688,1280]{1,0:T(8,128)(2,1)}, /*index=5*/s32[]{:T(128...) while((s32[]{:T(128)}, f32[2,1280,256]{2,1,0:T(8,128)}, ...), condition=%wide.region_1.2_spmd.clone, body=%wide.region_0.1_spmd.clone.sunk | while | flops 86540944 | bytes 10881568 | solution.py:69
  126.1 3.8 maximum_add_fusion.2
  133.0 3.8 maximum_add_fusion.2
  140.0 3.8 maximum_add_fusion.2
  146.9 3.8 maximum_add_fusion.2
  153.8 3.8 maximum_add_fusion.2
  174.7 3.8 maximum_add_fusion.2
  195.5 3.8 maximum_add_fusion.2
  209.4 3.8 maximum_add_fusion.2
  216.3 3.8 maximum_add_fusion.2
  223.3 3.8 maximum_add_fusion.2
  230.2 3.8 maximum_add_fusion.2
  244.1 3.8 maximum_add_fusion.2
  264.9 3.8 maximum_add_fusion.2
  268.7 8.6 %copy.63 = f32[1280,2,256]{2,1,0:T(2,128)S(1)} copy(f32[1280,2,256]{2,0,1:T(8,128)} %bitcast.76) | data formatting | bytes 5242880 | tf_op jit(solution)/shard_map/transpose | solution.py:70
  280.6 17.1 %all-to-all-start = ((bf16[2,320,2,2,256]{4,3,2,0,1:T(2,128)(2,1)}), bf16[2,320,2,2,256]{4,3,2,0,1:T(2,128)(2,1)S(1)}, u32[]{:S(2)}, u32[]{:S(2)}) async-start(bf16[2,320,2,2,256]{4,3,2,0,1:T(2,128)(2,1)} %copy.65), calls=%async_computation | async-start | bytes 2621440 | tf_op jit(solution)/shard_map/all_to_all | solution.py:85
  298.2 31.8 %all-to-all-done = bf16[2,320,2,2,256]{4,3,2,0,1:T(2,128)(2,1)S(1)} async-done(((bf16[2,320,2,2,256]{4,3,2,0,1:T(2,128)(2,1)}), bf16[2,320,2,2,256]{4,3,2,0,1:T(2,128)(2,1)S(1)}, u32[]{:S(2)}, u32[]{:S(2)}) %all-to-all-start) | async-done | bytes 1310752 | tf_op jit(solution)/shard_map/all_to_all | solution.py:85
  337.1 7.2 %while.23 = (s32[]{:T(128)}, f32[1281]{0:T(1024)S(1)}, s32[5,1]{1,0:T(8,128)S(1)}, f32[5,641]{1,0:T(8,128)S(1)}, s32[]{:T(128)}, /*index=5*/s32[]{:T(128)}) while((s32[]{:T(128)}, f32[1281]{0:T(1024)S(1)}, s32[5,1]{1,0:T(8,128)S(1)}, f32[5,641]{1,0:T(8,128)S(1)}, s32[]{:T(128)}, /*index=5*/s32[]{:T(128)}) %tuple.76), condition=%wide.while_cond, body=%wide.while_body.sunk | while | flops 2 | bytes 15473 | solution.py:80
  345.1 68.4 %all-reduce.4.cloned.1.call-done = bf16[5,2,256,641]{2,3,1,0:T(8,128)(2,1)} async-done(((bf16[5,2,256,641]{2,3,1,0:T(8,128)(2,1)}), bf16[5,2,256,641]{2,3,1,0:T(8,128)(2,1)}) %all-reduce.4.cloned.1.call-update) | async-done | bytes 3281936 | tf_op jit(solution)/shard_map/psum | solution.py:90
  424.5 13.4 %all-to-all-start.1 = ((bf16[2,5,2,128,256]{4,0,2,1,3:T(2,128)(2,1)}), bf16[2,5,2,128,256]{4,0,2,1,3:T(2,128)(2,1)}, u32[]{:S(2)}, u32[]{:S(2)}) async-start(bf16[2,5,2,128,256]{4,0,2,1,3:T(2,128)(2,1)} %copy.71), calls=%async_computation.1 | async-start | bytes 2621440 | tf_op jit(solution)/shard_map/all_to_all | solution.py:105
  441.3 27.1 %all-to-all-done.1 = bf16[2,5,2,128,256]{4,0,2,1,3:T(2,128)(2,1)} async-done(((bf16[2,5,2,128,256]{4,0,2,1,3:T(2,128)(2,1)}), bf16[2,5,2,128,256]{4,0,2,1,3:T(2,128)(2,1)}, u32[]{:S(2)}, u32[]{:S(2)}) %all-to-all-start.1) | async-done | bytes 1310752 | tf_op jit(solution)/shard_map/all_to_all | solution.py:105
  470.8 4.3 bitcast_multiply_fusion
  477.1 112.6 %while.22 = (s32[]{:T(128)}, f32[256,2688]{0,1:T(8,128)}, s32[22]{0:T(128)S(1)}, s32[]{:T(128)}, s32[]{:T(128)}, /*index=5*/pred[]{:T(512)}, bf16[1280,2,256]{2,...) while((s32[]{:T(128)}, f32[256,2688]{0,1:T(8,128)}, ...), condition=%wide.region_4.5_spmd, body=%wide.region_3.4_spmd.sunk | while | flops 84279952 | bytes 2949648 | solution.py:125
  (301 shorter events, 209.3 us)
Async XLA Ops:
  7.2 324.6 %copy-start = (bf16[5,128,641]{1,2,0:T(8,128)(2,1)S(1)}, bf16[5,128,641]{1,2,0:T(8,128)(2,1)}, u32[]{:S(2)}) copy-start(bf16[5,128,641]{1,2,0:T(8,128)(2,1)} %param.16) | copy-start | bytes 2461444
  7.2 6.1 %copy-start.2 = (s32[640]{0:T(1024)S(1)}, s32[640]{0:T(1024)}, u32[]{:S(2)}) copy-start(s32[640]{0:T(1024)} %param.15) | copy-start | bytes 7684
  268.7 8.6 %copy-start.4 = (f32[1,1,2]{2,1,0:T(1,128)S(1)}, f32[1,1,2]{2,1,0:T(1,128)}, u32[]{:S(2)}) copy-start(f32[1,1,2]{2,1,0:T(1,128)} %param.14) | copy-start | bytes 28
  280.6 49.3 %all-to-all-start = ((bf16[2,320,2,2,256]{4,3,2,0,1:T(2,128)(2,1)}), bf16[2,320,2,2,256]{4,3,2,0,1:T(2,128)(2,1)S(1)}, u32[]{:S(2)}, u32[]{:S(2)}) async-start(bf16[2,320,2,2,256]{4,3,2,0,1:T(2,128)(2,1)} %copy.65), calls=%async_computation | async-start | bytes 2621440 | tf_op jit(solution)/shard_map/all_to_all | solution.py:85
  297.7 115.8 %all-reduce.4.cloned.1.call-start = ((), (), s32[]{:S(2)}) async-start(), calls=%async_computation.2 | async-start | bytes 6635520 | tf_op jit(solution)/shard_map/psum | solution.py:90
  335.9 0.7 copy-start.3
  416.9 1.8 copy-start.1
  424.5 43.9 %all-to-all-start.1 = ((bf16[2,5,2,128,256]{4,0,2,1,3:T(2,128)(2,1)}), bf16[2,5,2,128,256]{4,0,2,1,3:T(2,128)(2,1)}, u32[]{:S(2)}, u32[]{:S(2)}) async-start(bf16[2,5,2,128,256]{4,0,2,1,3:T(2,128)(2,1)} %copy.71), calls=%async_computation.1 | async-start | bytes 2621440 | tf_op jit(solution)/shard_map/all_to_all | solution.py:105
Sparse Core Ops, SparseCore 0:
  336.1 77.4 all-reduce.3
where the time goes:
time: 608 us; the launch traced here: 599 us
  other arithmetic  199 us (33%)
  waiting for transfers between devices  127 us (21%)
  local copies, waits for them, and re-layouts  106 us (17%)
  matrix products  65.2 us (11%)
  loops' own time  56.3 us (9%)
  starting transfers between devices  30.5 us (5%)
  between operations  15 us (2%)
    another operation x1, other arithmetic  98.6 us
    add x22, other arithmetic, forward_slot(): totals + jnp.stack([product * (1.0 - second_share), product * second_share])  82.2 us
    psum x1, waiting for transfers between devices, on_device(): lax.psum(summed_local.astype(jnp.bfloat16), 'fld').astype(jnp.float32)  68.4 us
    all_to_all x1, waiting for transfers between devices, on_device(): lax.all_to_all(coefficients, 'band', split_axis=1, concat_axis=3, tiled=T...  31.8 us
    dot_general x22, matrix products, inverse_slot(): lax.dot_general(coefficient, table_rows, (((0,), (1,)), ((), ())), prefer...  30.8 us
    another operation x1, loops' own time, on_device(): rows_total, _ = lax.scan(inverse_slot, rows_init, slot_order)  29.9 us
    dot_general x22, matrix products, forward_slot(): lax.dot_general(table_rows, data_rows, (((0,), (1,)), ((), ())), preferre...  29.4 us
    all_to_all x1, waiting for transfers between devices, on_device(): lax.all_to_all(rebuilt, 'band', split_axis=3, concat_axis=1, tiled=True)  27.1 us
  transfers between devices with their start and end apart: 3, of which 3 were waited for; matrix products, arithmetic and copies ran while one was open for 2% of the time, Pallas kernels for 0%

commit v1 on v0

v1 whole, which is shorter than its diff:
```python
import functools

import jax
import jax.numpy as jnp
from jax import lax
from jax.experimental import pallas as pl
from jax.experimental.pallas import tpu as pltpu
from jax.sharding import PartitionSpec as P

PI = 3.141592653589793
LANES = 128
BLOCK = 256
STRIP = 64
VMEM_BYTES = 40 * 1024 * 1024
CHUNKS = ((0, 5),)


def unit_circle(waves, points, count):
    inverse = 1.0 / count
    product = waves * points
    residue = product - jnp.round(product * inverse) * count
    half = residue * (inverse * PI)
    square = half * half
    sine = 1.0 / 6227020800.0
    for term in (-1.0 / 39916800.0, 1.0 / 362880.0, -1.0 / 5040.0, 1.0 / 120.0, -1.0 / 6.0, 1.0):
        sine = sine * square + term
    sine = sine * half
    cosine = 1.0 / 479001600.0
    for term in (-1.0 / 3628800.0, 1.0 / 40320.0, -1.0 / 720.0, 1.0 / 24.0, -0.5, 1.0):
        cosine = cosine * square + term
    return cosine * cosine - sine * sine, -2.0 * sine * cosine


def turn(state, step):
    cosine, sine = state
    return cosine * step[0] - sine * step[1], sine * step[0] + cosine * step[1]


def cycle_facts(length, highest, pair_ids, trims):
    first = 20 + 4 * pair_ids[0, 0]
    counts = (first, length - first)
    limits = [
        jnp.maximum(jnp.minimum(highest, count // 2 - 1) - trims[0, 0, cycle], 0)
        for cycle, count in enumerate(counts)
    ]
    return first, [c.astype(jnp.float32) for c in counts], [l.astype(jnp.float32) for l in limits]


def fill_table(axis, chosen, step_waves, facts, blocks, write):
    first, counts, limits = facts
    shape = chosen.shape
    lane = lax.broadcasted_iota(jnp.int32, shape, axis)
    straddle = first // LANES

    def begin(cycle, offset):
        state = unit_circle(chosen, (lane + offset).astype(jnp.float32), counts[cycle])
        kept = chosen <= limits[cycle]
        return tuple(jnp.where(kept, part, 0.0) for part in state)

    steps = step_waves(counts)

    def advance(cycle):
        def body(block, state):
            write(block, state)
            return turn(state, steps[cycle])

        return body

    state = lax.fori_loop(0, straddle, advance(0), begin(0, 0))
    offset = straddle * LANES - first
    later = begin(1, offset)
    before = lane + offset < 0
    write(straddle, tuple(jnp.where(before, old, new) for old, new in zip(state, later)))
    lax.fori_loop(straddle + 1, blocks, advance(1), turn(later, steps[1]))


def forward_kernel(highest, bands, pair_ids, trims, weights, waves, grid, packed, table, totals, columns, rows):
    length, fields = grid.shape
    width = waves.shape[1]
    quarter = width // 2
    facts = cycle_facts(length, highest, pair_ids, trims)
    first, counts, _ = facts
    blocks = -(-length // LANES)
    columns[...] = jnp.broadcast_to(waves[...].astype(jnp.float32), (LANES, width)).T

    for strip in range(width // STRIP):
        chosen = columns[strip * STRIP:(strip + 1) * STRIP, :]

        def step_waves(counts):
            cycle_lane = lax.broadcasted_iota(jnp.int32, chosen.shape, 1)
            count = jnp.where(cycle_lane == 0, counts[0], counts[1])
            cosine, sine = unit_circle(chosen, float(LANES), count)
            return [
                tuple(jnp.broadcast_to(part[:, c:c + 1], chosen.shape) for part in (cosine, sine))
                for c in range(2)
            ]

        def write(block, state):
            for part in range(2):
                table[
                    part * width + strip * STRIP:part * width + (strip + 1) * STRIP,
                    pl.ds(pl.multiple_of(block * LANES, LANES), LANES),
                ] = state[part].astype(jnp.bfloat16)

        fill_table(1, chosen, step_waves, facts, blocks, write)

    full = length // BLOCK
    straddle = first // BLOCK
    position = lax.broadcasted_iota(jnp.int32, (BLOCK, fields), 0)

    def product(start, size, data):
        return jnp.dot(table[:, pl.ds(start, size)], data, preferred_element_type=jnp.float32)

    def data_of(block):
        return grid[pl.ds(pl.multiple_of(block * BLOCK, BLOCK), BLOCK), :]

    def add(cycle):
        def body(block, carry):
            totals[cycle] += product(pl.multiple_of(block * BLOCK, BLOCK), BLOCK, data_of(block))
            return carry

        return body

    data = data_of(straddle)
    before = position + straddle * BLOCK < first
    nothing = jnp.zeros_like(data)
    start = pl.multiple_of(straddle * BLOCK, BLOCK)
    totals[0] = product(start, BLOCK, jnp.where(before, data, nothing))
    totals[1] = product(start, BLOCK, jnp.where(before, nothing, data))
    lax.fori_loop(0, straddle, add(0), 0)
    lax.fori_loop(straddle + 1, full, add(1), 0)
    totals[1] += product(full * BLOCK, length - full * BLOCK, grid[full * BLOCK:, :])

    share = LANES // 4
    for group in range(fields // share):
        lanes = slice(group * share, (group + 1) * share)
        for cycle in range(2):
            scale = jnp.full((1, LANES), weights[0, 0, cycle]) / counts[cycle]
            joined = jnp.concatenate(
                [totals[cycle, part * quarter:(part + 1) * quarter, lanes] for part in (0, 2, 1, 3)], axis=1
            )
            rows[pl.ds(cycle, quarter, stride=2), :] = joined * scale
        packed[group] = rows[...].astype(jnp.bfloat16)


def table_kernel(length, highest, pair_ids, trims, *refs):
    *waves, table = refs
    facts = cycle_facts(length, highest, pair_ids, trims)
    blocks = -(-length // LANES)
    base = 0
    for chunk in waves:
        width = chunk.shape[1]
        for tile in range(width // LANES):
            row = chunk[:, tile * LANES:(tile + 1) * LANES].astype(jnp.float32)
            chosen = jnp.broadcast_to(row, (LANES, LANES))

            def step_waves(counts):
                wide = jnp.broadcast_to(row, (8, LANES))
                return [
                    tuple(part[:1] for part in unit_circle(wide, float(LANES), count)) for count in counts
                ]

            def write(block, state):
                for part in range(2):
                    left = base + part * width + tile * LANES
                    table[pl.ds(pl.multiple_of(block * LANES, LANES), LANES), left:left + LANES] = (
                        state[part].astype(jnp.bfloat16)
                    )

            fill_table(0, chosen, step_waves, facts, blocks, write)
        base += 2 * width


def legendre_kernel(start, highest, band, wavenumbers, values, legendre, damping, *refs):
    spectrum, rebuilt = refs[-2:]
    groups, _, degrees, each = legendre.shape
    matrix = jnp.concatenate([legendre[group, 0] for group in range(groups)], axis=1)
    sums = lax.dot_general(
        values[0].T, matrix, (((1,), (1,)), ((), ())), preferred_element_type=jnp.float32
    )
    fields = sums.shape[0] // 2
    pair = band[0] + start + pl.program_id(0)
    first_wave = wavenumbers[2 * pair]
    second_wave = wavenumbers[2 * pair + 1]
    width = damping.shape[1]
    degree = lax.broadcasted_iota(jnp.int32, (1, width), 1)
    kept = degree < highest + 1 - first_wave
    upper = pltpu.roll(damping[...], lax.rem(width - first_wave, width), 1)
    lower = pltpu.roll(damping[...], 1, 1)
    factor = jnp.where(kept, upper[:1], lower[:1])[:, :degrees]
    head = jnp.broadcast_to(kept[:, :degrees], (fields, degrees))
    filtered = (jnp.where(head, sums[:fields], sums[fields:]) * factor).astype(jnp.bfloat16)
    spectrum[0] = filtered
    nothing = jnp.zeros_like(filtered)
    parts = jnp.concatenate([jnp.where(head, filtered, nothing), jnp.where(head, nothing, filtered)], axis=0)
    products = jnp.dot(parts, matrix, preferred_element_type=jnp.float32)
    row = lax.broadcasted_iota(jnp.int32, products.shape, 0)
    wave = jnp.where(row < fields, first_wave, second_wave)
    doubled = products * jnp.where(wave == 0, 1.0, 2.0)
    rebuilt[0] = doubled.astype(jnp.bfloat16).T


def inverse_kernel(chunks, pair_ids, *refs):
    values = refs[:chunks]
    table, restored, rows, factors = refs[chunks:]
    block = pl.program_id(0)
    first = 20 + 4 * pair_ids[0, 0]
    share = LANES // 4

    @pl.when(block == 0)
    def _():
        base = 0
        for chunk in values:
            groups, height, _ = chunk.shape
            quarter = height // 2
            for side in range(groups // 4):
                for near in range(4):
                    rows[near, :height] = chunk[4 * side + near].astype(jnp.float32)
                for cycle in range(2):
                    turned = [
                        rows[near, pl.ds(cycle, quarter, stride=2), :].astype(jnp.bfloat16) for near in range(4)
                    ]
                    for part in range(4):
                        source = (0, 2, 1, 3)[part] * share
                        factors[
                            cycle,
                            base + part * quarter:base + (part + 1) * quarter,
                            side * LANES:(side + 1) * LANES,
                        ] = jnp.concatenate([one[:, source:source + share] for one in turned], axis=1)
            base += 4 * quarter

    def product(cycle):
        return jnp.dot(table[...], factors[cycle], preferred_element_type=jnp.float32)

    start = block * BLOCK
    end = start + BLOCK

    @pl.when(end <= first)
    def _():
        restored[...] = product(0).astype(jnp.bfloat16)

    @pl.when(start >= first)
    def _():
        restored[...] = product(1).astype(jnp.bfloat16)

    @pl.when((start < first) & (end > first))
    def _():
        position = start + lax.broadcasted_iota(jnp.int32, restored.shape, 0)
        restored[...] = jnp.where(position < first, product(0), product(1)).astype(jnp.bfloat16)


SMEM = pl.BlockSpec(memory_space=pltpu.SMEM)
VMEM = pl.BlockSpec(memory_space=pltpu.VMEM)


def parameters(*semantics):
    return pltpu.CompilerParams(dimension_semantics=semantics or None, vmem_limit_bytes=VMEM_BYTES)


def forward_call(highest, bands, pair_ids, trims, weights, waves, points):
    length, fields = points.shape
    width = waves.shape[1]
    blocks = -(-length // BLOCK)
    return pl.pallas_call(
        functools.partial(forward_kernel, highest, bands),
        in_specs=[SMEM, SMEM, SMEM, VMEM, VMEM],
        out_specs=VMEM,
        out_shape=jax.ShapeDtypeStruct((4 * fields // LANES, width, LANES), jnp.bfloat16),
        scratch_shapes=[
            pltpu.VMEM((2 * width, blocks * BLOCK), jnp.bfloat16),
            pltpu.VMEM((2, 2 * width, fields), jnp.float32),
            pltpu.VMEM((width, LANES), jnp.float32),
            pltpu.VMEM((width, LANES), jnp.float32),
        ],
        compiler_params=parameters(),
        cost_estimate=pl.CostEstimate(
            flops=2 * length * fields * 2 * width, bytes_accessed=length * fields * 2, transcendentals=0
        ),
        name="forward_dft",
    )(pair_ids, trims, weights, waves, points)


def table_call(highest, length, pair_ids, trims, chunk_waves):
    blocks = -(-length // BLOCK)
    total = 2 * sum(waves.shape[1] for waves in chunk_waves)
    return pl.pallas_call(
        functools.partial(table_kernel, length, highest),
        in_specs=[SMEM, SMEM] + [VMEM] * len(chunk_waves),
        out_specs=VMEM,
        out_shape=jax.ShapeDtypeStruct((blocks * BLOCK, total), jnp.bfloat16),
        compiler_params=parameters(),
        cost_estimate=pl.CostEstimate(flops=8 * length * total, bytes_accessed=2 * length * total, transcendentals=0),
        name="inverse_table",
    )(pair_ids, trims, *chunk_waves)


def legendre_call(highest, start, band, wavenumbers, values, gathered, damping, spectrum):
    groups, local_pairs, degrees, each = gathered.shape
    count, cycles, _ = values.shape
    fields = LANES // 2
    previous = [] if spectrum is None else [spectrum]
    return pl.pallas_call(
        functools.partial(legendre_kernel, start, highest),
        grid=(count,),
        in_specs=[
            SMEM,
            SMEM,
            pl.BlockSpec((1, cycles, LANES), lambda q: (q, 0, 0)),
            pl.BlockSpec((groups, 1, degrees, each), lambda q: (0, q + start, 0, 0)),
            pl.BlockSpec(damping.shape, lambda q: (0, 0)),
        ]
        + [pl.BlockSpec(memory_space=pl.ANY)] * len(previous),
        out_specs=[
            pl.BlockSpec((1, fields, degrees), lambda q: (q + start, 0, 0)),
            pl.BlockSpec((1, cycles, LANES), lambda q: (q, 0, 0)),
        ],
        out_shape=[
            jax.ShapeDtypeStruct((local_pairs, fields, degrees), jnp.bfloat16),
            jax.ShapeDtypeStruct((count, cycles, LANES), jnp.bfloat16),
        ],
        input_output_aliases={5: 0} if previous else {},
        compiler_params=parameters("arbitrary"),
        cost_estimate=pl.CostEstimate(
            flops=4 * count * cycles * LANES * degrees,
            bytes_accessed=2 * count * cycles * degrees,
            transcendentals=0,
        ),
        name="legendre_both_ways",
    )(band, wavenumbers, values, gathered, damping, *previous)


def inverse_call(length, fields, pair_ids, values, table):
    blocks = -(-length // BLOCK)
    total = table.shape[1]
    return pl.pallas_call(
        functools.partial(inverse_kernel, len(values)),
        grid=(blocks,),
        in_specs=[SMEM]
        + [pl.BlockSpec(one.shape, lambda i: (0, 0, 0)) for one in values]
        + [pl.BlockSpec((BLOCK, total), lambda i: (i, 0))],
        out_specs=pl.BlockSpec((BLOCK, fields), lambda i: (i, 0)),
        out_shape=jax.ShapeDtypeStruct((length, fields), jnp.bfloat16),
        scratch_shapes=[
            pltpu.VMEM((4, max(one.shape[1] for one in values), LANES), jnp.float32),
            pltpu.VMEM((2, total, fields), jnp.bfloat16),
        ],
        compiler_params=parameters("arbitrary"),
        cost_estimate=pl.CostEstimate(
            flops=2 * length * fields * total, bytes_accessed=2 * length * (fields + total), transcendentals=0
        ),
        name="inverse_dft",
    )(pair_ids, *values, table)


def on_device(grid, pair_ids, trims, weights, wavenumbers, legendre, damping):
    fields, length = grid.shape[2:]
    columns = wavenumbers.shape[0]
    highest = columns - 1
    local_pairs, local_cycles, degrees = legendre.shape
    groups = lax.axis_size("fld")
    bands = lax.axis_size("band")
    gathered = lax.all_gather(legendre.swapaxes(1, 2), "fld")
    points = grid[0, 0].T
    by_band = wavenumbers.reshape(bands, local_pairs, 2)
    chunk_waves = [
        by_band[:, start:end].transpose(2, 0, 1).reshape(1, 2 * bands * (end - start)) for start, end in CHUNKS
    ]
    padding = -(-degrees // LANES) * LANES - columns
    padded = jnp.broadcast_to(jnp.pad(damping, (0, padding))[None, :], (8, columns + padding))
    band = (lax.axis_index("band") * local_pairs).astype(jnp.int32).reshape(1)

    arrived = []
    for (start, end), waves in zip(CHUNKS, chunk_waves):
        packed = forward_call(highest, bands, pair_ids, trims, weights, waves, points)
        packed = packed.reshape(groups * bands, end - start, 2, LANES)
        arrived.append(lax.all_to_all(packed, ("fld", "band"), split_axis=0, concat_axis=0, tiled=True))
    table = table_call(highest, length, pair_ids, trims, chunk_waves)
    spectrum = None
    returned = []
    for (start, end), message in zip(CHUNKS, arrived):
        values = message.transpose(1, 0, 2, 3).reshape(end - start, groups * local_cycles, LANES)
        spectrum, rebuilt = legendre_call(
            highest, start, band, wavenumbers, values, gathered, padded, spectrum
        )
        leaving = rebuilt.reshape(end - start, groups * bands, 2, LANES).transpose(1, 0, 2, 3)
        message = lax.all_to_all(leaving, ("fld", "band"), split_axis=0, concat_axis=0, tiled=True)
        returned.append(message.reshape(groups, bands * (end - start) * 2, LANES))
    restored = inverse_call(length, fields, pair_ids, returned, table)
    return (
        spectrum.reshape(local_pairs, 2, fields // groups, degrees),
        restored.T.reshape(1, 1, fields, length),
    )


def solution(mesh):
    placed = (
        P("fld", "band", None, None),
        P("fld", "band"),
        P("fld", "band", None),
        P("fld", "band", None),
        P(),
        P("band", "fld", None),
        P(),
    )
    return jax.shard_map(
        on_device,
        mesh=mesh,
        in_specs=placed,
        out_specs=(P("band", None, "fld", None), P("fld", "band", None, None)),
        check_vma=False,
    )
```

time: 608 us -> 163 us (0.27); the launches traced: 599 us -> 163 us
  other arithmetic: 199 us -> 0 us
  local copies, waits for them, and re-layouts: 106 us -> 13.3 us
  matrix products: 65.2 us -> 0 us
  loops' own time: 56.3 us -> 0 us
  waiting for transfers between devices: 127 us -> 73.4 us
  Pallas kernels: 0 us -> 29.9 us
    another operation x3 -> x0, other arithmetic: 103 us -> none
    add x22 -> x0, other arithmetic: 82.2 us -> none  [forward_slot(): totals + jnp.stack([product * (1.0 - second_share), product * second_share])]
    psum x1 -> x0, waiting for transfers between devices: 68.4 us -> none  [on_device(): lax.psum(summed_local.astype(jnp.bfloat16), 'fld').astype(jnp.float32)]
    dot_general x46 -> x0, matrix products: 65.2 us -> none  [the longest x22 30.8 us: inverse_slot(): lax.dot_general(coefficient, table_rows, (((0,), (1,)), ((), ())), prefer...]
    another operation x3 -> x0, loops' own time: 56.3 us -> none  [the longest x1 29.9 us: on_device(): rows_total, _ = lax.scan(inverse_slot, rows_init, slot_order)]
    dynamic_slice x90 -> x0, local copies, waits for them, and re-layouts: 49.8 us -> none  [the longest x44 25.7 us: on_device(): cycle_totals, _ = lax.scan(forward_slot, totals_init, slot_order)]
    pallas_call x0 -> x4, Pallas kernels: none -> 29.9 us  [the longest x1 12.1 us: forward_call(): pl.pallas_call(functools.partial(forward_kernel, highest, bands), in_spec...]
    dynamic_update_slice x44 -> x0, local copies, waits for them, and re-layouts: 16.7 us -> none  [inverse_slot(): lax.dynamic_update_slice_in_dim(rows_total, current + product, row_start, 1)]
  transfers between devices with their start and end apart: 3 -> 3, of which waited for: 3 -> 2; matrix products, arithmetic and copies ran while one was open for 2% -> 2% of each run, Pallas kernels for 0% -> 10%
where the time goes in v1:
time: 163 us
  waiting for transfers between devices  73.4 us (45%)
  starting transfers between devices  31.4 us (19%)
  Pallas kernels  29.9 us (18%)
  between operations  14.8 us (9%)
  local copies, waits for them, and re-layouts  13.3 us (8%)
    all_to_all x1, waiting for transfers between devices, on_device(): lax.all_to_all(packed, ('fld', 'band'), split_axis=0, concat_axis=0, tile...  39.7 us
    all_to_all x1, waiting for transfers between devices, on_device(): lax.all_to_all(leaving, ('fld', 'band'), split_axis=0, concat_axis=0, til...  32.9 us
    all_to_all x1, starting transfers between devices, on_device(): lax.all_to_all(packed, ('fld', 'band'), split_axis=0, concat_axis=0, tile...  22.1 us
    pallas_call x1, Pallas kernels, forward_call(): pl.pallas_call(functools.partial(forward_kernel, highest, bands), in_spec...  12.1 us
    all_to_all x1, starting transfers between devices, on_device(): lax.all_to_all(leaving, ('fld', 'band'), split_axis=0, concat_axis=0, til...  9.23 us
    unnamed x16, local copies, waits for them, and re-layouts  8.84 us
    pallas_call x1, Pallas kernels, inverse_call(): pl.pallas_call(functools.partial(inverse_kernel, len(values)), grid=(bloc...  7.31 us
    pallas_call x1, Pallas kernels, legendre_call(): pl.pallas_call(functools.partial(legendre_kernel, start, highest), grid=(...  6.61 us
  transfers between devices with their start and end apart: 3, of which 2 were waited for; matrix products, arithmetic and copies ran while one was open for 2% of the time, Pallas kernels for 10%

profile of v1, /device:TPU:1, one launch (start us, length us, event | category | flops | bytes accessed | tf_op | source)
XLA Modules:
  0.0 162.7 jit_solution(14946273402345830047)
XLA Ops:
  7.2 0.0 copy-start.4
  7.2 0.0 copy-start.6
  7.2 0.0 copy-start.5
  7.2 0.0 all-gather.3.cloned.1.call-start
  7.2 0.7 all-gather.3.cloned.1.call-update
  8.6 0.8 reshape.33
  9.4 0.5 copy.14
  9.9 0.2 reshape.34.waves.refs_0_
  10.2 12.1 %forward_dft.1 = bf16[8,640,128]{2,1,0:T(8,128)(2,1)} custom-call(s32[1,1]{1,0:T(1,128)S(6)} %copy.19.pair_ids, s32[1,1,2]{2,1,0:T(1,128)S(1)} %copy-done.4, f32[1,1,2]{2,1,0:T(1,128)S(1)} %copy-done.6, s32[1,640]{1,0:T(1,128)S(1)} %reshape.34.waves.refs_0_, bf16[2596,256]{1,0:T(8,128)(2,1)S(1)} %bitcast.23), custom_call_target="tpu_custom_call" | custom-call | flops 1701314560 | bytes 1329152 | tf_op jit(solution)/shard_map/forward_dft/pallas_call | solution.py:264
  22.2 22.1 %all-to-all-start = ((bf16[512,5,2,128]{3,2,1,0:T(2,128)(2,1)}), bf16[512,5,2,128]{3,2,1,0:T(2,128)(2,1)S(1)}, u32[]{:S(2)}, u32[]{:S(2)}) async-start(bf16[512,5,2,128]{3,2,1,0:T(2,128)(2,1)} %bitcast.4), calls=%async_computation | async-start | bytes 2621440 | tf_op jit(solution)/shard_map/all_to_all | solution.py:376
  44.4 39.7 %all-to-all-done = bf16[512,5,2,128]{3,2,1,0:T(2,128)(2,1)S(1)} async-done(((bf16[512,5,2,128]{3,2,1,0:T(2,128)(2,1)}), bf16[512,5,2,128]{3,2,1,0:T(2,128)(2,1)S(1)}, u32[]{:S(2)}, u32[]{:S(2)}) %all-to-all-start) | async-done | bytes 1310752 | tf_op jit(solution)/shard_map/all_to_all | solution.py:376
  84.1 0.9 copy.15
  85.0 0.0 all-gather.3.cloned.1.call-done
  85.0 0.0 copy-done.3
  85.0 0.0 copy-start.2
  85.0 2.9 %copy-done.2 = bf16[40,641,128]{2,1,0:T(8,128)(2,1)S(1)} copy-done((bf16[40,641,128]{2,1,0:T(8,128)(2,1)S(1)}, bf16[40,641,128]{2,1,0:T(8,128)(2,1)}, u32[]{:S(2)}) %copy-start.2) | copy-done | bytes 6563864
  87.9 6.6 %legendre_both_ways.1 = (bf16[5,64,641]{2,1,0:T(8,128)(2,1)}, bf16[5,1024,128]{2,1,0:T(8,128)(2,1)S(1)}) custom-call(s32[1]{0:T(128)} %bitcast.band, s32[640]{0:T(1024)S(1)} %copy-done.3, bf16[5,1024,128]{2,1,0:T(8,128)(2,1)S(1)} %bitcast.21, bf16[8,5,641,128]{3,2,1,0:T(8,128)(2,1)S(1)} %bitcast.19, f32[8,768]{1,0:T(8,128)S(1)} %broadcast_in_dim.2.damping), custom_call_target="tpu_custom_call" | custom-call | flops 1680343040 | bytes 6563840 | tf_op jit(solution)/shard_map/legendre_both_ways/pallas_call | solution.py:302
  94.5 2.0 %copy.18 = bf16[5,512,2,128]{3,2,0,1:T(2,128)(2,1)} copy(bf16[5,512,2,128]{3,2,1,0:T(2,128)(2,1)S(1)} %bitcast.22) | data formatting | bytes 2621440 | tf_op jit(solution)/shard_map/reshape | solution.py:385
  96.5 9.2 %all-to-all-start.1 = ((bf16[512,5,2,128]{3,2,1,0:T(2,128)(2,1)}), bf16[512,5,2,128]{3,2,1,0:T(2,128)(2,1)S(1)}, u32[]{:S(2)}, u32[]{:S(2)}) async-start(bf16[512,5,2,128]{3,2,1,0:T(2,128)(2,1)} %bitcast.18), calls=%async_computation.1 | async-start | bytes 2621440 | tf_op jit(solution)/shard_map/all_to_all | solution.py:386
  105.7 3.9 %inverse_table.1.refs_1_ = bf16[2816,1280]{1,0:T(8,128)(2,1)S(1)} custom-call(s32[1,1]{1,0:T(1,128)S(6)} %copy.19.pair_ids, s32[1,1,2]{2,1,0:T(1,128)S(1)} %copy-done.4, s32[1,640]{1,0:T(1,128)S(1)} %reshape.34.waves.refs_0_), custom_call_target="tpu_custom_call" | custom-call | flops 26583040 | bytes 6645760 | tf_op jit(solution)/shard_map/inverse_table/pallas_call | solution.py:286
  109.6 2.9 %copy-done = bf16[2816,1280]{1,0:T(8,128)(2,1)} copy-done((bf16[2816,1280]{1,0:T(8,128)(2,1)}, bf16[2816,1280]{1,0:T(8,128)(2,1)S(1)}, u32[]{:S(2)}) %copy-start) | copy-done | bytes 7208984
  112.5 32.9 %all-to-all-done.1 = bf16[512,5,2,128]{3,2,1,0:T(2,128)(2,1)S(1)} async-done(((bf16[512,5,2,128]{3,2,1,0:T(2,128)(2,1)}), bf16[512,5,2,128]{3,2,1,0:T(2,128)(2,1)S(1)}, u32[]{:S(2)}, u32[]{:S(2)}) %all-to-all-start.1) | async-done | bytes 1310752 | tf_op jit(solution)/shard_map/all_to_all | solution.py:386
  145.5 3.0 %copy-done.1 = bf16[2816,1280]{1,0:T(8,128)(2,1)S(1)} copy-done((bf16[2816,1280]{1,0:T(8,128)(2,1)S(1)}, bf16[2816,1280]{1,0:T(8,128)(2,1)}, u32[]{:S(2)}) %copy-start.1) | copy-done | bytes 7208984
  148.5 7.3 %inverse_dft.1 = bf16[2596,256]{1,0:T(8,128)(2,1)} custom-call(s32[1,1]{1,0:T(1,128)S(6)} %copy.19.pair_ids, bf16[8,640,128]{2,1,0:T(8,128)(2,1)S(1)} %bitcast.20, bf16[2816,1280]{1,0:T(8,128)(2,1)S(1)} %copy-done.1), custom_call_target="tpu_custom_call" | custom-call | flops 1701314560 | bytes 7974912 | tf_op jit(solution)/shard_map/inverse_dft/pallas_call | solution.py:335
  (10 shorter events, 0.0 us)
Async XLA Ops:
  7.2 3.0 %copy-start.4 = (s32[1,1,2]{2,1,0:T(1,128)S(1)}, s32[1,1,2]{2,1,0:T(1,128)}, u32[]{:S(2)}) copy-start(s32[1,1,2]{2,1,0:T(1,128)} %trims.3) | copy-start | bytes 28
  7.2 3.0 %copy-start.6 = (f32[1,1,2]{2,1,0:T(1,128)S(1)}, f32[1,1,2]{2,1,0:T(1,128)}, u32[]{:S(2)}) copy-start(f32[1,1,2]{2,1,0:T(1,128)} %weights.1) | copy-start | bytes 28
  7.2 3.0 %copy-start.5 = (bf16[1,1,256,2596]{2,3,1,0:T(8,128)(2,1)S(1)}, bf16[1,1,256,2596]{2,3,1,0:T(8,128)(2,1)}, u32[]{:S(2)}) copy-start(bf16[1,1,256,2596]{2,3,1,0:T(8,128)(2,1)} %param.7) | copy-start | bytes 3987460
  7.2 77.8 %all-gather.3.cloned.1.call-start = ((), (), s32[]{:S(2)}) async-start(), calls=%async_computation.2 | async-start | bytes 7464960 | tf_op jit(solution)/shard_map/all_gather | solution.py:362
  22.2 22.1 %copy-start.7 = (f32[640]{0:T(1024)S(1)}, f32[640]{0:T(1024)}, u32[]{:S(2)}) copy-start(f32[640]{0:T(1024)} %param.13) | copy-start | bytes 7684
  22.2 61.9 %all-to-all-start = ((bf16[512,5,2,128]{3,2,1,0:T(2,128)(2,1)}), bf16[512,5,2,128]{3,2,1,0:T(2,128)(2,1)S(1)}, u32[]{:S(2)}, u32[]{:S(2)}) async-start(bf16[512,5,2,128]{3,2,1,0:T(2,128)(2,1)} %bitcast.4), calls=%async_computation | async-start | bytes 2621440 | tf_op jit(solution)/shard_map/all_to_all | solution.py:376
  84.1 0.9 copy-start.3
  85.0 2.9 %copy-start.2 = (bf16[40,641,128]{2,1,0:T(8,128)(2,1)S(1)}, bf16[40,641,128]{2,1,0:T(8,128)(2,1)}, u32[]{:S(2)}) copy-start(bf16[40,641,128]{2,1,0:T(8,128)(2,1)} %all-gather.3.cloned.1.call-done) | copy-start | bytes 19691524
  96.5 49.0 %all-to-all-start.1 = ((bf16[512,5,2,128]{3,2,1,0:T(2,128)(2,1)}), bf16[512,5,2,128]{3,2,1,0:T(2,128)(2,1)S(1)}, u32[]{:S(2)}, u32[]{:S(2)}) async-start(bf16[512,5,2,128]{3,2,1,0:T(2,128)(2,1)} %bitcast.18), calls=%async_computation.1 | async-start | bytes 2621440 | tf_op jit(solution)/shard_map/all_to_all | solution.py:386
  109.6 2.9 %copy-start = (bf16[2816,1280]{1,0:T(8,128)(2,1)}, bf16[2816,1280]{1,0:T(8,128)(2,1)S(1)}, u32[]{:S(2)}) copy-start(bf16[2816,1280]{1,0:T(8,128)(2,1)S(1)} %inverse_table.1.refs_1_) | copy-start | bytes 21626884
  145.5 3.0 %copy-start.1 = (bf16[2816,1280]{1,0:T(8,128)(2,1)S(1)}, bf16[2816,1280]{1,0:T(8,128)(2,1)}, u32[]{:S(2)}) copy-start(bf16[2816,1280]{1,0:T(8,128)(2,1)} %copy-done) | copy-start | bytes 21626884
Sparse Core Ops, SparseCore 0:
  10.2 65.3 all-gather.2

commit v2 on v1

--- a/solution.py
+++ b/solution.py
@@ -2,6 +2,7 @@
 
 import jax
 import jax.numpy as jnp
+import numpy as np
 from jax import lax
 from jax.experimental import pallas as pl
 from jax.experimental.pallas import tpu as pltpu
@@ -9,10 +10,16 @@
 
 PI = 3.141592653589793
 LANES = 128
-BLOCK = 256
+STEP = 512
+INVERSE_BLOCK = 656
 STRIP = 64
-VMEM_BYTES = 40 * 1024 * 1024
+VMEM_BYTES = 56 * 1024 * 1024
 CHUNKS = ((0, 5),)
+RING = 8
+BAND_ORDER = [
+    RING * sum((p >> (5 - 2 * bit) & 1) << bit for bit in range(3)) + sum((p >> (4 - 2 * bit) & 1) << bit for bit in range(3))
+    for p in range(RING * RING)
+]
 
 
 def unit_circle(waves, points, count):
@@ -74,14 +81,25 @@
     lax.fori_loop(straddle + 1, blocks, advance(1), turn(later, steps[1]))
 
 
-def forward_kernel(highest, bands, pair_ids, trims, weights, waves, grid, packed, table, totals, columns, rows):
+def ordered_columns(chunk, wavenumbers, raw, columns):
+    total = wavenumbers.shape[1]
+    stride = total // len(BAND_ORDER)
+    count = chunk[1] - chunk[0]
+    raw[...] = jnp.broadcast_to(wavenumbers[...].astype(jnp.float32), (LANES, total)).T
+    for column in range(2):
+        for place, band in enumerate(BAND_ORDER):
+            target = (column * len(BAND_ORDER) + place) * count
+            columns[target:target + count, :] = raw[pl.ds(band * stride + 2 * chunk[0] + column, count, stride=2), :]
+
+
+def forward_kernel(highest, chunk, pair_ids, trims, weights, wavenumbers, grid, packed, table, totals, raw, columns, rows):
     length, fields = grid.shape
-    width = waves.shape[1]
+    width = columns.shape[0]
     quarter = width // 2
     facts = cycle_facts(length, highest, pair_ids, trims)
     first, counts, _ = facts
     blocks = -(-length // LANES)
-    columns[...] = jnp.broadcast_to(waves[...].astype(jnp.float32), (LANES, width)).T
+    ordered_columns(chunk, wavenumbers, raw, columns)
 
     for strip in range(width // STRIP):
         chosen = columns[strip * STRIP:(strip + 1) * STRIP, :]
@@ -104,32 +122,32 @@
 
         fill_table(1, chosen, step_waves, facts, blocks, write)
 
-    full = length // BLOCK
-    straddle = first // BLOCK
-    position = lax.broadcasted_iota(jnp.int32, (BLOCK, fields), 0)
+    full = length // STEP
+    straddle = first // STEP
+    position = lax.broadcasted_iota(jnp.int32, (STEP, fields), 0)
 
     def product(start, size, data):
         return jnp.dot(table[:, pl.ds(start, size)], data, preferred_element_type=jnp.float32)
 
     def data_of(block):
-        return grid[pl.ds(pl.multiple_of(block * BLOCK, BLOCK), BLOCK), :]
+        return grid[pl.ds(pl.multiple_of(block * STEP, STEP), STEP), :]
 
     def add(cycle):
         def body(block, carry):
-            totals[cycle] += product(pl.multiple_of(block * BLOCK, BLOCK), BLOCK, data_of(block))
+            totals[cycle] += product(pl.multiple_of(block * STEP, STEP), STEP, data_of(block))
             return carry
 
         return body
 
     data = data_of(straddle)
-    before = position + straddle * BLOCK < first
+    before = position + straddle * STEP < first
     nothing = jnp.zeros_like(data)
-    start = pl.multiple_of(straddle * BLOCK, BLOCK)
-    totals[0] = product(start, BLOCK, jnp.where(before, data, nothing))
-    totals[1] = product(start, BLOCK, jnp.where(before, nothing, data))
+    start = pl.multiple_of(straddle * STEP, STEP)
+    totals[0] = product(start, STEP, jnp.where(before, data, nothing))
+    totals[1] = product(start, STEP, jnp.where(before, nothing, data))
     lax.fori_loop(0, straddle, add(0), 0)
     lax.fori_loop(straddle + 1, full, add(1), 0)
-    totals[1] += product(full * BLOCK, length - full * BLOCK, grid[full * BLOCK:, :])
+    totals[1] += product(full * STEP, length - full * STEP, grid[full * STEP:, :])
 
     share = LANES // 4
     for group in range(fields // share):
@@ -143,21 +161,19 @@
         packed[group] = rows[...].astype(jnp.bfloat16)
 
 
-def table_kernel(length, highest, pair_ids, trims, *refs):
-    *waves, table = refs
+def table_kernel(length, highest, pair_ids, trims, wavenumbers, table, raw, columns):
     facts = cycle_facts(length, highest, pair_ids, trims)
     blocks = -(-length // LANES)
     base = 0
-    for chunk in waves:
-        width = chunk.shape[1]
+    for chunk in CHUNKS:
+        width = 2 * len(BAND_ORDER) * (chunk[1] - chunk[0])
+        ordered_columns(chunk, wavenumbers, raw, columns)
         for tile in range(width // LANES):
-            row = chunk[:, tile * LANES:(tile + 1) * LANES].astype(jnp.float32)
-            chosen = jnp.broadcast_to(row, (LANES, LANES))
+            chosen = columns[tile * LANES:(tile + 1) * LANES, :].T
 
             def step_waves(counts):
-                wide = jnp.broadcast_to(row, (8, LANES))
                 return [
-                    tuple(part[:1] for part in unit_circle(wide, float(LANES), count)) for count in counts
+                    tuple(part[:1] for part in unit_circle(chosen[:8], float(LANES), count)) for count in counts
                 ]
 
             def write(block, state):
@@ -171,13 +187,17 @@
         base += 2 * width
 
 
-def legendre_kernel(start, highest, band, wavenumbers, values, legendre, damping, *refs):
+def legendre_kernel(start, highest, band, wavenumbers, ordering, values, legendre, damping, *refs):
     spectrum, rebuilt = refs[-2:]
     groups, _, degrees, each = legendre.shape
     matrix = jnp.concatenate([legendre[group, 0] for group in range(groups)], axis=1)
-    sums = lax.dot_general(
-        values[0].T, matrix, (((1,), (1,)), ((), ())), preferred_element_type=jnp.float32
-    )
+    from_order = ordering[...].T
+    natural = [
+        jnp.dot(from_order, values[0, group * each:(group + 1) * each], preferred_element_type=jnp.float32)
+        for group in range(groups)
+    ]
+    natural = jnp.concatenate(natural, axis=0).astype(jnp.bfloat16)
+    sums = jnp.dot(matrix, natural, preferred_element_type=jnp.float32).T
     fields = sums.shape[0] // 2
     pair = band[0] + start + pl.program_id(0)
     first_wave = wavenumbers[2 * pair]
@@ -197,7 +217,12 @@
     row = lax.broadcasted_iota(jnp.int32, products.shape, 0)
     wave = jnp.where(row < fields, first_wave, second_wave)
     doubled = products * jnp.where(wave == 0, 1.0, 2.0)
-    rebuilt[0] = doubled.astype(jnp.bfloat16).T
+    doubled = doubled.astype(jnp.bfloat16)
+    for group in range(groups):
+        part = slice(group * each, (group + 1) * each)
+        rebuilt[0, part] = lax.dot_general(
+            ordering[...], doubled[:, part], (((1,), (1,)), ((), ())), preferred_element_type=jnp.float32
+        ).astype(jnp.bfloat16)
 
 
 def inverse_kernel(chunks, pair_ids, *refs):
@@ -232,8 +257,8 @@
     def product(cycle):
         return jnp.dot(table[...], factors[cycle], preferred_element_type=jnp.float32)
 
-    start = block * BLOCK
-    end = start + BLOCK
+    start = block * INVERSE_BLOCK
+    end = start + INVERSE_BLOCK
 
     @pl.when(end <= first)
     def _():
@@ -257,18 +282,19 @@
     return pltpu.CompilerParams(dimension_semantics=semantics or None, vmem_limit_bytes=VMEM_BYTES)
 
 
-def forward_call(highest, bands, pair_ids, trims, weights, waves, points):
+def forward_call(highest, chunk, pair_ids, trims, weights, wavenumbers, points):
     length, fields = points.shape
-    width = waves.shape[1]
-    blocks = -(-length // BLOCK)
+    width = 2 * len(BAND_ORDER) * (chunk[1] - chunk[0])
+    blocks = -(-length // LANES)
     return pl.pallas_call(
-        functools.partial(forward_kernel, highest, bands),
+        functools.partial(forward_kernel, highest, chunk),
         in_specs=[SMEM, SMEM, SMEM, VMEM, VMEM],
         out_specs=VMEM,
         out_shape=jax.ShapeDtypeStruct((4 * fields // LANES, width, LANES), jnp.bfloat16),
         scratch_shapes=[
-            pltpu.VMEM((2 * width, blocks * BLOCK), jnp.bfloat16),
+            pltpu.VMEM((2 * width, blocks * LANES), jnp.bfloat16),
             pltpu.VMEM((2, 2 * width, fields), jnp.float32),
+            pltpu.VMEM((wavenumbers.shape[1], LANES), jnp.float32),
             pltpu.VMEM((width, LANES), jnp.float32),
             pltpu.VMEM((width, LANES), jnp.float32),
         ],
@@ -277,21 +303,25 @@
             flops=2 * length * fields * 2 * width, bytes_accessed=length * fields * 2, transcendentals=0
         ),
         name="forward_dft",
-    )(pair_ids, trims, weights, waves, points)
-
-
-def table_call(highest, length, pair_ids, trims, chunk_waves):
-    blocks = -(-length // BLOCK)
-    total = 2 * sum(waves.shape[1] for waves in chunk_waves)
+    )(pair_ids, trims, weights, wavenumbers, points)
+
+
+def table_call(highest, length, pair_ids, trims, wavenumbers):
+    blocks = -(-length // LANES)
+    total = 2 * wavenumbers.shape[1]
     return pl.pallas_call(
         functools.partial(table_kernel, length, highest),
-        in_specs=[SMEM, SMEM] + [VMEM] * len(chunk_waves),
+        in_specs=[SMEM, SMEM, VMEM],
         out_specs=VMEM,
-        out_shape=jax.ShapeDtypeStruct((blocks * BLOCK, total), jnp.bfloat16),
+        out_shape=jax.ShapeDtypeStruct((blocks * LANES, total), jnp.bfloat16),
+        scratch_shapes=[
+            pltpu.VMEM((wavenumbers.shape[1], LANES), jnp.float32),
+            pltpu.VMEM((wavenumbers.shape[1], LANES), jnp.float32),
+        ],
         compiler_params=parameters(),
         cost_estimate=pl.CostEstimate(flops=8 * length * total, bytes_accessed=2 * length * total, transcendentals=0),
         name="inverse_table",
-    )(pair_ids, trims, *chunk_waves)
+    )(pair_ids, trims, wavenumbers)
 
 
 def legendre_call(highest, start, band, wavenumbers, values, gathered, damping, spectrum):
@@ -299,12 +329,17 @@
     count, cycles, _ = values.shape
     fields = LANES // 2
     previous = [] if spectrum is None else [spectrum]
+    ordering = np.zeros((len(BAND_ORDER), 2, len(BAND_ORDER), 2), np.float32)
+    for place, one in enumerate(BAND_ORDER):
+        ordering[place, 0, one, 0] = ordering[place, 1, one, 1] = 1.0
+    ordering = jnp.asarray(ordering.reshape(each, each), jnp.bfloat16)
     return pl.pallas_call(
         functools.partial(legendre_kernel, start, highest),
         grid=(count,),
         in_specs=[
             SMEM,
             SMEM,
+            pl.BlockSpec(ordering.shape, lambda q: (0, 0)),
             pl.BlockSpec((1, cycles, LANES), lambda q: (q, 0, 0)),
             pl.BlockSpec((groups, 1, degrees, each), lambda q: (0, q + start, 0, 0)),
             pl.BlockSpec(damping.shape, lambda q: (0, 0)),
@@ -318,7 +353,7 @@
             jax.ShapeDtypeStruct((local_pairs, fields, degrees), jnp.bfloat16),
             jax.ShapeDtypeStruct((count, cycles, LANES), jnp.bfloat16),
         ],
-        input_output_aliases={5: 0} if previous else {},
+        input_output_aliases={6: 0} if previous else {},
         compiler_params=parameters("arbitrary"),
         cost_estimate=pl.CostEstimate(
             flops=4 * count * cycles * LANES * degrees,
@@ -326,19 +361,19 @@
             transcendentals=0,
         ),
         name="legendre_both_ways",
-    )(band, wavenumbers, values, gathered, damping, *previous)
+    )(band, wavenumbers, ordering, values, gathered, damping, *previous)
 
 
 def inverse_call(length, fields, pair_ids, values, table):
-    blocks = -(-length // BLOCK)
+    blocks = -(-length // INVERSE_BLOCK)
     total = table.shape[1]
     return pl.pallas_call(
         functools.partial(inverse_kernel, len(values)),
         grid=(blocks,),
         in_specs=[SMEM]
         + [pl.BlockSpec(one.shape, lambda i: (0, 0, 0)) for one in values]
-        + [pl.BlockSpec((BLOCK, total), lambda i: (i, 0))],
-        out_specs=pl.BlockSpec((BLOCK, fields), lambda i: (i, 0)),
+        + [pl.BlockSpec((INVERSE_BLOCK, total), lambda i: (i, 0))],
+        out_specs=pl.BlockSpec((INVERSE_BLOCK, fields), lambda i: (i, 0)),
         out_shape=jax.ShapeDtypeStruct((length, fields), jnp.bfloat16),
         scratch_shapes=[
             pltpu.VMEM((4, max(one.shape[1] for one in values), LANES), jnp.float32),
@@ -352,6 +387,14 @@
     )(pair_ids, *values, table)
 
 
+def exchange(message, groups):
+    bands = len(BAND_ORDER)
+    partners = [group * bands + band for group in range(groups) for band in BAND_ORDER]
+    return lax.all_to_all(
+        message, ("fld", "band"), split_axis=0, concat_axis=0, tiled=True, axis_index_groups=[partners]
+    )
+
+
 def on_device(grid, pair_ids, trims, weights, wavenumbers, legendre, damping):
     fields, length = grid.shape[2:]
     columns = wavenumbers.shape[0]
@@ -361,30 +404,27 @@
     bands = lax.axis_size("band")
     gathered = lax.all_gather(legendre.swapaxes(1, 2), "fld")
     points = grid[0, 0].T
-    by_band = wavenumbers.reshape(bands, local_pairs, 2)
-    chunk_waves = [
-        by_band[:, start:end].transpose(2, 0, 1).reshape(1, 2 * bands * (end - start)) for start, end in CHUNKS
-    ]
+    waves = wavenumbers[None, :]
     padding = -(-degrees // LANES) * LANES - columns
     padded = jnp.broadcast_to(jnp.pad(damping, (0, padding))[None, :], (8, columns + padding))
     band = (lax.axis_index("band") * local_pairs).astype(jnp.int32).reshape(1)
 
     arrived = []
-    for (start, end), waves in zip(CHUNKS, chunk_waves):
-        packed = forward_call(highest, bands, pair_ids, trims, weights, waves, points)
-        packed = packed.reshape(groups * bands, end - start, 2, LANES)
-        arrived.append(lax.all_to_all(packed, ("fld", "band"), split_axis=0, concat_axis=0, tiled=True))
-    table = table_call(highest, length, pair_ids, trims, chunk_waves)
+    for chunk in CHUNKS:
+        packed = forward_call(highest, chunk, pair_ids, trims, weights, waves, points)
+        arrived.append(exchange(packed.reshape(groups * bands, chunk[1] - chunk[0], 2, LANES), groups))
+    table = table_call(highest, length, pair_ids, trims, waves)
     spectrum = None
     returned = []
     for (start, end), message in zip(CHUNKS, arrived):
-        values = message.transpose(1, 0, 2, 3).reshape(end - start, groups * local_cycles, LANES)
+        count = end - start
+        values = message.transpose(1, 0, 2, 3).reshape(count, groups * local_cycles, LANES)
         spectrum, rebuilt = legendre_call(
             highest, start, band, wavenumbers, values, gathered, padded, spectrum
         )
-        leaving = rebuilt.reshape(end - start, groups * bands, 2, LANES).transpose(1, 0, 2, 3)
-        message = lax.all_to_all(leaving, ("fld", "band"), split_axis=0, concat_axis=0, tiled=True)
-        returned.append(message.reshape(groups, bands * (end - start) * 2, LANES))
+        leaving = rebuilt.reshape(count, groups * bands, 2, LANES).transpose(1, 0, 2, 3)
+        message = exchange(leaving, groups)
+        returned.append(message.reshape(groups, bands * count * 2, LANES))
     restored = inverse_call(length, fields, pair_ids, returned, table)
     return (
         spectrum.reshape(local_pairs, 2, fields // groups, degrees),

time: 163 us -> 166 us (1.018)
  Pallas kernels: 29.9 us -> 38.7 us
  local copies, waits for them, and re-layouts: 13.3 us -> 8.2 us
    unnamed x16 -> x4, local copies, waits for them, and re-layouts: 8.84 us -> 1.08 us
    pallas_call x1, Pallas kernels: 6.61 us -> 11.7 us  [legendre_call(): pl.pallas_call(functools.partial(legendre_kernel, start, highest), grid=(...]
    pallas_call x1, Pallas kernels: 3.88 us -> 7.18 us  [table_call(): pl.pallas_call(functools.partial(table_kernel, length, highest), in_specs...]
  transfers between devices with their start and end apart: 3 -> 3, of which waited for: 2 -> 2; matrix products, arithmetic and copies ran while one was open for 2% -> 2% of each run, Pallas kernels for 10% -> 12%
where the time goes in v2:
time: 166 us
  waiting for transfers between devices  73.1 us (44%)
  Pallas kernels  38.7 us (23%)
  starting transfers between devices  31.1 us (19%)
  between operations  14.7 us (9%)
  local copies, waits for them, and re-layouts  8.2 us (5%)
    all_to_all x2, waiting for transfers between devices, exchange(): lax.all_to_all(message, ('fld', 'band'), split_axis=0, concat_axis=0, til...  72.4 us
    all_to_all x2, starting transfers between devices, exchange(): lax.all_to_all(message, ('fld', 'band'), split_axis=0, concat_axis=0, til...  31 us
    pallas_call x1, Pallas kernels, forward_call(): pl.pallas_call(functools.partial(forward_kernel, highest, chunk), in_spec...  12 us
    pallas_call x1, Pallas kernels, legendre_call(): pl.pallas_call(functools.partial(legendre_kernel, start, highest), grid=(...  11.7 us
    pallas_call x1, Pallas kernels, inverse_call(): pl.pallas_call(functools.partial(inverse_kernel, len(values)), grid=(bloc...  7.74 us
    pallas_call x1, Pallas kernels, table_call(): pl.pallas_call(functools.partial(table_kernel, length, highest), in_specs...  7.18 us
  transfers between devices with their start and end apart: 3, of which 2 were waited for; matrix products, arithmetic and copies ran while one was open for 2% of the time, Pallas kernels for 12%

profile of v2, /device:TPU:1, one launch (start us, length us, event | category | flops | bytes accessed | tf_op | source)
XLA Modules:
  0.0 165.7 jit_solution(18078626459650556039)
XLA Ops:
  7.2 0.0 all-gather.3.cloned.1.call-start
  7.2 0.7 all-gather.3.cloned.1.call-update
  8.5 1.3 broadcast_in_dim.4.wavenumbers
  9.8 12.0 %forward_dft.1 = bf16[8,640,128]{2,1,0:T(8,128)(2,1)} custom-call(s32[1,1]{1,0:T(1,128)S(6)} %copy.16.pair_ids, s32[1,1,2]{2,1,0:T(1,128)} %trims.3, f32[1,1,2]{2,1,0:T(1,128)} %weights.1, s32[1,640]{1,0:T(1,128)} %broadcast_in_dim.4.wavenumbers, bf16[2596,256]{1,0:T(8,128)(2,1)} %bitcast.26), custom_call_target="tpu_custom_call" | custom-call | flops 1701314560 | bytes 1329152 | tf_op jit(solution)/shard_map/forward_dft/pallas_call | solution.py:289
  21.9 0.0 copy-start.1
  21.9 22.3 %all-to-all-start = ((bf16[512,5,2,128]{3,2,1,0:T(2,128)(2,1)}), bf16[512,5,2,128]{3,2,1,0:T(2,128)(2,1)S(1)}, u32[]{:S(2)}, u32[]{:S(2)}) async-start(bf16[512,5,2,128]{3,2,1,0:T(2,128)(2,1)} %bitcast.23), calls=%async_computation | async-start | bytes 2621440 | tf_op jit(solution)/shard_map/all_to_all | solution.py:393
  44.2 0.0 copy-done.1
  44.2 39.7 %all-to-all-done = bf16[512,5,2,128]{3,2,1,0:T(2,128)(2,1)S(1)} async-done(((bf16[512,5,2,128]{3,2,1,0:T(2,128)(2,1)}), bf16[512,5,2,128]{3,2,1,0:T(2,128)(2,1)S(1)}, u32[]{:S(2)}, u32[]{:S(2)}) %all-to-all-start) | async-done | bytes 1310752 | tf_op jit(solution)/shard_map/all_to_all | solution.py:393
  83.9 2.0 %copy.12 = bf16[5,512,2,128]{3,2,1,0:T(2,128)(2,1)} copy(bf16[5,512,2,128]{3,2,0,1:T(2,128)(2,1)S(1)} %bitcast.21) | data formatting | bytes 2621440 | tf_op jit(solution)/shard_map/transpose | solution.py:421
  85.8 0.0 all-gather.3.cloned.1.call-done
  85.8 0.6 broadcast_in_dim.10.damping
  86.4 11.7 %legendre_both_ways.1 = (bf16[5,64,641]{2,1,0:T(8,128)(2,1)}, bf16[5,1024,128]{2,1,0:T(8,128)(2,1)}) custom-call(s32[1]{0:T(128)} %bitcast.band, s32[640]{0:T(1024)} %wavenumbers.1, bf16[128,128]{1,0:T(8,128)(2,1)} %constant.13.clone.ordering, bf16[5,1024,128]{2,1,0:T(8,128)(2,1)} %bitcast.20, bf16[8,5,641,128]{3,2,1,0:T(8,128)(2,1)} %bitcast.18, ...), custom_call_target="tpu_custom_call" | custom-call | flops 1680343040 | bytes 6563840 | tf_op jit(solution)/shard_map/legendre_both_ways/pallas_call | solution.py:336
  98.2 3.3 %copy.15 = bf16[5,512,2,128]{3,2,0,1:T(2,128)(2,1)} copy(bf16[5,512,2,128]{3,2,1,0:T(2,128)(2,1)} %bitcast.24) | data formatting | bytes 2621440 | tf_op jit(solution)/shard_map/reshape | solution.py:425
  101.4 8.8 %all-to-all-start.1 = ((bf16[512,5,2,128]{3,2,1,0:T(2,128)(2,1)}), bf16[512,5,2,128]{3,2,1,0:T(2,128)(2,1)S(1)}, u32[]{:S(2)}, u32[]{:S(2)}) async-start(bf16[512,5,2,128]{3,2,1,0:T(2,128)(2,1)} %bitcast.17), calls=%async_computation.1 | async-start | bytes 2621440 | tf_op jit(solution)/shard_map/all_to_all | solution.py:393
  110.2 7.2 %inverse_table.1.refs_1_ = bf16[2688,1280]{1,0:T(8,128)(2,1)} custom-call(s32[1,1]{1,0:T(1,128)S(6)} %copy.16.pair_ids, s32[1,1,2]{2,1,0:T(1,128)} %trims.3, s32[1,640]{1,0:T(1,128)} %broadcast_in_dim.4.wavenumbers), custom_call_target="tpu_custom_call" | custom-call | flops 26583040 | bytes 6645760 | tf_op jit(solution)/shard_map/inverse_table/pallas_call | solution.py:312
  117.4 32.7 %all-to-all-done.1 = bf16[512,5,2,128]{3,2,1,0:T(2,128)(2,1)S(1)} async-done(((bf16[512,5,2,128]{3,2,1,0:T(2,128)(2,1)}), bf16[512,5,2,128]{3,2,1,0:T(2,128)(2,1)S(1)}, u32[]{:S(2)}, u32[]{:S(2)}) %all-to-all-start.1) | async-done | bytes 1310752 | tf_op jit(solution)/shard_map/all_to_all | solution.py:393
  150.1 0.0 copy-start
  150.1 1.1 copy-done
  151.1 7.7 %inverse_dft.1 = bf16[2596,256]{1,0:T(8,128)(2,1)} custom-call(s32[1,1]{1,0:T(1,128)S(6)} %copy.16.pair_ids, bf16[8,640,128]{2,1,0:T(8,128)(2,1)} %bitcast.19, bf16[2688,1280]{1,0:T(8,128)(2,1)} %inverse_table.1.refs_1_), custom_call_target="tpu_custom_call" | custom-call | flops 1701314560 | bytes 7974912 | tf_op jit(solution)/shard_map/inverse_dft/pallas_call | solution.py:370
  (1 shorter events, 0.0 us)
Async XLA Ops:
  7.2 78.7 %all-gather.3.cloned.1.call-start = ((), (), s32[]{:S(2)}) async-start(), calls=%async_computation.2 | async-start | bytes 7464960 | tf_op jit(solution)/shard_map/all_gather | solution.py:405
  21.9 22.3 %copy-start.1 = (f32[640]{0:T(1024)S(1)}, f32[640]{0:T(1024)}, u32[]{:S(2)}) copy-start(f32[640]{0:T(1024)} %param.14) | copy-start | bytes 7684
  21.9 62.0 %all-to-all-start = ((bf16[512,5,2,128]{3,2,1,0:T(2,128)(2,1)}), bf16[512,5,2,128]{3,2,1,0:T(2,128)(2,1)S(1)}, u32[]{:S(2)}, u32[]{:S(2)}) async-start(bf16[512,5,2,128]{3,2,1,0:T(2,128)(2,1)} %bitcast.23), calls=%async_computation | async-start | bytes 2621440 | tf_op jit(solution)/shard_map/all_to_all | solution.py:393
  101.4 48.6 %all-to-all-start.1 = ((bf16[512,5,2,128]{3,2,1,0:T(2,128)(2,1)}), bf16[512,5,2,128]{3,2,1,0:T(2,128)(2,1)S(1)}, u32[]{:S(2)}, u32[]{:S(2)}) async-start(bf16[512,5,2,128]{3,2,1,0:T(2,128)(2,1)} %bitcast.17), calls=%async_computation.1 | async-start | bytes 2621440 | tf_op jit(solution)/shard_map/all_to_all | solution.py:393
  150.1 1.1 copy-start
Sparse Core Ops, SparseCore 0:
  10.2 64.7 all-gather.2

commit v3 on v2

--- a/solution.py
+++ b/solution.py
@@ -2,7 +2,6 @@
 
 import jax
 import jax.numpy as jnp
-import numpy as np
 from jax import lax
 from jax.experimental import pallas as pl
 from jax.experimental.pallas import tpu as pltpu
@@ -13,13 +12,9 @@
 STEP = 512
 INVERSE_BLOCK = 656
 STRIP = 64
-VMEM_BYTES = 56 * 1024 * 1024
-CHUNKS = ((0, 5),)
-RING = 8
-BAND_ORDER = [
-    RING * sum((p >> (5 - 2 * bit) & 1) << bit for bit in range(3)) + sum((p >> (4 - 2 * bit) & 1) << bit for bit in range(3))
-    for p in range(RING * RING)
-]
+VMEM_BYTES = 40 * 1024 * 1024
+LARGE_VMEM_BYTES = 57_000_000
+CHUNKS = ((0, 3), (3, 5))
 
 
 def unit_circle(waves, points, count):
@@ -81,25 +76,24 @@
     lax.fori_loop(straddle + 1, blocks, advance(1), turn(later, steps[1]))
 
 
-def ordered_columns(chunk, wavenumbers, raw, columns):
-    total = wavenumbers.shape[1]
-    stride = total // len(BAND_ORDER)
-    count = chunk[1] - chunk[0]
-    raw[...] = jnp.broadcast_to(wavenumbers[...].astype(jnp.float32), (LANES, total)).T
+def ordered_columns(chunk, stride, wavenumbers, raw, columns):
+    total = wavenumbers.shape[0]
+    raw[...] = jnp.broadcast_to(wavenumbers[...].astype(jnp.float32)[None, :], (LANES, total)).T
+    target = 0
     for column in range(2):
-        for place, band in enumerate(BAND_ORDER):
-            target = (column * len(BAND_ORDER) + place) * count
-            columns[target:target + count, :] = raw[pl.ds(band * stride + 2 * chunk[0] + column, count, stride=2), :]
-
-
-def forward_kernel(highest, chunk, pair_ids, trims, weights, wavenumbers, grid, packed, table, totals, raw, columns, rows):
+        for pair in range(*chunk):
+            columns[target:target + STRIP, :] = raw[pl.ds(2 * pair + column, STRIP, stride=stride), :]
+            target += STRIP
+
+
+def forward_kernel(highest, chunk, stride, pair_ids, trims, weights, wavenumbers, grid, packed, table, totals, raw, columns, rows):
     length, fields = grid.shape
     width = columns.shape[0]
     quarter = width // 2
     facts = cycle_facts(length, highest, pair_ids, trims)
     first, counts, _ = facts
     blocks = -(-length // LANES)
-    ordered_columns(chunk, wavenumbers, raw, columns)
+    ordered_columns(chunk, stride, wavenumbers, raw, columns)
 
     for strip in range(width // STRIP):
         chosen = columns[strip * STRIP:(strip + 1) * STRIP, :]
@@ -157,17 +151,21 @@
             joined = jnp.concatenate(
                 [totals[cycle, part * quarter:(part + 1) * quarter, lanes] for part in (0, 2, 1, 3)], axis=1
             )
-            rows[pl.ds(cycle, quarter, stride=2), :] = joined * scale
+            joined = joined * scale
+            for pair in range(quarter // STRIP):
+                rows[pl.ds(2 * pair + cycle, STRIP, stride=2 * quarter // STRIP), :] = (
+                    joined[pair * STRIP:(pair + 1) * STRIP]
+                )
         packed[group] = rows[...].astype(jnp.bfloat16)
 
 
-def table_kernel(length, highest, pair_ids, trims, wavenumbers, table, raw, columns):
+def table_kernel(length, highest, stride, pair_ids, trims, wavenumbers, table, raw, columns):
     facts = cycle_facts(length, highest, pair_ids, trims)
     blocks = -(-length // LANES)
     base = 0
     for chunk in CHUNKS:
-        width = 2 * len(BAND_ORDER) * (chunk[1] - chunk[0])
-        ordered_columns(chunk, wavenumbers, raw, columns)
+        width = 2 * STRIP * (chunk[1] - chunk[0])
+        ordered_columns(chunk, stride, wavenumbers, raw, columns)
         for tile in range(width // LANES):
             chosen = columns[tile * LANES:(tile + 1) * LANES, :].T
 
@@ -187,17 +185,13 @@
         base += 2 * width
 
 
-def legendre_kernel(start, highest, band, wavenumbers, ordering, values, legendre, damping, *refs):
+def legendre_kernel(start, highest, band, wavenumbers, values, legendre, damping, *refs):
     spectrum, rebuilt = refs[-2:]
     groups, _, degrees, each = legendre.shape
     matrix = jnp.concatenate([legendre[group, 0] for group in range(groups)], axis=1)
-    from_order = ordering[...].T
-    natural = [
-        jnp.dot(from_order, values[0, group * each:(group + 1) * each], preferred_element_type=jnp.float32)
-        for group in range(groups)
-    ]
-    natural = jnp.concatenate(natural, axis=0).astype(jnp.bfloat16)
-    sums = jnp.dot(matrix, natural, preferred_element_type=jnp.float32).T
+    sums = lax.dot_general(
+        values[0].T, matrix, (((1,), (1,)), ((), ())), preferred_element_type=jnp.float32
+    )
     fields = sums.shape[0] // 2
     pair = band[0] + start + pl.program_id(0)
     first_wave = wavenumbers[2 * pair]
@@ -217,12 +211,7 @@
     row = lax.broadcasted_iota(jnp.int32, products.shape, 0)
     wave = jnp.where(row < fields, first_wave, second_wave)
     doubled = products * jnp.where(wave == 0, 1.0, 2.0)
-    doubled = doubled.astype(jnp.bfloat16)
-    for group in range(groups):
-        part = slice(group * each, (group + 1) * each)
-        rebuilt[0, part] = lax.dot_general(
-            ordering[...], doubled[:, part], (((1,), (1,)), ((), ())), preferred_element_type=jnp.float32
-        ).astype(jnp.bfloat16)
+    rebuilt[0] = doubled.astype(jnp.bfloat16).T
 
 
 def inverse_kernel(chunks, pair_ids, *refs):
@@ -243,7 +232,14 @@
                     rows[near, :height] = chunk[4 * side + near].astype(jnp.float32)
                 for cycle in range(2):
                     turned = [
-                        rows[near, pl.ds(cycle, quarter, stride=2), :].astype(jnp.bfloat16) for near in range(4)
+                        jnp.concatenate(
+                            [
+                                rows[near, pl.ds(2 * pair + cycle, STRIP, stride=2 * quarter // STRIP), :]
+                                for pair in range(quarter // STRIP)
+                            ],
+                            axis=0,
+                        ).astype(jnp.bfloat16)
+                        for near in range(4)
                     ]
                     for part in range(4):
                         source = (0, 2, 1, 3)[part] * share
@@ -278,23 +274,23 @@
 VMEM = pl.BlockSpec(memory_space=pltpu.VMEM)
 
 
-def parameters(*semantics):
-    return pltpu.CompilerParams(dimension_semantics=semantics or None, vmem_limit_bytes=VMEM_BYTES)
-
-
-def forward_call(highest, chunk, pair_ids, trims, weights, wavenumbers, points):
+def parameters(*semantics, limit=VMEM_BYTES):
+    return pltpu.CompilerParams(dimension_semantics=semantics or None, vmem_limit_bytes=limit)
+
+
+def forward_call(highest, chunk, stride, pair_ids, trims, weights, wavenumbers, points):
     length, fields = points.shape
-    width = 2 * len(BAND_ORDER) * (chunk[1] - chunk[0])
+    width = 2 * STRIP * (chunk[1] - chunk[0])
     blocks = -(-length // LANES)
     return pl.pallas_call(
-        functools.partial(forward_kernel, highest, chunk),
+        functools.partial(forward_kernel, highest, chunk, stride),
         in_specs=[SMEM, SMEM, SMEM, VMEM, VMEM],
         out_specs=VMEM,
         out_shape=jax.ShapeDtypeStruct((4 * fields // LANES, width, LANES), jnp.bfloat16),
         scratch_shapes=[
             pltpu.VMEM((2 * width, blocks * LANES), jnp.bfloat16),
             pltpu.VMEM((2, 2 * width, fields), jnp.float32),
-            pltpu.VMEM((wavenumbers.shape[1], LANES), jnp.float32),
+            pltpu.VMEM((wavenumbers.shape[0], LANES), jnp.float32),
             pltpu.VMEM((width, LANES), jnp.float32),
             pltpu.VMEM((width, LANES), jnp.float32),
         ],
@@ -306,17 +302,17 @@
     )(pair_ids, trims, weights, wavenumbers, points)
 
 
-def table_call(highest, length, pair_ids, trims, wavenumbers):
+def table_call(highest, length, stride, pair_ids, trims, wavenumbers):
     blocks = -(-length // LANES)
-    total = 2 * wavenumbers.shape[1]
+    total = 2 * wavenumbers.shape[0]
     return pl.pallas_call(
-        functools.partial(table_kernel, length, highest),
+        functools.partial(table_kernel, length, highest, stride),
         in_specs=[SMEM, SMEM, VMEM],
         out_specs=VMEM,
         out_shape=jax.ShapeDtypeStruct((blocks * LANES, total), jnp.bfloat16),
         scratch_shapes=[
-            pltpu.VMEM((wavenumbers.shape[1], LANES), jnp.float32),
-            pltpu.VMEM((wavenumbers.shape[1], LANES), jnp.float32),
+            pltpu.VMEM((wavenumbers.shape[0], LANES), jnp.float32),
+            pltpu.VMEM((wavenumbers.shape[0], LANES), jnp.float32),
         ],
         compiler_params=parameters(),
         cost_estimate=pl.CostEstimate(flops=8 * length * total, bytes_accessed=2 * length * total, transcendentals=0),
@@ -329,17 +325,12 @@
     count, cycles, _ = values.shape
     fields = LANES // 2
     previous = [] if spectrum is None else [spectrum]
-    ordering = np.zeros((len(BAND_ORDER), 2, len(BAND_ORDER), 2), np.float32)
-    for place, one in enumerate(BAND_ORDER):
-        ordering[place, 0, one, 0] = ordering[place, 1, one, 1] = 1.0
-    ordering = jnp.asarray(ordering.reshape(each, each), jnp.bfloat16)
     return pl.pallas_call(
         functools.partial(legendre_kernel, start, highest),
         grid=(count,),
         in_specs=[
             SMEM,
             SMEM,
-            pl.BlockSpec(ordering.shape, lambda q: (0, 0)),
             pl.BlockSpec((1, cycles, LANES), lambda q: (q, 0, 0)),
             pl.BlockSpec((groups, 1, degrees, each), lambda q: (0, q + start, 0, 0)),
             pl.BlockSpec(damping.shape, lambda q: (0, 0)),
@@ -353,15 +344,15 @@
             jax.ShapeDtypeStruct((local_pairs, fields, degrees), jnp.bfloat16),
             jax.ShapeDtypeStruct((count, cycles, LANES), jnp.bfloat16),
         ],
-        input_output_aliases={6: 0} if previous else {},
-        compiler_params=parameters("arbitrary"),
+        input_output_aliases={5: 0} if previous else {},
+        compiler_params=parameters("arbitrary", limit=LARGE_VMEM_BYTES),
         cost_estimate=pl.CostEstimate(
             flops=4 * count * cycles * LANES * degrees,
             bytes_accessed=2 * count * cycles * degrees,
             transcendentals=0,
         ),
         name="legendre_both_ways",
-    )(band, wavenumbers, ordering, values, gathered, damping, *previous)
+    )(band, wavenumbers, values, gathered, damping, *previous)
 
 
 def inverse_call(length, fields, pair_ids, values, table):
@@ -379,7 +370,7 @@
             pltpu.VMEM((4, max(one.shape[1] for one in values), LANES), jnp.float32),
             pltpu.VMEM((2, total, fields), jnp.bfloat16),
         ],
-        compiler_params=parameters("arbitrary"),
+        compiler_params=parameters("arbitrary", limit=LARGE_VMEM_BYTES),
         cost_estimate=pl.CostEstimate(
             flops=2 * length * fields * total, bytes_accessed=2 * length * (fields + total), transcendentals=0
         ),
@@ -387,12 +378,8 @@
     )(pair_ids, *values, table)
 
 
-def exchange(message, groups):
-    bands = len(BAND_ORDER)
-    partners = [group * bands + band for group in range(groups) for band in BAND_ORDER]
-    return lax.all_to_all(
-        message, ("fld", "band"), split_axis=0, concat_axis=0, tiled=True, axis_index_groups=[partners]
-    )
+def exchange(message):
+    return lax.all_to_all(message, ("fld", "band"), split_axis=0, concat_axis=0, tiled=True)
 
 
 def on_device(grid, pair_ids, trims, weights, wavenumbers, legendre, damping):
@@ -404,16 +391,16 @@
     bands = lax.axis_size("band")
     gathered = lax.all_gather(legendre.swapaxes(1, 2), "fld")
     points = grid[0, 0].T
-    waves = wavenumbers[None, :]
+    stride = 2 * local_pairs
     padding = -(-degrees // LANES) * LANES - columns
     padded = jnp.broadcast_to(jnp.pad(damping, (0, padding))[None, :], (8, columns + padding))
     band = (lax.axis_index("band") * local_pairs).astype(jnp.int32).reshape(1)
 
     arrived = []
     for chunk in CHUNKS:
-        packed = forward_call(highest, chunk, pair_ids, trims, weights, waves, points)
-        arrived.append(exchange(packed.reshape(groups * bands, chunk[1] - chunk[0], 2, LANES), groups))
-    table = table_call(highest, length, pair_ids, trims, waves)
+        packed = forward_call(highest, chunk, stride, pair_ids, trims, weights, wavenumbers, points)
+        arrived.append(exchange(packed.reshape(groups * bands, chunk[1] - chunk[0], 2, LANES)))
+    table = table_call(highest, length, stride, pair_ids, trims, wavenumbers)
     spectrum = None
     returned = []
     for (start, end), message in zip(CHUNKS, arrived):
@@ -423,7 +410,7 @@
             highest, start, band, wavenumbers, values, gathered, padded, spectrum
         )
         leaving = rebuilt.reshape(count, groups * bands, 2, LANES).transpose(1, 0, 2, 3)
-        message = exchange(leaving, groups)
+        message = exchange(leaving)
         returned.append(message.reshape(groups, bands * count * 2, LANES))
     restored = inverse_call(length, fields, pair_ids, returned, table)
     return (

time: 166 us -> 200 us (1.20)
  starting transfers between devices: 31.1 us -> 48.1 us
  waiting for transfers between devices: 73.1 us -> 83 us
  local copies, waits for them, and re-layouts: 8.2 us -> 17.2 us
  Pallas kernels: 38.7 us -> 36 us
    all_to_all x2 -> x4, starting transfers between devices: 31 us -> 48 us  [exchange(): lax.all_to_all(message, ('fld', 'band'), split_axis=0, concat_axis=0, til...]
    all_to_all x2 -> x4, waiting for transfers between devices: 72.4 us -> 82.3 us  [exchange(): lax.all_to_all(message, ('fld', 'band'), split_axis=0, concat_axis=0, til...]
    unnamed x4 -> x30, local copies, waits for them, and re-layouts: 1.08 us -> 10.4 us
    pallas_call x1 -> x2, Pallas kernels: 11.7 us -> 10 us  [legendre_call(): pl.pallas_call(functools.partial(legendre_kernel, start, highest), grid=(...]
    pallas_call x2 -> x3, Pallas kernels: 19.2 us -> 18.4 us  [the longest x2 13.5 us: forward_call(): pl.pallas_call(functools.partial(forward_kernel, highest, chunk, stride),...]
  transfers between devices with their start and end apart: 3 -> 5, of which waited for: 2 -> 4; matrix products, arithmetic and copies ran while one was open for 2% -> 2% of each run, Pallas kernels for 12% -> 9%
where the time goes in v3:
time: 200 us; the launch traced here: 199 us
  waiting for transfers between devices  83 us (42%)
  starting transfers between devices  48.1 us (24%)
  Pallas kernels  36 us (18%)
  local copies, waits for them, and re-layouts  17.2 us (9%)
  between operations  14.8 us (7%)
    all_to_all x4, waiting for transfers between devices, exchange(): lax.all_to_all(message, ('fld', 'band'), split_axis=0, concat_axis=0, til...  82.3 us
    all_to_all x4, starting transfers between devices, exchange(): lax.all_to_all(message, ('fld', 'band'), split_axis=0, concat_axis=0, til...  48 us
    pallas_call x2, Pallas kernels, forward_call(): pl.pallas_call(functools.partial(forward_kernel, highest, chunk, stride),...  13.5 us
    unnamed x30, local copies, waits for them, and re-layouts  10.4 us
    pallas_call x2, Pallas kernels, legendre_call(): pl.pallas_call(functools.partial(legendre_kernel, start, highest), grid=(...  10 us
    pallas_call x1, Pallas kernels, inverse_call(): pl.pallas_call(functools.partial(inverse_kernel, len(values)), grid=(bloc...  7.65 us
    pallas_call x1, Pallas kernels, table_call(): pl.pallas_call(functools.partial(table_kernel, length, highest, stride),...  4.82 us
  transfers between devices with their start and end apart: 5, of which 4 were waited for; matrix products, arithmetic and copies ran while one was open for 2% of the time, Pallas kernels for 9%

profile of v3, /device:TPU:1, one launch (start us, length us, event | category | flops | bytes accessed | tf_op | source)
XLA Modules:
  0.0 199.1 jit_solution(9493380113391864739)
XLA Ops:
  7.2 0.7 all-gather.3.cloned.1.call-update
  9.9 1.3 copy-done.7
  11.9 5.9 %forward_dft.2 = bf16[8,256,128]{2,1,0:T(8,128)(2,1)} custom-call(s32[1,1]{1,0:T(1,128)S(6)} %copy.23.pair_ids, s32[1,1,2]{2,1,0:T(1,128)S(1)} %copy-done.4, f32[1,1,2]{2,1,0:T(1,128)S(1)} %copy-done.9, s32[640]{0:T(1024)S(1)} %copy-done.1, bf16[2596,256]{1,0:T(8,128)(2,1)S(1)} %bitcast.26), custom_call_target="tpu_custom_call" | custom-call | flops 680525824 | bytes 1329152 | tf_op jit(solution)/shard_map/forward_dft/pallas_call | solution.py:285
  17.7 22.1 %all-to-all-start = ((bf16[512,2,2,128]{3,2,1,0:T(2,128)(2,1)}), bf16[512,2,2,128]{3,2,1,0:T(2,128)(2,1)S(1)}, u32[]{:S(2)}, u32[]{:S(2)}) async-start(bf16[512,2,2,128]{3,2,1,0:T(2,128)(2,1)} %bitcast.3), calls=%async_computation | async-start | bytes 1048576 | tf_op jit(solution)/shard_map/all_to_all | solution.py:382
  39.9 0.7 copy-done.2
  41.3 1.3 copy-done.8
  43.2 7.7 %forward_dft.3 = bf16[8,384,128]{2,1,0:T(8,128)(2,1)} custom-call(s32[1,1]{1,0:T(1,128)S(6)} %copy.23.pair_ids, s32[1,1,2]{2,1,0:T(1,128)S(1)} %copy-done.5, f32[1,1,2]{2,1,0:T(1,128)S(1)} %copy-done.10, s32[640]{0:T(1024)S(1)} %copy-done.2, bf16[2596,256]{1,0:T(8,128)(2,1)S(1)} %bitcast.27), custom_call_target="tpu_custom_call" | custom-call | flops 1020788736 | bytes 1329152 | tf_op jit(solution)/shard_map/forward_dft/pallas_call | solution.py:285
  50.9 12.1 %all-to-all-done = bf16[512,2,2,128]{3,2,1,0:T(2,128)(2,1)S(1)} async-done(((bf16[512,2,2,128]{3,2,1,0:T(2,128)(2,1)}), bf16[512,2,2,128]{3,2,1,0:T(2,128)(2,1)S(1)}, u32[]{:S(2)}, u32[]{:S(2)}) %all-to-all-start) | async-done | bytes 524320 | tf_op jit(solution)/shard_map/all_to_all | solution.py:382
  63.0 8.6 %all-to-all-start.1 = ((bf16[512,3,2,128]{3,2,1,0:T(2,128)(2,1)}), bf16[512,3,2,128]{3,2,1,0:T(2,128)(2,1)S(1)}, u32[]{:S(2)}, u32[]{:S(2)}) async-start(bf16[512,3,2,128]{3,2,1,0:T(2,128)(2,1)} %bitcast.9), calls=%async_computation.1 | async-start | bytes 1572864 | tf_op jit(solution)/shard_map/all_to_all | solution.py:382
  71.7 1.2 copy.14
  72.9 27.4 %all-to-all-done.1 = bf16[512,3,2,128]{3,2,1,0:T(2,128)(2,1)S(1)} async-done(((bf16[512,3,2,128]{3,2,1,0:T(2,128)(2,1)}), bf16[512,3,2,128]{3,2,1,0:T(2,128)(2,1)S(1)}, u32[]{:S(2)}, u32[]{:S(2)}) %all-to-all-start.1) | async-done | bytes 786464 | tf_op jit(solution)/shard_map/all_to_all | solution.py:382
  100.3 1.4 copy.15
  102.3 5.7 %legendre_both_ways.2 = (bf16[5,64,641]{2,1,0:T(8,128)(2,1)}, bf16[3,1024,128]{2,1,0:T(8,128)(2,1)}) custom-call(s32[1]{0:T(128)} %bitcast.band, s32[640]{0:T(1024)} %wavenumbers.9, bf16[3,1024,128]{2,1,0:T(8,128)(2,1)} %bitcast.32, bf16[8,5,641,128]{3,2,1,0:T(8,128)(2,1)} %bitcast.28, f32[8,768]{1,0:T(8,128)} %broadcast_in_dim.2.damping), custom_call_target="tpu_custom_call" | custom-call | flops 1008205824 | bytes 3938304 | tf_op jit(solution)/shard_map/legendre_both_ways/pallas_call | solution.py:328
  108.0 4.3 %legendre_both_ways.3 = (bf16[5,64,641]{2,1,0:T(8,128)(2,1)}, bf16[2,1024,128]{2,1,0:T(8,128)(2,1)}) custom-call(s32[1]{0:T(128)} %bitcast.band, s32[640]{0:T(1024)} %wavenumbers.9, bf16[2,1024,128]{2,1,0:T(8,128)(2,1)} %bitcast.34, bf16[8,5,641,128]{3,2,1,0:T(8,128)(2,1)} %bitcast.29, ...), custom_call_target="tpu_custom_call", output_to_operand_aliasing={{0}: (5, {})} | custom-call | flops 672137216 | bytes 2625536 | tf_op jit(solution)/shard_map/legendre_both_ways/pallas_call | solution.py:328
  112.4 2.2 %copy.21 = bf16[2,512,2,128]{3,2,0,1:T(2,128)(2,1)} copy(bf16[2,512,2,128]{3,2,1,0:T(2,128)(2,1)} %bitcast.39) | data formatting | bytes 1048576 | tf_op jit(solution)/shard_map/reshape | solution.py:412
  114.6 8.6 %all-to-all-start.3 = ((bf16[512,2,2,128]{3,2,1,0:T(2,128)(2,1)}), bf16[512,2,2,128]{3,2,1,0:T(2,128)(2,1)S(1)}, u32[]{:S(2)}, u32[]{:S(2)}) async-start(bf16[512,2,2,128]{3,2,1,0:T(2,128)(2,1)} %bitcast.25), calls=%async_computation.3 | async-start | bytes 1048576 | tf_op jit(solution)/shard_map/all_to_all | solution.py:382
  123.2 1.4 copy.20
  124.6 21.8 %all-to-all-done.3 = bf16[512,2,2,128]{3,2,1,0:T(2,128)(2,1)S(1)} async-done(((bf16[512,2,2,128]{3,2,1,0:T(2,128)(2,1)}), bf16[512,2,2,128]{3,2,1,0:T(2,128)(2,1)S(1)}, u32[]{:S(2)}, u32[]{:S(2)}) %all-to-all-start.3) | async-done | bytes 524320 | tf_op jit(solution)/shard_map/all_to_all | solution.py:382
  146.5 8.6 %all-to-all-start.2 = ((bf16[512,3,2,128]{3,2,1,0:T(2,128)(2,1)}), bf16[512,3,2,128]{3,2,1,0:T(2,128)(2,1)S(1)}, u32[]{:S(2)}, u32[]{:S(2)}) async-start(bf16[512,3,2,128]{3,2,1,0:T(2,128)(2,1)} %bitcast.24), calls=%async_computation.2 | async-start | bytes 1572864 | tf_op jit(solution)/shard_map/all_to_all | solution.py:382
  155.1 4.8 %inverse_table.1.refs_2_ = bf16[2688,1280]{1,0:T(8,128)(2,1)S(1)} custom-call(s32[1,1]{1,0:T(1,128)S(6)} %copy.23.pair_ids, s32[1,1,2]{2,1,0:T(1,128)S(1)} %copy-done.6, s32[640]{0:T(1024)S(1)} %copy-done.3), custom_call_target="tpu_custom_call" | custom-call | flops 26583040 | bytes 6645760 | tf_op jit(solution)/shard_map/inverse_table/pallas_call | solution.py:308
  160.0 2.8 %copy-done = bf16[2688,1280]{1,0:T(8,128)(2,1)} copy-done((bf16[2688,1280]{1,0:T(8,128)(2,1)}, bf16[2688,1280]{1,0:T(8,128)(2,1)S(1)}, u32[]{:S(2)}) %copy-start) | copy-done | bytes 6881304
  162.8 21.0 %all-to-all-done.2 = bf16[512,3,2,128]{3,2,1,0:T(2,128)(2,1)S(1)} async-done(((bf16[512,3,2,128]{3,2,1,0:T(2,128)(2,1)}), bf16[512,3,2,128]{3,2,1,0:T(2,128)(2,1)S(1)}, u32[]{:S(2)}, u32[]{:S(2)}) %all-to-all-start.2) | async-done | bytes 786464 | tf_op jit(solution)/shard_map/all_to_all | solution.py:382
  183.7 0.9 copy-done.11
  184.6 7.6 %inverse_dft.1 = bf16[2596,256]{1,0:T(8,128)(2,1)} custom-call(s32[1,1]{1,0:T(1,128)S(6)} %copy.23.pair_ids, bf16[8,384,128]{2,1,0:T(8,128)(2,1)} %bitcast.30, bf16[8,256,128]{2,1,0:T(8,128)(2,1)} %bitcast.33, bf16[2688,1280]{1,0:T(8,128)(2,1)} %copy-done), custom_call_target="tpu_custom_call" | custom-call | flops 1701314560 | bytes 7974912 | tf_op jit(solution)/shard_map/inverse_dft/pallas_call | solution.py:361
  (29 shorter events, 4.0 us)
Async XLA Ops:
  7.2 64.5 %copy-start.14 = (f32[640]{0:T(1024)S(1)}, f32[640]{0:T(1024)}, u32[]{:S(2)}) copy-start(f32[640]{0:T(1024)} %param.13) | copy-start | bytes 7684
  7.2 94.5 %all-gather.3.cloned.1.call-start = ((), (), s32[]{:S(2)}) async-start(), calls=%async_computation.4 | async-start | bytes 7464960 | tf_op jit(solution)/shard_map/all_gather | solution.py:392
  8.6 0.7 copy-start.1
  9.2 0.7 copy-start.4
  9.9 1.3 copy-start.7
  11.2 0.7 copy-start.9
  17.7 45.3 %all-to-all-start = ((bf16[512,2,2,128]{3,2,1,0:T(2,128)(2,1)}), bf16[512,2,2,128]{3,2,1,0:T(2,128)(2,1)S(1)}, u32[]{:S(2)}, u32[]{:S(2)}) async-start(bf16[512,2,2,128]{3,2,1,0:T(2,128)(2,1)} %bitcast.3), calls=%async_computation | async-start | bytes 1048576 | tf_op jit(solution)/shard_map/all_to_all | solution.py:382
  39.9 0.7 copy-start.2
  40.6 0.7 copy-start.5
  41.3 1.3 copy-start.8
  42.6 0.7 copy-start.10
  63.0 37.3 %all-to-all-start.1 = ((bf16[512,3,2,128]{3,2,1,0:T(2,128)(2,1)}), bf16[512,3,2,128]{3,2,1,0:T(2,128)(2,1)S(1)}, u32[]{:S(2)}, u32[]{:S(2)}) async-start(bf16[512,3,2,128]{3,2,1,0:T(2,128)(2,1)} %bitcast.9), calls=%async_computation.1 | async-start | bytes 1572864 | tf_op jit(solution)/shard_map/all_to_all | solution.py:382
  108.0 15.2 %copy-start.13 = (bf16[3,1024,128]{2,1,0:T(8,128)(2,1)S(1)}, bf16[3,1024,128]{2,1,0:T(8,128)(2,1)}, u32[]{:S(2)}) copy-start(bf16[3,1024,128]{2,1,0:T(8,128)(2,1)} %get-tuple-element.8) | copy-start | bytes 2359300
  108.0 47.1 %copy-start.3 = (s32[640]{0:T(1024)S(1)}, s32[640]{0:T(1024)}, u32[]{:S(2)}) copy-start(s32[640]{0:T(1024)} %wavenumbers.9) | copy-start | bytes 7684
  108.0 47.1 %copy-start.6 = (s32[1,1,2]{2,1,0:T(1,128)S(1)}, s32[1,1,2]{2,1,0:T(1,128)}, u32[]{:S(2)}) copy-start(s32[1,1,2]{2,1,0:T(1,128)} %trims.5) | copy-start | bytes 28
  114.6 31.9 %all-to-all-start.3 = ((bf16[512,2,2,128]{3,2,1,0:T(2,128)(2,1)}), bf16[512,2,2,128]{3,2,1,0:T(2,128)(2,1)S(1)}, u32[]{:S(2)}, u32[]{:S(2)}) async-start(bf16[512,2,2,128]{3,2,1,0:T(2,128)(2,1)} %bitcast.25), calls=%async_computation.3 | async-start | bytes 1048576 | tf_op jit(solution)/shard_map/all_to_all | solution.py:382
  146.5 37.3 %copy-start.12 = (bf16[512,2,2,128]{3,2,1,0:T(2,128)(2,1)}, bf16[512,2,2,128]{3,2,1,0:T(2,128)(2,1)S(1)}, u32[]{:S(2)}) copy-start(bf16[512,2,2,128]{3,2,1,0:T(2,128)(2,1)S(1)} %all-to-all-done.3) | copy-start | bytes 1572868
  146.5 37.3 %all-to-all-start.2 = ((bf16[512,3,2,128]{3,2,1,0:T(2,128)(2,1)}), bf16[512,3,2,128]{3,2,1,0:T(2,128)(2,1)S(1)}, u32[]{:S(2)}, u32[]{:S(2)}) async-start(bf16[512,3,2,128]{3,2,1,0:T(2,128)(2,1)} %bitcast.24), calls=%async_computation.2 | async-start | bytes 1572864 | tf_op jit(solution)/shard_map/all_to_all | solution.py:382
  159.9 2.8 %copy-start = (bf16[2688,1280]{1,0:T(8,128)(2,1)}, bf16[2688,1280]{1,0:T(8,128)(2,1)S(1)}, u32[]{:S(2)}) copy-start(bf16[2688,1280]{1,0:T(8,128)(2,1)S(1)} %inverse_table.1.refs_2_) | copy-start | bytes 20643844
  183.7 0.9 copy-start.11
Sparse Core Ops, SparseCore 0:
  10.2 59.1 all-gather.2

commit v4 on v3

--- a/solution.py
+++ b/solution.py
@@ -13,8 +13,9 @@
 INVERSE_BLOCK = 656
 STRIP = 64
 VMEM_BYTES = 40 * 1024 * 1024
-LARGE_VMEM_BYTES = 57_000_000
-CHUNKS = ((0, 3), (3, 5))
+LARGE_VMEM_BYTES = 50_000_000
+WHOLE_VMEM_BYTES = 58_000_000
+CHUNKS = ((0, 5),)
 
 
 def unit_circle(waves, points, count):
@@ -116,32 +117,31 @@
 
         fill_table(1, chosen, step_waves, facts, blocks, write)
 
-    full = length // STEP
-    straddle = first // STEP
+    split = -(-(length // 2) // STEP) * STEP
+    totals[0] = jnp.zeros(totals.shape[1:], jnp.float32)
+    totals[1] = jnp.dot(table[:, split:length], grid[split:, :], preferred_element_type=jnp.float32)
     position = lax.broadcasted_iota(jnp.int32, (STEP, fields), 0)
-
-    def product(start, size, data):
-        return jnp.dot(table[:, pl.ds(start, size)], data, preferred_element_type=jnp.float32)
-
-    def data_of(block):
-        return grid[pl.ds(pl.multiple_of(block * STEP, STEP), STEP), :]
-
-    def add(cycle):
-        def body(block, carry):
-            totals[cycle] += product(pl.multiple_of(block * STEP, STEP), STEP, data_of(block))
-            return carry
-
-        return body
-
-    data = data_of(straddle)
-    before = position + straddle * STEP < first
-    nothing = jnp.zeros_like(data)
-    start = pl.multiple_of(straddle * STEP, STEP)
-    totals[0] = product(start, STEP, jnp.where(before, data, nothing))
-    totals[1] = product(start, STEP, jnp.where(before, nothing, data))
-    lax.fori_loop(0, straddle, add(0), 0)
-    lax.fori_loop(straddle + 1, full, add(1), 0)
-    totals[1] += product(full * STEP, length - full * STEP, grid[full * STEP:, :])
+    for start in range(0, split, STEP):
+        block = slice(start, start + STEP)
+        data = grid[block, :]
+        nothing = jnp.zeros_like(data)
+
+        def add(cycle, data):
+            totals[cycle] += jnp.dot(table[:, block], data, preferred_element_type=jnp.float32)
+
+        @pl.when(first >= start + STEP)
+        def _():
+            add(0, data)
+
+        @pl.when(first <= start)
+        def _():
+            add(1, data)
+
+        @pl.when((first > start) & (first < start + STEP))
+        def _():
+            before = position + start < first
+            add(0, jnp.where(before, data, nothing))
+            add(1, jnp.where(before, nothing, data))
 
     share = LANES // 4
     for group in range(fields // share):
@@ -189,9 +189,7 @@
     spectrum, rebuilt = refs[-2:]
     groups, _, degrees, each = legendre.shape
     matrix = jnp.concatenate([legendre[group, 0] for group in range(groups)], axis=1)
-    sums = lax.dot_general(
-        values[0].T, matrix, (((1,), (1,)), ((), ())), preferred_element_type=jnp.float32
-    )
+    sums = jnp.dot(matrix, values[0], preferred_element_type=jnp.float32).T
     fields = sums.shape[0] // 2
     pair = band[0] + start + pl.program_id(0)
     first_wave = wavenumbers[2 * pair]
@@ -294,7 +292,7 @@
             pltpu.VMEM((width, LANES), jnp.float32),
             pltpu.VMEM((width, LANES), jnp.float32),
         ],
-        compiler_params=parameters(),
+        compiler_params=parameters(limit=WHOLE_VMEM_BYTES),
         cost_estimate=pl.CostEstimate(
             flops=2 * length * fields * 2 * width, bytes_accessed=length * fields * 2, transcendentals=0
         ),

time: 200 us -> 159 us (0.80)
  starting transfers between devices: 48.1 us -> 33 us
  local copies, waits for them, and re-layouts: 17.2 us -> 5.72 us
  waiting for transfers between devices: 83 us -> 73 us
  Pallas kernels: 36 us -> 32 us
    all_to_all x4 -> x2, starting transfers between devices: 48 us -> 33 us  [exchange(): lax.all_to_all(message, ('fld', 'band'), split_axis=0, concat_axis=0, til...]
    all_to_all x4 -> x2, waiting for transfers between devices: 82.3 us -> 72.3 us  [exchange(): lax.all_to_all(message, ('fld', 'band'), split_axis=0, concat_axis=0, til...]
    unnamed x30 -> x8, local copies, waits for them, and re-layouts: 10.4 us -> 2.86 us
    pallas_call x2 -> x1, Pallas kernels: 10 us -> 8.44 us  [legendre_call(): pl.pallas_call(functools.partial(legendre_kernel, start, highest), grid=(...]
    pallas_call x2 -> x1, Pallas kernels: 13.5 us -> 12 us  [forward_call(): pl.pallas_call(functools.partial(forward_kernel, highest, chunk, stride),...]
  transfers between devices with their start and end apart: 5 -> 3, of which waited for: 4 -> 2; matrix products, arithmetic and copies ran while one was open for 2% -> 1% of each run, Pallas kernels for 9% -> 10%
where the time goes in v4:
time: 159 us
  waiting for transfers between devices  73 us (46%)
  starting transfers between devices  33 us (21%)
  Pallas kernels  32 us (20%)
  between operations  14.8 us (9%)
  local copies, waits for them, and re-layouts  5.72 us (4%)
    all_to_all x2, waiting for transfers between devices, exchange(): lax.all_to_all(message, ('fld', 'band'), split_axis=0, concat_axis=0, til...  72.3 us
    all_to_all x2, starting transfers between devices, exchange(): lax.all_to_all(message, ('fld', 'band'), split_axis=0, concat_axis=0, til...  33 us
    pallas_call x1, Pallas kernels, forward_call(): pl.pallas_call(functools.partial(forward_kernel, highest, chunk, stride),...  12 us
    pallas_call x1, Pallas kernels, legendre_call(): pl.pallas_call(functools.partial(legendre_kernel, start, highest), grid=(...  8.44 us
    pallas_call x1, Pallas kernels, inverse_call(): pl.pallas_call(functools.partial(inverse_kernel, len(values)), grid=(bloc...  7.35 us
    pallas_call x1, Pallas kernels, table_call(): pl.pallas_call(functools.partial(table_kernel, length, highest, stride),...  4.23 us
  transfers between devices with their start and end apart: 3, of which 2 were waited for; matrix products, arithmetic and copies ran while one was open for 1% of the time, Pallas kernels for 10%

profile of v4, /device:TPU:1, one launch (start us, length us, event | category | flops | bytes accessed | tf_op | source)
XLA Modules:
  0.0 158.6 jit_solution(12095318535931678800)
XLA Ops:
  7.2 0.0 all-gather.3.cloned.1.call-start
  7.2 0.7 all-gather.3.cloned.1.call-update
  8.5 12.0 %forward_dft.1 = bf16[8,640,128]{2,1,0:T(8,128)(2,1)} custom-call(s32[1,1]{1,0:T(1,128)S(6)} %copy.15.pair_ids, s32[1,1,2]{2,1,0:T(1,128)} %trims.3, f32[1,1,2]{2,1,0:T(1,128)} %weights.1, s32[640]{0:T(1024)} %wavenumbers.5, bf16[2596,256]{1,0:T(8,128)(2,1)} %bitcast.26), custom_call_target="tpu_custom_call" | custom-call | flops 1701314560 | bytes 1329152 | tf_op jit(solution)/shard_map/forward_dft/pallas_call | solution.py:283
  20.5 0.0 copy-start.3
  20.5 22.3 %all-to-all-start = ((bf16[512,5,2,128]{3,2,1,0:T(2,128)(2,1)}), bf16[512,5,2,128]{3,2,1,0:T(2,128)(2,1)S(1)}, u32[]{:S(2)}, u32[]{:S(2)}) async-start(bf16[512,5,2,128]{3,2,1,0:T(2,128)(2,1)} %bitcast.24), calls=%async_computation | async-start | bytes 2621440 | tf_op jit(solution)/shard_map/all_to_all | solution.py:380
  42.8 0.0 copy-done.3
  42.9 39.7 %all-to-all-done = bf16[512,5,2,128]{3,2,1,0:T(2,128)(2,1)S(1)} async-done(((bf16[512,5,2,128]{3,2,1,0:T(2,128)(2,1)}), bf16[512,5,2,128]{3,2,1,0:T(2,128)(2,1)S(1)}, u32[]{:S(2)}, u32[]{:S(2)}) %all-to-all-start) | async-done | bytes 1310752 | tf_op jit(solution)/shard_map/all_to_all | solution.py:380
  82.6 0.0 copy-start.1
  82.6 0.9 copy.11
  83.5 0.0 all-gather.3.cloned.1.call-done
  83.5 0.0 copy-done.1
  83.5 8.4 %legendre_both_ways.1 = (bf16[5,64,641]{2,1,0:T(8,128)(2,1)}, bf16[5,1024,128]{2,1,0:T(8,128)(2,1)S(1)}) custom-call(s32[1]{0:T(128)} %bitcast.band, s32[640]{0:T(1024)S(1)} %copy-done.1, bf16[5,1024,128]{2,1,0:T(8,128)(2,1)S(1)} %bitcast.19, bf16[8,5,641,128]{3,2,1,0:T(8,128)(2,1)} %bitcast.21, f32[8,768]{1,0:T(8,128)S(1)} %broadcast_in_dim.2.damping), custom_call_target="tpu_custom_call" | custom-call | flops 1680343040 | bytes 6563840 | tf_op jit(solution)/shard_map/legendre_both_ways/pallas_call | solution.py:326
  92.0 2.0 %copy.14 = bf16[5,512,2,128]{3,2,0,1:T(2,128)(2,1)} copy(bf16[5,512,2,128]{3,2,1,0:T(2,128)(2,1)S(1)} %bitcast.20) | data formatting | bytes 2621440 | tf_op jit(solution)/shard_map/reshape | solution.py:410
  93.9 0.0 copy-start.2
  93.9 10.7 %all-to-all-start.1 = ((bf16[512,5,2,128]{3,2,1,0:T(2,128)(2,1)}), bf16[512,5,2,128]{3,2,1,0:T(2,128)(2,1)S(1)}, u32[]{:S(2)}, u32[]{:S(2)}) async-start(bf16[512,5,2,128]{3,2,1,0:T(2,128)(2,1)} %bitcast.17), calls=%async_computation.1 | async-start | bytes 2621440 | tf_op jit(solution)/shard_map/all_to_all | solution.py:380
  104.6 0.0 copy-done.2
  104.6 4.2 %inverse_table.1.refs_1_ = bf16[2688,1280]{1,0:T(8,128)(2,1)S(1)} custom-call(s32[1,1]{1,0:T(1,128)S(6)} %copy.15.pair_ids, s32[1,1,2]{2,1,0:T(1,128)S(1)} %copy-done.2, s32[640]{0:T(1024)S(1)} %copy-done.1), custom_call_target="tpu_custom_call" | custom-call | flops 26583040 | bytes 6645760 | tf_op jit(solution)/shard_map/inverse_table/pallas_call | solution.py:306
  108.9 0.0 copy-start
  108.9 2.8 %copy-done = bf16[2688,1280]{1,0:T(8,128)(2,1)} copy-done((bf16[2688,1280]{1,0:T(8,128)(2,1)}, bf16[2688,1280]{1,0:T(8,128)(2,1)S(1)}, u32[]{:S(2)}) %copy-start) | copy-done | bytes 6881304
  111.7 32.6 %all-to-all-done.1 = bf16[512,5,2,128]{3,2,1,0:T(2,128)(2,1)S(1)} async-done(((bf16[512,5,2,128]{3,2,1,0:T(2,128)(2,1)}), bf16[512,5,2,128]{3,2,1,0:T(2,128)(2,1)S(1)}, u32[]{:S(2)}, u32[]{:S(2)}) %all-to-all-start.1) | async-done | bytes 1310752 | tf_op jit(solution)/shard_map/all_to_all | solution.py:380
  144.4 7.4 %inverse_dft.1 = bf16[2596,256]{1,0:T(8,128)(2,1)} custom-call(s32[1,1]{1,0:T(1,128)S(6)} %copy.15.pair_ids, bf16[8,640,128]{2,1,0:T(8,128)(2,1)S(1)} %bitcast.18, bf16[2688,1280]{1,0:T(8,128)(2,1)} %copy-done), custom_call_target="tpu_custom_call" | custom-call | flops 1701314560 | bytes 7974912 | tf_op jit(solution)/shard_map/inverse_dft/pallas_call | solution.py:359
  (2 shorter events, 0.0 us)
Async XLA Ops:
  7.2 76.3 %all-gather.3.cloned.1.call-start = ((), (), s32[]{:S(2)}) async-start(), calls=%async_computation.2 | async-start | bytes 7464960 | tf_op jit(solution)/shard_map/all_gather | solution.py:390
  20.5 22.3 %copy-start.3 = (f32[640]{0:T(1024)S(1)}, f32[640]{0:T(1024)}, u32[]{:S(2)}) copy-start(f32[640]{0:T(1024)} %param.13) | copy-start | bytes 7684
  20.5 62.0 %all-to-all-start = ((bf16[512,5,2,128]{3,2,1,0:T(2,128)(2,1)}), bf16[512,5,2,128]{3,2,1,0:T(2,128)(2,1)S(1)}, u32[]{:S(2)}, u32[]{:S(2)}) async-start(bf16[512,5,2,128]{3,2,1,0:T(2,128)(2,1)} %bitcast.24), calls=%async_computation | async-start | bytes 2621440 | tf_op jit(solution)/shard_map/all_to_all | solution.py:380
  82.6 0.9 copy-start.1
  93.9 10.7 %copy-start.2 = (s32[1,1,2]{2,1,0:T(1,128)S(1)}, s32[1,1,2]{2,1,0:T(1,128)}, u32[]{:S(2)}) copy-start(s32[1,1,2]{2,1,0:T(1,128)} %trims.3) | copy-start | bytes 28
  93.9 50.4 %all-to-all-start.1 = ((bf16[512,5,2,128]{3,2,1,0:T(2,128)(2,1)}), bf16[512,5,2,128]{3,2,1,0:T(2,128)(2,1)S(1)}, u32[]{:S(2)}, u32[]{:S(2)}) async-start(bf16[512,5,2,128]{3,2,1,0:T(2,128)(2,1)} %bitcast.17), calls=%async_computation.1 | async-start | bytes 2621440 | tf_op jit(solution)/shard_map/all_to_all | solution.py:380
  108.9 2.9 %copy-start = (bf16[2688,1280]{1,0:T(8,128)(2,1)}, bf16[2688,1280]{1,0:T(8,128)(2,1)S(1)}, u32[]{:S(2)}) copy-start(bf16[2688,1280]{1,0:T(8,128)(2,1)S(1)} %inverse_table.1.refs_1_) | copy-start | bytes 20643844
Sparse Core Ops, SparseCore 0:
  10.2 66.1 all-gather.2

commit v5 on v4

--- a/solution.py
+++ b/solution.py
@@ -87,9 +87,12 @@
             target += STRIP
 
 
-def forward_kernel(highest, chunk, stride, pair_ids, trims, weights, wavenumbers, grid, packed, table, totals, raw, columns, rows):
+def forward_kernel(highest, chunk, stride, pair_ids, trims, weights, wavenumbers, grid_hbm, packed_hbm,
+                   grid, packed, table, totals, raw, columns, rows, sems):
     length, fields = grid.shape
     width = columns.shape[0]
+    arriving = pltpu.make_async_copy(grid_hbm, grid, sems.at[packed.shape[0]])
+    arriving.start()
     quarter = width // 2
     facts = cycle_facts(length, highest, pair_ids, trims)
     first, counts, _ = facts
@@ -117,6 +120,7 @@
 
         fill_table(1, chosen, step_waves, facts, blocks, write)
 
+    arriving.wait()
     split = -(-(length // 2) // STEP) * STEP
     totals[0] = jnp.zeros(totals.shape[1:], jnp.float32)
     totals[1] = jnp.dot(table[:, split:length], grid[split:, :], preferred_element_type=jnp.float32)
@@ -144,6 +148,7 @@
             add(1, jnp.where(before, nothing, data))
 
     share = LANES // 4
+    leaving = []
     for group in range(fields // share):
         lanes = slice(group * share, (group + 1) * share)
         for cycle in range(2):
@@ -157,6 +162,10 @@
                     joined[pair * STRIP:(pair + 1) * STRIP]
                 )
         packed[group] = rows[...].astype(jnp.bfloat16)
+        leaving.append(pltpu.make_async_copy(packed.at[group], packed_hbm.at[group], sems.at[group]))
+        leaving[-1].start()
+    for copy in leaving:
+        copy.wait()
 
 
 def table_kernel(length, highest, stride, pair_ids, trims, wavenumbers, table, raw, columns):
@@ -189,7 +198,8 @@
     spectrum, rebuilt = refs[-2:]
     groups, _, degrees, each = legendre.shape
     matrix = jnp.concatenate([legendre[group, 0] for group in range(groups)], axis=1)
-    sums = jnp.dot(matrix, values[0], preferred_element_type=jnp.float32).T
+    rows = (groups * each, LANES)
+    sums = jnp.dot(matrix, values.reshape(*rows)[...], preferred_element_type=jnp.float32).T
     fields = sums.shape[0] // 2
     pair = band[0] + start + pl.program_id(0)
     first_wave = wavenumbers[2 * pair]
@@ -209,18 +219,24 @@
     row = lax.broadcasted_iota(jnp.int32, products.shape, 0)
     wave = jnp.where(row < fields, first_wave, second_wave)
     doubled = products * jnp.where(wave == 0, 1.0, 2.0)
-    rebuilt[0] = doubled.astype(jnp.bfloat16).T
+    rebuilt.reshape(*rows)[...] = doubled.astype(jnp.bfloat16).T
 
 
 def inverse_kernel(chunks, pair_ids, *refs):
     values = refs[:chunks]
-    table, restored, rows, factors = refs[chunks:]
+    table_hbm, restored, table, rows, factors, sems = refs[chunks:]
     block = pl.program_id(0)
     first = 20 + 4 * pair_ids[0, 0]
     share = LANES // 4
 
+    def arriving(block):
+        part = pl.ds(pl.multiple_of(block * INVERSE_BLOCK, 16), INVERSE_BLOCK)
+        return pltpu.make_async_copy(table_hbm.at[part, :], table.at[part, :], sems.at[block])
+
     @pl.when(block == 0)
     def _():
+        for one in range(sems.shape[0]):
+            arriving(one).start()
         base = 0
         for chunk in values:
             groups, height, _ = chunk.shape
@@ -248,10 +264,14 @@
                         ] = jnp.concatenate([one[:, source:source + share] for one in turned], axis=1)
             base += 4 * quarter
 
+    arriving(block).wait()
+    start = pl.multiple_of(block * INVERSE_BLOCK, 16)
+
     def product(cycle):
-        return jnp.dot(table[...], factors[cycle], preferred_element_type=jnp.float32)
-
-    start = block * INVERSE_BLOCK
+        return jnp.dot(
+            table[pl.ds(start, INVERSE_BLOCK), :], factors[cycle], preferred_element_type=jnp.float32
+        )
+
     end = start + INVERSE_BLOCK
 
     @pl.when(end <= first)
@@ -280,17 +300,21 @@
     length, fields = points.shape
     width = 2 * STRIP * (chunk[1] - chunk[0])
     blocks = -(-length // LANES)
+    groups = 4 * fields // LANES
     return pl.pallas_call(
         functools.partial(forward_kernel, highest, chunk, stride),
-        in_specs=[SMEM, SMEM, SMEM, VMEM, VMEM],
-        out_specs=VMEM,
-        out_shape=jax.ShapeDtypeStruct((4 * fields // LANES, width, LANES), jnp.bfloat16),
+        in_specs=[SMEM, SMEM, SMEM, VMEM, pl.BlockSpec(memory_space=pl.ANY)],
+        out_specs=pl.BlockSpec(memory_space=pl.ANY),
+        out_shape=jax.ShapeDtypeStruct((groups, width, LANES), jnp.bfloat16),
         scratch_shapes=[
+            pltpu.VMEM((length, fields), jnp.bfloat16),
+            pltpu.VMEM((groups, width, LANES), jnp.bfloat16),
             pltpu.VMEM((2 * width, blocks * LANES), jnp.bfloat16),
             pltpu.VMEM((2, 2 * width, fields), jnp.float32),
             pltpu.VMEM((wavenumbers.shape[0], LANES), jnp.float32),
             pltpu.VMEM((width, LANES), jnp.float32),
             pltpu.VMEM((width, LANES), jnp.float32),
+            pltpu.SemaphoreType.DMA((groups + 1,)),
         ],
         compiler_params=parameters(limit=WHOLE_VMEM_BYTES),
         cost_estimate=pl.CostEstimate(
@@ -320,7 +344,9 @@
 
 def legendre_call(highest, start, band, wavenumbers, values, gathered, damping, spectrum):
     groups, local_pairs, degrees, each = gathered.shape
-    count, cycles, _ = values.shape
+    cycles = groups * each
+    count = values.shape[1]
+    pair_block = pl.BlockSpec((cycles // 2, 1, 2, LANES), lambda q: (0, q, 0, 0))
     fields = LANES // 2
     previous = [] if spectrum is None else [spectrum]
     return pl.pallas_call(
@@ -329,18 +355,18 @@
         in_specs=[
             SMEM,
             SMEM,
-            pl.BlockSpec((1, cycles, LANES), lambda q: (q, 0, 0)),
+            pair_block,
             pl.BlockSpec((groups, 1, degrees, each), lambda q: (0, q + start, 0, 0)),
             pl.BlockSpec(damping.shape, lambda q: (0, 0)),
         ]
         + [pl.BlockSpec(memory_space=pl.ANY)] * len(previous),
         out_specs=[
             pl.BlockSpec((1, fields, degrees), lambda q: (q + start, 0, 0)),
-            pl.BlockSpec((1, cycles, LANES), lambda q: (q, 0, 0)),
+            pair_block,
         ],
         out_shape=[
             jax.ShapeDtypeStruct((local_pairs, fields, degrees), jnp.bfloat16),
-            jax.ShapeDtypeStruct((count, cycles, LANES), jnp.bfloat16),
+            jax.ShapeDtypeStruct(values.shape, jnp.bfloat16),
         ],
         input_output_aliases={5: 0} if previous else {},
         compiler_params=parameters("arbitrary", limit=LARGE_VMEM_BYTES),
@@ -361,12 +387,14 @@
         grid=(blocks,),
         in_specs=[SMEM]
         + [pl.BlockSpec(one.shape, lambda i: (0, 0, 0)) for one in values]
-        + [pl.BlockSpec((INVERSE_BLOCK, total), lambda i: (i, 0))],
+        + [pl.BlockSpec(memory_space=pl.ANY)],
         out_specs=pl.BlockSpec((INVERSE_BLOCK, fields), lambda i: (i, 0)),
         out_shape=jax.ShapeDtypeStruct((length, fields), jnp.bfloat16),
         scratch_shapes=[
+            pltpu.VMEM((blocks * INVERSE_BLOCK, total), jnp.bfloat16),
             pltpu.VMEM((4, max(one.shape[1] for one in values), LANES), jnp.float32),
             pltpu.VMEM((2, total, fields), jnp.bfloat16),
+            pltpu.SemaphoreType.DMA((blocks,)),
         ],
         compiler_params=parameters("arbitrary", limit=LARGE_VMEM_BYTES),
         cost_estimate=pl.CostEstimate(
@@ -397,19 +425,17 @@
     arrived = []
     for chunk in CHUNKS:
         packed = forward_call(highest, chunk, stride, pair_ids, trims, weights, wavenumbers, points)
+        packed, trims = lax.optimization_barrier((packed, trims))
         arrived.append(exchange(packed.reshape(groups * bands, chunk[1] - chunk[0], 2, LANES)))
     table = table_call(highest, length, stride, pair_ids, trims, wavenumbers)
     spectrum = None
     returned = []
     for (start, end), message in zip(CHUNKS, arrived):
-        count = end - start
-        values = message.transpose(1, 0, 2, 3).reshape(count, groups * local_cycles, LANES)
         spectrum, rebuilt = legendre_call(
-            highest, start, band, wavenumbers, values, gathered, padded, spectrum
+            highest, start, band, wavenumbers, message, gathered, padded, spectrum
         )
-        leaving = rebuilt.reshape(count, groups * bands, 2, LANES).transpose(1, 0, 2, 3)
-        message = exchange(leaving)
-        returned.append(message.reshape(groups, bands * count * 2, LANES))
+        message = exchange(rebuilt)
+        returned.append(message.reshape(groups, bands * (end - start) * 2, LANES))
     restored = inverse_call(length, fields, pair_ids, returned, table)
     return (
         spectrum.reshape(local_pairs, 2, fields // groups, degrees),

time: 159 us -> 157 us (0.987)
  local copies, waits for them, and re-layouts: 5.72 us -> 2.87 us
  starting transfers between devices: 33 us -> 34.8 us
    reshape x1 -> x0, local copies, waits for them, and re-layouts: 1.96 us -> none  [on_device(): rebuilt.reshape(count, groups * bands, 2, LANES).transpose(1, 0, 2, 3)]
    all_to_all x2, starting transfers between devices: 33 us -> 34.8 us  [exchange(): lax.all_to_all(message, ('fld', 'band'), split_axis=0, concat_axis=0, til...]
  transfers between devices with their start and end apart: 3 -> 3, of which waited for: 2 -> 2; matrix products, arithmetic and copies ran while one was open for 1% -> 0% of each run, Pallas kernels for 10% -> 10%
where the time goes in v5:
time: 157 us
  waiting for transfers between devices  73 us (46%)
  starting transfers between devices  34.8 us (22%)
  Pallas kernels  31.4 us (20%)
  between operations  14.8 us (9%)
  local copies, waits for them, and re-layouts  2.87 us (2%)
    all_to_all x2, waiting for transfers between devices, exchange(): lax.all_to_all(message, ('fld', 'band'), split_axis=0, concat_axis=0, til...  72.3 us
    all_to_all x2, starting transfers between devices, exchange(): lax.all_to_all(message, ('fld', 'band'), split_axis=0, concat_axis=0, til...  34.8 us
    pallas_call x1, Pallas kernels, forward_call(): pl.pallas_call(functools.partial(forward_kernel, highest, chunk, stride),...  11.1 us
    pallas_call x1, Pallas kernels, legendre_call(): pl.pallas_call(functools.partial(legendre_kernel, start, highest), grid=(...  9.8 us
    pallas_call x1, Pallas kernels, inverse_call(): pl.pallas_call(functools.partial(inverse_kernel, len(values)), grid=(bloc...  6.3 us
    pallas_call x1, Pallas kernels, table_call(): pl.pallas_call(functools.partial(table_kernel, length, highest, stride),...  4.26 us
  transfers between devices with their start and end apart: 3, of which 2 were waited for; matrix products, arithmetic and copies ran while one was open for 0% of the time, Pallas kernels for 10%

profile of v5, /device:TPU:1, one launch (start us, length us, event | category | flops | bytes accessed | tf_op | source)
XLA Modules:
  0.0 156.9 jit_solution(13333381562350163574)
XLA Ops:
  7.2 0.0 all-gather.3.cloned.1.call-start
  7.2 0.7 all-gather.3.cloned.1.call-update
  8.5 11.1 %forward_dft.1 = bf16[8,640,128]{2,1,0:T(8,128)(2,1)} custom-call(s32[1,1]{1,0:T(1,128)S(6)} %copy.9.pair_ids, s32[1,1,2]{2,1,0:T(1,128)} %trims.2, f32[1,1,2]{2,1,0:T(1,128)} %weights.1, s32[640]{0:T(1024)} %wavenumbers.5, bf16[2596,256]{1,0:T(8,128)(2,1)} %bitcast.17), custom_call_target="tpu_custom_call" | custom-call | flops 1701314560 | bytes 1329152 | tf_op jit(solution)/shard_map/forward_dft/pallas_call | solution.py:304
  19.6 0.0 copy-start.3
  19.6 0.0 copy-start.1
  19.7 22.2 %all-to-all-start = ((bf16[512,5,2,128]{3,2,1,0:T(2,128)(2,1)}), bf16[512,5,2,128]{3,2,1,0:T(2,128)(2,1)S(1)}, u32[]{:S(2)}, u32[]{:S(2)}) async-start(bf16[512,5,2,128]{3,2,1,0:T(2,128)(2,1)} %bitcast.15), calls=%async_computation | async-start | bytes 2621440 | tf_op jit(solution)/shard_map/all_to_all | solution.py:408
  41.9 0.0 copy-done.3
  41.9 39.7 %all-to-all-done.values = bf16[512,5,2,128]{3,2,1,0:T(2,128)(2,1)S(1)} async-done(((bf16[512,5,2,128]{3,2,1,0:T(2,128)(2,1)}), bf16[512,5,2,128]{3,2,1,0:T(2,128)(2,1)S(1)}, u32[]{:S(2)}, u32[]{:S(2)}) %all-to-all-start) | async-done | bytes 1310752 | tf_op jit(solution)/shard_map/all_to_all | solution.py:408
  81.6 0.0 all-gather.3.cloned.1.call-done
  81.6 0.0 copy-done.1
  81.6 9.8 %legendre_both_ways.1 = (bf16[5,64,641]{2,1,0:T(8,128)(2,1)}, bf16[512,5,2,128]{3,2,1,0:T(2,128)(2,1)}) custom-call(s32[1]{0:T(128)} %bitcast.band, s32[640]{0:T(1024)S(1)} %copy-done.1, bf16[512,5,2,128]{3,2,1,0:T(2,128)(2,1)S(1)} %all-to-all-done.values, bf16[8,5,641,128]{3,2,1,0:T(8,128)(2,1)} %bitcast.13, f32[8,768]{1,0:T(8,128)S(1)} %broadcast_in_dim.2.damping), custom_call_target="tpu_custom_call" | custom-call | flops 1680343040 | bytes 6563840 | tf_op jit(solution)/shard_map/legendre_both_ways/pallas_call | solution.py:352
  91.4 0.0 copy-start.2
  91.4 12.6 %all-to-all-start.1 = ((bf16[512,5,2,128]{3,2,1,0:T(2,128)(2,1)}), bf16[512,5,2,128]{3,2,1,0:T(2,128)(2,1)S(1)}, u32[]{:S(2)}, u32[]{:S(2)}) async-start(bf16[512,5,2,128]{3,2,1,0:T(2,128)(2,1)} %get-tuple-element.8), calls=%async_computation.1 | async-start | bytes 2621440 | tf_op jit(solution)/shard_map/all_to_all | solution.py:408
  104.0 0.0 copy-done.2
  104.0 4.3 %inverse_table.1.refs_1_ = bf16[2688,1280]{1,0:T(8,128)(2,1)S(1)} custom-call(s32[1,1]{1,0:T(1,128)S(6)} %copy.9.pair_ids, s32[1,1,2]{2,1,0:T(1,128)S(1)} %copy-done.2, s32[640]{0:T(1024)S(1)} %copy-done.1), custom_call_target="tpu_custom_call" | custom-call | flops 26583040 | bytes 6645760 | tf_op jit(solution)/shard_map/inverse_table/pallas_call | solution.py:330
  108.3 0.0 copy-start
  108.3 2.8 %copy-done = bf16[2688,1280]{1,0:T(8,128)(2,1)} copy-done((bf16[2688,1280]{1,0:T(8,128)(2,1)}, bf16[2688,1280]{1,0:T(8,128)(2,1)S(1)}, u32[]{:S(2)}) %copy-start) | copy-done | bytes 6881304
  111.2 32.6 %all-to-all-done.1 = bf16[512,5,2,128]{3,2,1,0:T(2,128)(2,1)S(1)} async-done(((bf16[512,5,2,128]{3,2,1,0:T(2,128)(2,1)}), bf16[512,5,2,128]{3,2,1,0:T(2,128)(2,1)S(1)}, u32[]{:S(2)}, u32[]{:S(2)}) %all-to-all-start.1) | async-done | bytes 1310752 | tf_op jit(solution)/shard_map/all_to_all | solution.py:408
  143.8 6.3 %inverse_dft.1 = bf16[2596,256]{1,0:T(8,128)(2,1)} custom-call(s32[1,1]{1,0:T(1,128)S(6)} %copy.9.pair_ids, bf16[8,640,128]{2,1,0:T(8,128)(2,1)S(1)} %bitcast.12, bf16[2688,1280]{1,0:T(8,128)(2,1)} %copy-done), custom_call_target="tpu_custom_call" | custom-call | flops 1701314560 | bytes 7974912 | tf_op jit(solution)/shard_map/inverse_dft/pallas_call | solution.py:385
  (2 shorter events, 0.0 us)
Async XLA Ops:
  7.2 74.5 %all-gather.3.cloned.1.call-start = ((), (), s32[]{:S(2)}) async-start(), calls=%async_computation.2 | async-start | bytes 7464960 | tf_op jit(solution)/shard_map/all_gather | solution.py:418
  19.6 22.3 %copy-start.3 = (f32[640]{0:T(1024)S(1)}, f32[640]{0:T(1024)}, u32[]{:S(2)}) copy-start(f32[640]{0:T(1024)} %param.13) | copy-start | bytes 7684
  19.6 62.0 %copy-start.1 = (s32[640]{0:T(1024)S(1)}, s32[640]{0:T(1024)}, u32[]{:S(2)}) copy-start(s32[640]{0:T(1024)} %wavenumbers.5) | copy-start | bytes 7684
  19.7 62.0 %all-to-all-start = ((bf16[512,5,2,128]{3,2,1,0:T(2,128)(2,1)}), bf16[512,5,2,128]{3,2,1,0:T(2,128)(2,1)S(1)}, u32[]{:S(2)}, u32[]{:S(2)}) async-start(bf16[512,5,2,128]{3,2,1,0:T(2,128)(2,1)} %bitcast.15), calls=%async_computation | async-start | bytes 2621440 | tf_op jit(solution)/shard_map/all_to_all | solution.py:408
  91.4 12.6 %copy-start.2 = (s32[1,1,2]{2,1,0:T(1,128)S(1)}, s32[1,1,2]{2,1,0:T(1,128)}, u32[]{:S(2)}) copy-start(s32[1,1,2]{2,1,0:T(1,128)} %trims.2) | copy-start | bytes 28
  91.4 52.3 %all-to-all-start.1 = ((bf16[512,5,2,128]{3,2,1,0:T(2,128)(2,1)}), bf16[512,5,2,128]{3,2,1,0:T(2,128)(2,1)S(1)}, u32[]{:S(2)}, u32[]{:S(2)}) async-start(bf16[512,5,2,128]{3,2,1,0:T(2,128)(2,1)} %get-tuple-element.8), calls=%async_computation.1 | async-start | bytes 2621440 | tf_op jit(solution)/shard_map/all_to_all | solution.py:408
  108.3 2.9 %copy-start = (bf16[2688,1280]{1,0:T(8,128)(2,1)}, bf16[2688,1280]{1,0:T(8,128)(2,1)S(1)}, u32[]{:S(2)}) copy-start(bf16[2688,1280]{1,0:T(8,128)(2,1)S(1)} %inverse_table.1.refs_1_) | copy-start | bytes 20643844
Sparse Core Ops, SparseCore 0:
  10.2 66.5 all-gather.2

commit v6 on v5

--- a/solution.py
+++ b/solution.py
@@ -13,9 +13,10 @@
 INVERSE_BLOCK = 656
 STRIP = 64
 VMEM_BYTES = 40 * 1024 * 1024
-LARGE_VMEM_BYTES = 50_000_000
+LARGE_VMEM_BYTES = 52_000_000
 WHOLE_VMEM_BYTES = 58_000_000
 CHUNKS = ((0, 5),)
+GATHERS = ((0, 3), (3, 5))
 
 
 def unit_circle(waves, points, count):
@@ -342,13 +343,12 @@
     )(pair_ids, trims, wavenumbers)
 
 
-def legendre_call(highest, start, band, wavenumbers, values, gathered, damping, spectrum):
-    groups, local_pairs, degrees, each = gathered.shape
+def legendre_call(highest, start, band, wavenumbers, values, gathered, damping, previous):
+    groups, count, degrees, each = gathered.shape
     cycles = groups * each
-    count = values.shape[1]
-    pair_block = pl.BlockSpec((cycles // 2, 1, 2, LANES), lambda q: (0, q, 0, 0))
+    local_pairs = values.shape[1]
     fields = LANES // 2
-    previous = [] if spectrum is None else [spectrum]
+    pair_block = pl.BlockSpec((cycles // 2, 1, 2, LANES), lambda q: (0, q + start, 0, 0))
     return pl.pallas_call(
         functools.partial(legendre_kernel, start, highest),
         grid=(count,),
@@ -356,7 +356,7 @@
             SMEM,
             SMEM,
             pair_block,
-            pl.BlockSpec((groups, 1, degrees, each), lambda q: (0, q + start, 0, 0)),
+            pl.BlockSpec((groups, 1, degrees, each), lambda q: (0, q, 0, 0)),
             pl.BlockSpec(damping.shape, lambda q: (0, 0)),
         ]
         + [pl.BlockSpec(memory_space=pl.ANY)] * len(previous),
@@ -368,7 +368,7 @@
             jax.ShapeDtypeStruct((local_pairs, fields, degrees), jnp.bfloat16),
             jax.ShapeDtypeStruct(values.shape, jnp.bfloat16),
         ],
-        input_output_aliases={5: 0} if previous else {},
+        input_output_aliases={5 + one: one for one in range(len(previous))},
         compiler_params=parameters("arbitrary", limit=LARGE_VMEM_BYTES),
         cost_estimate=pl.CostEstimate(
             flops=4 * count * cycles * LANES * degrees,
@@ -415,7 +415,9 @@
     local_pairs, local_cycles, degrees = legendre.shape
     groups = lax.axis_size("fld")
     bands = lax.axis_size("band")
-    gathered = lax.all_gather(legendre.swapaxes(1, 2), "fld")
+    gathered = [
+        lax.all_gather(legendre[start:end].swapaxes(1, 2), "fld") for start, end in GATHERS
+    ]
     points = grid[0, 0].T
     stride = 2 * local_pairs
     padding = -(-degrees // LANES) * LANES - columns
@@ -428,14 +430,12 @@
         packed, trims = lax.optimization_barrier((packed, trims))
         arrived.append(exchange(packed.reshape(groups * bands, chunk[1] - chunk[0], 2, LANES)))
     table = table_call(highest, length, stride, pair_ids, trims, wavenumbers)
-    spectrum = None
-    returned = []
-    for (start, end), message in zip(CHUNKS, arrived):
-        spectrum, rebuilt = legendre_call(
-            highest, start, band, wavenumbers, message, gathered, padded, spectrum
-        )
-        message = exchange(rebuilt)
-        returned.append(message.reshape(groups, bands * (end - start) * 2, LANES))
+    message = arrived[0]
+    previous = []
+    for (start, _), part in zip(GATHERS, gathered):
+        previous = legendre_call(highest, start, band, wavenumbers, message, part, padded, previous)
+    spectrum, rebuilt = previous
+    returned = [exchange(rebuilt).reshape(groups, bands * local_pairs * 2, LANES)]
     restored = inverse_call(length, fields, pair_ids, returned, table)
     return (
         spectrum.reshape(local_pairs, 2, fields // groups, degrees),

time: 157 us -> 167 us (1.064)
  starting transfers between devices: 34.8 us -> 38.6 us
  local copies, waits for them, and re-layouts: 2.87 us -> 6.45 us
  Pallas kernels: 31.4 us -> 33.5 us
    all_to_all x2, starting transfers between devices: 34.8 us -> 38.5 us  [exchange(): lax.all_to_all(message, ('fld', 'band'), split_axis=0, concat_axis=0, til...]
    transpose x0 -> x2, local copies, waits for them, and re-layouts: none -> 3.58 us  [on_device(): legendre[start:end].swapaxes(1, 2)]
    pallas_call x1 -> x2, Pallas kernels: 9.8 us -> 11.7 us  [legendre_call(): pl.pallas_call(functools.partial(legendre_kernel, start, highest), grid=(...]
  transfers between devices with their start and end apart: 3 -> 4, of which waited for: 2 -> 3; matrix products, arithmetic and copies ran while one was open for 0% -> 1% of each run, Pallas kernels for 10% -> 13%
where the time goes in v6:
time: 167 us; the launch traced here: 166 us
  waiting for transfers between devices  73.1 us (44%)
  starting transfers between devices  38.6 us (23%)
  Pallas kernels  33.5 us (20%)
  between operations  14.8 us (9%)
  local copies, waits for them, and re-layouts  6.45 us (4%)
    all_to_all x2, waiting for transfers between devices, exchange(): lax.all_to_all(message, ('fld', 'band'), split_axis=0, concat_axis=0, til...  72.3 us
    all_to_all x2, starting transfers between devices, exchange(): lax.all_to_all(message, ('fld', 'band'), split_axis=0, concat_axis=0, til...  38.5 us
    pallas_call x2, Pallas kernels, legendre_call(): pl.pallas_call(functools.partial(legendre_kernel, start, highest), grid=(...  11.7 us
    pallas_call x1, Pallas kernels, forward_call(): pl.pallas_call(functools.partial(forward_kernel, highest, chunk, stride),...  11.2 us
    pallas_call x1, Pallas kernels, inverse_call(): pl.pallas_call(functools.partial(inverse_kernel, len(values)), grid=(bloc...  6.31 us
    pallas_call x1, Pallas kernels, table_call(): pl.pallas_call(functools.partial(table_kernel, length, highest, stride),...  4.4 us
    transpose x2, local copies, waits for them, and re-layouts, on_device(): legendre[start:end].swapaxes(1, 2)  3.58 us
  transfers between devices with their start and end apart: 4, of which 3 were waited for; matrix products, arithmetic and copies ran while one was open for 1% of the time, Pallas kernels for 13%

profile of v6, /device:TPU:1, one launch (start us, length us, event | category | flops | bytes accessed | tf_op | source)
XLA Modules:
  0.0 166.5 jit_solution(679503654767429953)
XLA Ops:
  7.2 0.0 all-gather.7.cloned.1.call-start
  7.2 1.9 %slice_bitcast_fusion = bf16[3,641,128]{2,1,0:T(8,128)(2,1)} fusion(bf16[5,128,641]{1,2,0:T(8,128)(2,1)} %param.12), kind=kLoop, calls=%fused_computation | loop fusion | bytes 984576 | tf_op jit(solution)/shard_map/transpose | solution.py:419
  9.1 0.0 all-gather.7.cloned.1.call-update
  9.1 0.0 all-gather.5.cloned.1.call-start
  9.1 1.7 %slice_bitcast_fusion.1 = bf16[2,641,128]{2,1,0:T(8,128)(2,1)} fusion(bf16[5,128,641]{1,2,0:T(8,128)(2,1)} %param.12), kind=kLoop, calls=%fused_computation.1 | loop fusion | bytes 656384 | tf_op jit(solution)/shard_map/transpose | solution.py:419
  10.9 0.0 all-gather.5.cloned.1.call-update
  11.5 11.2 %forward_dft.1 = bf16[8,640,128]{2,1,0:T(8,128)(2,1)} custom-call(s32[1,1]{1,0:T(1,128)S(6)} %copy.13.pair_ids, s32[1,1,2]{2,1,0:T(1,128)} %trims.2, f32[1,1,2]{2,1,0:T(1,128)} %weights.1, s32[640]{0:T(1024)} %wavenumbers.7, bf16[2596,256]{1,0:T(8,128)(2,1)} %bitcast.22), custom_call_target="tpu_custom_call" | custom-call | flops 1701314560 | bytes 1329152 | tf_op jit(solution)/shard_map/forward_dft/pallas_call | solution.py:305
  22.7 0.0 copy-start.3
  22.7 0.0 copy-start.1
  22.7 22.2 %all-to-all-start = ((bf16[512,5,2,128]{3,2,1,0:T(2,128)(2,1)}), bf16[512,5,2,128]{3,2,1,0:T(2,128)(2,1)S(1)}, u32[]{:S(2)}, u32[]{:S(2)}) async-start(bf16[512,5,2,128]{3,2,1,0:T(2,128)(2,1)} %bitcast.20), calls=%async_computation | async-start | bytes 2621440 | tf_op jit(solution)/shard_map/all_to_all | solution.py:408
  44.9 0.0 copy-done.3
  45.0 39.8 %all-to-all-done.values = bf16[512,5,2,128]{3,2,1,0:T(2,128)(2,1)S(1)} async-done(((bf16[512,5,2,128]{3,2,1,0:T(2,128)(2,1)}), bf16[512,5,2,128]{3,2,1,0:T(2,128)(2,1)S(1)}, u32[]{:S(2)}, u32[]{:S(2)}) %all-to-all-start) | async-done | bytes 1310752 | tf_op jit(solution)/shard_map/all_to_all | solution.py:408
  84.8 0.0 all-gather.7.cloned.1.call-done
  84.8 0.0 copy-done.1
  84.8 6.7 %legendre_both_ways.2 = (bf16[5,64,641]{2,1,0:T(8,128)(2,1)}, bf16[512,5,2,128]{3,2,1,0:T(2,128)(2,1)}) custom-call(s32[1]{0:T(128)} %bitcast.band, s32[640]{0:T(1024)S(1)} %copy-done.1, bf16[512,5,2,128]{3,2,1,0:T(2,128)(2,1)S(1)} %all-to-all-done.values, bf16[8,3,641,128]{3,2,1,0:T(8,128)(2,1)} %bitcast.17, f32[8,768]{1,0:T(8,128)S(1)} %broadcast_in_dim.2.damping), custom_call_target="tpu_custom_call" | custom-call | flops 1008205824 | bytes 3938304 | tf_op jit(solution)/shard_map/legendre_both_ways/pallas_call | solution.py:352
  91.5 0.8 all-gather.5.cloned.1.call-done
  92.2 5.0 %legendre_both_ways.3 = (bf16[5,64,641]{2,1,0:T(8,128)(2,1)}, bf16[512,5,2,128]{3,2,1,0:T(2,128)(2,1)}) custom-call(s32[1]{0:T(128)} %bitcast.band, s32[640]{0:T(1024)S(1)} %copy-done.1, bf16[512,5,2,128]{3,2,1,0:T(2,128)(2,1)S(1)} %all-to-all-done.values, bf16[8,2,641,128]{3,2,1,0:T(8,128)(2,1)} %bitcast.18, ...), custom_call_target="tpu_custom_call", output_to_operand_aliasing={{0}: (5, {}), {1}: (6, {})} | custom-call | flops 672137216 | bytes 2625536 | tf_op jit(solution)/shard_map/legendre_both_ways/pallas_call | solution.py:352
  97.3 16.3 %all-to-all-start.1 = ((bf16[512,5,2,128]{3,2,1,0:T(2,128)(2,1)}), bf16[512,5,2,128]{3,2,1,0:T(2,128)(2,1)S(1)}, u32[]{:S(2)}, u32[]{:S(2)}) async-start(bf16[512,5,2,128]{3,2,1,0:T(2,128)(2,1)} %get-tuple-element.12), calls=%async_computation.1 | async-start | bytes 2621440 | tf_op jit(solution)/shard_map/all_to_all | solution.py:408
  113.6 0.0 copy-done.2
  113.6 4.4 %inverse_table.1.refs_1_ = bf16[2688,1280]{1,0:T(8,128)(2,1)S(1)} custom-call(s32[1,1]{1,0:T(1,128)S(6)} %copy.13.pair_ids, s32[1,1,2]{2,1,0:T(1,128)S(1)} %copy-done.2, s32[640]{0:T(1024)S(1)} %copy-done.1), custom_call_target="tpu_custom_call" | custom-call | flops 26583040 | bytes 6645760 | tf_op jit(solution)/shard_map/inverse_table/pallas_call | solution.py:331
  118.0 0.0 copy-start
  118.0 2.8 %copy-done = bf16[2688,1280]{1,0:T(8,128)(2,1)} copy-done((bf16[2688,1280]{1,0:T(8,128)(2,1)}, bf16[2688,1280]{1,0:T(8,128)(2,1)S(1)}, u32[]{:S(2)}) %copy-start) | copy-done | bytes 6881304
  120.8 32.5 %all-to-all-done.1 = bf16[512,5,2,128]{3,2,1,0:T(2,128)(2,1)S(1)} async-done(((bf16[512,5,2,128]{3,2,1,0:T(2,128)(2,1)}), bf16[512,5,2,128]{3,2,1,0:T(2,128)(2,1)S(1)}, u32[]{:S(2)}, u32[]{:S(2)}) %all-to-all-start.1) | async-done | bytes 1310752 | tf_op jit(solution)/shard_map/all_to_all | solution.py:408
  153.3 6.3 %inverse_dft.1 = bf16[2596,256]{1,0:T(8,128)(2,1)} custom-call(s32[1,1]{1,0:T(1,128)S(6)} %copy.13.pair_ids, bf16[8,640,128]{2,1,0:T(8,128)(2,1)S(1)} %bitcast.16, bf16[2688,1280]{1,0:T(8,128)(2,1)} %copy-done), custom_call_target="tpu_custom_call" | custom-call | flops 1701314560 | bytes 7974912 | tf_op jit(solution)/shard_map/inverse_dft/pallas_call | solution.py:385
  (3 shorter events, 0.0 us)
Async XLA Ops:
  7.2 77.6 %all-gather.7.cloned.1.call-start = ((), (), s32[]{:S(2)}) async-start(), calls=%async_computation.3 | async-start | bytes 4478976 | tf_op jit(solution)/shard_map/all_gather | solution.py:419
  9.1 83.2 %all-gather.5.cloned.1.call-start = ((), (), s32[]{:S(2)}) async-start(), calls=%async_computation.2 | async-start | bytes 2985984 | tf_op jit(solution)/shard_map/all_gather | solution.py:419
  22.7 22.2 %copy-start.3 = (f32[640]{0:T(1024)S(1)}, f32[640]{0:T(1024)}, u32[]{:S(2)}) copy-start(f32[640]{0:T(1024)} %param.13) | copy-start | bytes 7684
  22.7 62.1 %copy-start.1 = (s32[640]{0:T(1024)S(1)}, s32[640]{0:T(1024)}, u32[]{:S(2)}) copy-start(s32[640]{0:T(1024)} %wavenumbers.7) | copy-start | bytes 7684
  22.7 62.0 %all-to-all-start = ((bf16[512,5,2,128]{3,2,1,0:T(2,128)(2,1)}), bf16[512,5,2,128]{3,2,1,0:T(2,128)(2,1)S(1)}, u32[]{:S(2)}, u32[]{:S(2)}) async-start(bf16[512,5,2,128]{3,2,1,0:T(2,128)(2,1)} %bitcast.20), calls=%async_computation | async-start | bytes 2621440 | tf_op jit(solution)/shard_map/all_to_all | solution.py:408
  97.3 16.3 %copy-start.2 = (s32[1,1,2]{2,1,0:T(1,128)S(1)}, s32[1,1,2]{2,1,0:T(1,128)}, u32[]{:S(2)}) copy-start(s32[1,1,2]{2,1,0:T(1,128)} %trims.2) | copy-start | bytes 28
  97.3 56.0 %all-to-all-start.1 = ((bf16[512,5,2,128]{3,2,1,0:T(2,128)(2,1)}), bf16[512,5,2,128]{3,2,1,0:T(2,128)(2,1)S(1)}, u32[]{:S(2)}, u32[]{:S(2)}) async-start(bf16[512,5,2,128]{3,2,1,0:T(2,128)(2,1)} %get-tuple-element.12), calls=%async_computation.1 | async-start | bytes 2621440 | tf_op jit(solution)/shard_map/all_to_all | solution.py:408
  118.0 2.9 %copy-start = (bf16[2688,1280]{1,0:T(8,128)(2,1)}, bf16[2688,1280]{1,0:T(8,128)(2,1)S(1)}, u32[]{:S(2)}) copy-start(bf16[2688,1280]{1,0:T(8,128)(2,1)S(1)} %inverse_table.1.refs_1_) | copy-start | bytes 20643844
Sparse Core Ops, SparseCore 0:
  10.2 43.7 all-gather.6
  56.1 36.1 all-gather.4

commit v7 on v5

--- a/solution.py
+++ b/solution.py
@@ -10,7 +10,7 @@
 PI = 3.141592653589793
 LANES = 128
 STEP = 512
-INVERSE_BLOCK = 656
+INVERSE_BLOCK = 672
 STRIP = 64
 VMEM_BYTES = 40 * 1024 * 1024
 LARGE_VMEM_BYTES = 50_000_000
@@ -197,9 +197,12 @@
 def legendre_kernel(start, highest, band, wavenumbers, values, legendre, damping, *refs):
     spectrum, rebuilt = refs[-2:]
     groups, _, degrees, each = legendre.shape
-    matrix = jnp.concatenate([legendre[group, 0] for group in range(groups)], axis=1)
+
+    def matrix(start, count):
+        return jnp.concatenate([legendre[group, 0] for group in range(start, start + count)], axis=1)
+
     rows = (groups * each, LANES)
-    sums = jnp.dot(matrix, values.reshape(*rows)[...], preferred_element_type=jnp.float32).T
+    sums = jnp.dot(matrix(0, groups), values.reshape(*rows)[...], preferred_element_type=jnp.float32).T
     fields = sums.shape[0] // 2
     pair = band[0] + start + pl.program_id(0)
     first_wave = wavenumbers[2 * pair]
@@ -214,12 +217,14 @@
     filtered = (jnp.where(head, sums[:fields], sums[fields:]) * factor).astype(jnp.bfloat16)
     spectrum[0] = filtered
     nothing = jnp.zeros_like(filtered)
-    parts = jnp.concatenate([jnp.where(head, filtered, nothing), jnp.where(head, nothing, filtered)], axis=0)
-    products = jnp.dot(parts, matrix, preferred_element_type=jnp.float32)
-    row = lax.broadcasted_iota(jnp.int32, products.shape, 0)
-    wave = jnp.where(row < fields, first_wave, second_wave)
-    doubled = products * jnp.where(wave == 0, 1.0, 2.0)
-    rebuilt.reshape(*rows)[...] = doubled.astype(jnp.bfloat16).T
+    doubled = [
+        filtered * jnp.where(wave == 0, 1.0, 2.0).astype(jnp.bfloat16) for wave in (first_wave, second_wave)
+    ]
+    parts = jnp.concatenate([jnp.where(head, doubled[0], nothing), jnp.where(head, nothing, doubled[1])], axis=0)
+    leaving = rebuilt.reshape(*rows)
+    for start in range(0, groups, 2):
+        products = jnp.dot(parts, matrix(start, 2), preferred_element_type=jnp.float32)
+        leaving[start * each:(start + 2) * each, :] = products.astype(jnp.bfloat16).T
 
 
 def inverse_kernel(chunks, pair_ids, *refs):
@@ -265,27 +270,27 @@
             base += 4 * quarter
 
     arriving(block).wait()
-    start = pl.multiple_of(block * INVERSE_BLOCK, 16)
-
-    def product(cycle):
-        return jnp.dot(
-            table[pl.ds(start, INVERSE_BLOCK), :], factors[cycle], preferred_element_type=jnp.float32
-        )
-
-    end = start + INVERSE_BLOCK
-
-    @pl.when(end <= first)
-    def _():
-        restored[...] = product(0).astype(jnp.bfloat16)
-
-    @pl.when(start >= first)
-    def _():
-        restored[...] = product(1).astype(jnp.bfloat16)
-
-    @pl.when((start < first) & (end > first))
-    def _():
-        position = start + lax.broadcasted_iota(jnp.int32, restored.shape, 0)
-        restored[...] = jnp.where(position < first, product(0), product(1)).astype(jnp.bfloat16)
+    half = INVERSE_BLOCK // 2
+    for side in range(2):
+        start = pl.multiple_of(block * INVERSE_BLOCK + side * half, 16)
+        end = start + half
+        target = slice(side * half, (side + 1) * half)
+
+        def product(cycle):
+            return jnp.dot(table[pl.ds(start, half), :], factors[cycle], preferred_element_type=jnp.float32)
+
+        @pl.when(end <= first)
+        def _():
+            restored[target, :] = product(0).astype(jnp.bfloat16)
+
+        @pl.when(start >= first)
+        def _():
+            restored[target, :] = product(1).astype(jnp.bfloat16)
+
+        @pl.when((start < first) & (end > first))
+        def _():
+            position = start + lax.broadcasted_iota(jnp.int32, (half, restored.shape[1]), 0)
+            restored[target, :] = jnp.where(position < first, product(0), product(1)).astype(jnp.bfloat16)
 
 
 SMEM = pl.BlockSpec(memory_space=pltpu.SMEM)

time: 157 us -> 158 us (level)
  no operation moved by 1% of the time
where the time goes in v7:
time: 158 us; the launch traced here: 157 us
  waiting for transfers between devices  73 us (46%)
  starting transfers between devices  34.8 us (22%)
  Pallas kernels  32 us (20%)
  between operations  14.8 us (9%)
  local copies, waits for them, and re-layouts  2.87 us (2%)
    all_to_all x2, waiting for transfers between devices, exchange(): lax.all_to_all(message, ('fld', 'band'), split_axis=0, concat_axis=0, til...  72.3 us
    all_to_all x2, starting transfers between devices, exchange(): lax.all_to_all(message, ('fld', 'band'), split_axis=0, concat_axis=0, til...  34.8 us
    pallas_call x1, Pallas kernels, forward_call(): pl.pallas_call(functools.partial(forward_kernel, highest, chunk, stride),...  11.1 us
    pallas_call x1, Pallas kernels, legendre_call(): pl.pallas_call(functools.partial(legendre_kernel, start, highest), grid=(...  9.81 us
    pallas_call x1, Pallas kernels, inverse_call(): pl.pallas_call(functools.partial(inverse_kernel, len(values)), grid=(bloc...  6.78 us
    pallas_call x1, Pallas kernels, table_call(): pl.pallas_call(functools.partial(table_kernel, length, highest, stride),...  4.3 us
  transfers between devices with their start and end apart: 3, of which 2 were waited for; matrix products, arithmetic and copies ran while one was open for 0% of the time, Pallas kernels for 10%

profile of v7, /device:TPU:1, one launch (start us, length us, event | category | flops | bytes accessed | tf_op | source)
XLA Modules:
  0.0 157.4 jit_solution(8559828565414983325)
XLA Ops:
  7.2 0.0 all-gather.3.cloned.1.call-start
  7.2 0.7 all-gather.3.cloned.1.call-update
  8.5 11.1 %forward_dft.1 = bf16[8,640,128]{2,1,0:T(8,128)(2,1)} custom-call(s32[1,1]{1,0:T(1,128)S(6)} %copy.9.pair_ids, s32[1,1,2]{2,1,0:T(1,128)} %trims.2, f32[1,1,2]{2,1,0:T(1,128)} %weights.1, s32[640]{0:T(1024)} %wavenumbers.5, bf16[2596,256]{1,0:T(8,128)(2,1)} %bitcast.17), custom_call_target="tpu_custom_call" | custom-call | flops 1701314560 | bytes 1329152 | tf_op jit(solution)/shard_map/forward_dft/pallas_call | solution.py:309
  19.7 0.0 copy-start.3
  19.7 0.0 copy-start.1
  19.7 22.3 %all-to-all-start = ((bf16[512,5,2,128]{3,2,1,0:T(2,128)(2,1)}), bf16[512,5,2,128]{3,2,1,0:T(2,128)(2,1)S(1)}, u32[]{:S(2)}, u32[]{:S(2)}) async-start(bf16[512,5,2,128]{3,2,1,0:T(2,128)(2,1)} %bitcast.15), calls=%async_computation | async-start | bytes 2621440 | tf_op jit(solution)/shard_map/all_to_all | solution.py:413
  42.0 0.0 copy-done.3
  42.0 39.7 %all-to-all-done.values = bf16[512,5,2,128]{3,2,1,0:T(2,128)(2,1)S(1)} async-done(((bf16[512,5,2,128]{3,2,1,0:T(2,128)(2,1)}), bf16[512,5,2,128]{3,2,1,0:T(2,128)(2,1)S(1)}, u32[]{:S(2)}, u32[]{:S(2)}) %all-to-all-start) | async-done | bytes 1310752 | tf_op jit(solution)/shard_map/all_to_all | solution.py:413
  81.7 0.0 all-gather.3.cloned.1.call-done
  81.7 0.0 copy-done.1
  81.7 9.8 %legendre_both_ways.1 = (bf16[5,64,641]{2,1,0:T(8,128)(2,1)}, bf16[512,5,2,128]{3,2,1,0:T(2,128)(2,1)}) custom-call(s32[1]{0:T(128)} %bitcast.band, s32[640]{0:T(1024)S(1)} %copy-done.1, bf16[512,5,2,128]{3,2,1,0:T(2,128)(2,1)S(1)} %all-to-all-done.values, bf16[8,5,641,128]{3,2,1,0:T(8,128)(2,1)} %bitcast.13, f32[8,768]{1,0:T(8,128)S(1)} %broadcast_in_dim.2.damping), custom_call_target="tpu_custom_call" | custom-call | flops 1680343040 | bytes 6563840 | tf_op jit(solution)/shard_map/legendre_both_ways/pallas_call | solution.py:357
  91.5 0.0 copy-start.2
  91.5 12.5 %all-to-all-start.1 = ((bf16[512,5,2,128]{3,2,1,0:T(2,128)(2,1)}), bf16[512,5,2,128]{3,2,1,0:T(2,128)(2,1)S(1)}, u32[]{:S(2)}, u32[]{:S(2)}) async-start(bf16[512,5,2,128]{3,2,1,0:T(2,128)(2,1)} %get-tuple-element.8), calls=%async_computation.1 | async-start | bytes 2621440 | tf_op jit(solution)/shard_map/all_to_all | solution.py:413
  104.0 0.0 copy-done.2
  104.0 4.3 %inverse_table.1.refs_1_ = bf16[2688,1280]{1,0:T(8,128)(2,1)S(1)} custom-call(s32[1,1]{1,0:T(1,128)S(6)} %copy.9.pair_ids, s32[1,1,2]{2,1,0:T(1,128)S(1)} %copy-done.2, s32[640]{0:T(1024)S(1)} %copy-done.1), custom_call_target="tpu_custom_call" | custom-call | flops 26583040 | bytes 6645760 | tf_op jit(solution)/shard_map/inverse_table/pallas_call | solution.py:335
  108.4 0.0 copy-start
  108.4 2.8 %copy-done = bf16[2688,1280]{1,0:T(8,128)(2,1)} copy-done((bf16[2688,1280]{1,0:T(8,128)(2,1)}, bf16[2688,1280]{1,0:T(8,128)(2,1)S(1)}, u32[]{:S(2)}) %copy-start) | copy-done | bytes 6881304
  111.2 32.6 %all-to-all-done.1 = bf16[512,5,2,128]{3,2,1,0:T(2,128)(2,1)S(1)} async-done(((bf16[512,5,2,128]{3,2,1,0:T(2,128)(2,1)}), bf16[512,5,2,128]{3,2,1,0:T(2,128)(2,1)S(1)}, u32[]{:S(2)}, u32[]{:S(2)}) %all-to-all-start.1) | async-done | bytes 1310752 | tf_op jit(solution)/shard_map/all_to_all | solution.py:413
  143.8 6.8 %inverse_dft.1 = bf16[2596,256]{1,0:T(8,128)(2,1)} custom-call(s32[1,1]{1,0:T(1,128)S(6)} %copy.9.pair_ids, bf16[8,640,128]{2,1,0:T(8,128)(2,1)S(1)} %bitcast.12, bf16[2688,1280]{1,0:T(8,128)(2,1)} %copy-done), custom_call_target="tpu_custom_call" | custom-call | flops 1701314560 | bytes 7974912 | tf_op jit(solution)/shard_map/inverse_dft/pallas_call | solution.py:390
  (2 shorter events, 0.0 us)
Async XLA Ops:
  7.2 74.5 %all-gather.3.cloned.1.call-start = ((), (), s32[]{:S(2)}) async-start(), calls=%async_computation.2 | async-start | bytes 7464960 | tf_op jit(solution)/shard_map/all_gather | solution.py:423
  19.7 22.3 %copy-start.3 = (f32[640]{0:T(1024)S(1)}, f32[640]{0:T(1024)}, u32[]{:S(2)}) copy-start(f32[640]{0:T(1024)} %param.13) | copy-start | bytes 7684
  19.7 62.0 %copy-start.1 = (s32[640]{0:T(1024)S(1)}, s32[640]{0:T(1024)}, u32[]{:S(2)}) copy-start(s32[640]{0:T(1024)} %wavenumbers.5) | copy-start | bytes 7684
  19.7 62.0 %all-to-all-start = ((bf16[512,5,2,128]{3,2,1,0:T(2,128)(2,1)}), bf16[512,5,2,128]{3,2,1,0:T(2,128)(2,1)S(1)}, u32[]{:S(2)}, u32[]{:S(2)}) async-start(bf16[512,5,2,128]{3,2,1,0:T(2,128)(2,1)} %bitcast.15), calls=%async_computation | async-start | bytes 2621440 | tf_op jit(solution)/shard_map/all_to_all | solution.py:413
  91.5 12.5 %copy-start.2 = (s32[1,1,2]{2,1,0:T(1,128)S(1)}, s32[1,1,2]{2,1,0:T(1,128)}, u32[]{:S(2)}) copy-start(s32[1,1,2]{2,1,0:T(1,128)} %trims.2) | copy-start | bytes 28
  91.5 52.3 %all-to-all-start.1 = ((bf16[512,5,2,128]{3,2,1,0:T(2,128)(2,1)}), bf16[512,5,2,128]{3,2,1,0:T(2,128)(2,1)S(1)}, u32[]{:S(2)}, u32[]{:S(2)}) async-start(bf16[512,5,2,128]{3,2,1,0:T(2,128)(2,1)} %get-tuple-element.8), calls=%async_computation.1 | async-start | bytes 2621440 | tf_op jit(solution)/shard_map/all_to_all | solution.py:413
  108.4 2.9 %copy-start = (bf16[2688,1280]{1,0:T(8,128)(2,1)}, bf16[2688,1280]{1,0:T(8,128)(2,1)S(1)}, u32[]{:S(2)}) copy-start(bf16[2688,1280]{1,0:T(8,128)(2,1)S(1)} %inverse_table.1.refs_1_) | copy-start | bytes 20643844
Sparse Core Ops, SparseCore 0:
  10.2 66.5 all-gather.2

commit v8 on v5

--- a/solution.py
+++ b/solution.py
@@ -197,9 +197,12 @@
 def legendre_kernel(start, highest, band, wavenumbers, values, legendre, damping, *refs):
     spectrum, rebuilt = refs[-2:]
     groups, _, degrees, each = legendre.shape
-    matrix = jnp.concatenate([legendre[group, 0] for group in range(groups)], axis=1)
+
+    def matrix(start, count):
+        return jnp.concatenate([legendre[group, 0] for group in range(start, start + count)], axis=1)
+
     rows = (groups * each, LANES)
-    sums = jnp.dot(matrix, values.reshape(*rows)[...], preferred_element_type=jnp.float32).T
+    sums = jnp.dot(matrix(0, groups), values.reshape(*rows)[...], preferred_element_type=jnp.float32).T
     fields = sums.shape[0] // 2
     pair = band[0] + start + pl.program_id(0)
     first_wave = wavenumbers[2 * pair]
@@ -214,12 +217,14 @@
     filtered = (jnp.where(head, sums[:fields], sums[fields:]) * factor).astype(jnp.bfloat16)
     spectrum[0] = filtered
     nothing = jnp.zeros_like(filtered)
-    parts = jnp.concatenate([jnp.where(head, filtered, nothing), jnp.where(head, nothing, filtered)], axis=0)
-    products = jnp.dot(parts, matrix, preferred_element_type=jnp.float32)
-    row = lax.broadcasted_iota(jnp.int32, products.shape, 0)
-    wave = jnp.where(row < fields, first_wave, second_wave)
-    doubled = products * jnp.where(wave == 0, 1.0, 2.0)
-    rebuilt.reshape(*rows)[...] = doubled.astype(jnp.bfloat16).T
+    doubled = [
+        filtered * jnp.where(wave == 0, 1.0, 2.0).astype(jnp.bfloat16) for wave in (first_wave, second_wave)
+    ]
+    parts = jnp.concatenate([jnp.where(head, doubled[0], nothing), jnp.where(head, nothing, doubled[1])], axis=0)
+    leaving = rebuilt.reshape(*rows)
+    for start in range(0, groups, 2):
+        products = jnp.dot(parts, matrix(start, 2), preferred_element_type=jnp.float32)
+        leaving[start * each:(start + 2) * each, :] = products.astype(jnp.bfloat16).T
 
 
 def inverse_kernel(chunks, pair_ids, *refs):

time: 157 us -> 157 us (level)
  no operation moved by 1% of the time
where the time goes in v8:
time: 157 us
  waiting for transfers between devices  72.8 us (46%)
  starting transfers between devices  34.7 us (22%)
  Pallas kernels  31.9 us (20%)
  between operations  14.8 us (9%)
  local copies, waits for them, and re-layouts  2.87 us (2%)
    all_to_all x2, waiting for transfers between devices, exchange(): lax.all_to_all(message, ('fld', 'band'), split_axis=0, concat_axis=0, til...  72.1 us
    all_to_all x2, starting transfers between devices, exchange(): lax.all_to_all(message, ('fld', 'band'), split_axis=0, concat_axis=0, til...  34.6 us
    pallas_call x1, Pallas kernels, forward_call(): pl.pallas_call(functools.partial(forward_kernel, highest, chunk, stride),...  11.2 us
    pallas_call x1, Pallas kernels, legendre_call(): pl.pallas_call(functools.partial(legendre_kernel, start, highest), grid=(...  9.81 us
    pallas_call x1, Pallas kernels, inverse_call(): pl.pallas_call(functools.partial(inverse_kernel, len(values)), grid=(bloc...  6.31 us
    pallas_call x1, Pallas kernels, table_call(): pl.pallas_call(functools.partial(table_kernel, length, highest, stride),...  4.49 us
  transfers between devices with their start and end apart: 3, of which 2 were waited for; matrix products, arithmetic and copies ran while one was open for 0% of the time, Pallas kernels for 10%

profile of v8, /device:TPU:1, one launch (start us, length us, event | category | flops | bytes accessed | tf_op | source)
XLA Modules:
  0.0 156.9 jit_solution(663494218320975361)
XLA Ops:
  7.2 0.0 all-gather.3.cloned.1.call-start
  7.2 0.7 all-gather.3.cloned.1.call-update
  8.5 11.2 %forward_dft.1 = bf16[8,640,128]{2,1,0:T(8,128)(2,1)} custom-call(s32[1,1]{1,0:T(1,128)S(6)} %copy.9.pair_ids, s32[1,1,2]{2,1,0:T(1,128)} %trims.2, f32[1,1,2]{2,1,0:T(1,128)} %weights.1, s32[640]{0:T(1024)} %wavenumbers.5, bf16[2596,256]{1,0:T(8,128)(2,1)} %bitcast.17), custom_call_target="tpu_custom_call" | custom-call | flops 1701314560 | bytes 1329152 | tf_op jit(solution)/shard_map/forward_dft/pallas_call | solution.py:309
  19.8 0.0 copy-start.3
  19.8 0.0 copy-start.1
  19.8 22.1 %all-to-all-start = ((bf16[512,5,2,128]{3,2,1,0:T(2,128)(2,1)}), bf16[512,5,2,128]{3,2,1,0:T(2,128)(2,1)S(1)}, u32[]{:S(2)}, u32[]{:S(2)}) async-start(bf16[512,5,2,128]{3,2,1,0:T(2,128)(2,1)} %bitcast.15), calls=%async_computation | async-start | bytes 2621440 | tf_op jit(solution)/shard_map/all_to_all | solution.py:413
  42.0 0.0 copy-done.3
  42.0 39.7 %all-to-all-done.values = bf16[512,5,2,128]{3,2,1,0:T(2,128)(2,1)S(1)} async-done(((bf16[512,5,2,128]{3,2,1,0:T(2,128)(2,1)}), bf16[512,5,2,128]{3,2,1,0:T(2,128)(2,1)S(1)}, u32[]{:S(2)}, u32[]{:S(2)}) %all-to-all-start) | async-done | bytes 1310752 | tf_op jit(solution)/shard_map/all_to_all | solution.py:413
  81.7 0.0 all-gather.3.cloned.1.call-done
  81.7 0.0 copy-done.1
  81.7 9.8 %legendre_both_ways.1 = (bf16[5,64,641]{2,1,0:T(8,128)(2,1)}, bf16[512,5,2,128]{3,2,1,0:T(2,128)(2,1)}) custom-call(s32[1]{0:T(128)} %bitcast.band, s32[640]{0:T(1024)S(1)} %copy-done.1, bf16[512,5,2,128]{3,2,1,0:T(2,128)(2,1)S(1)} %all-to-all-done.values, bf16[8,5,641,128]{3,2,1,0:T(8,128)(2,1)} %bitcast.13, f32[8,768]{1,0:T(8,128)S(1)} %broadcast_in_dim.2.damping), custom_call_target="tpu_custom_call" | custom-call | flops 1680343040 | bytes 6563840 | tf_op jit(solution)/shard_map/legendre_both_ways/pallas_call | solution.py:357
  91.5 0.0 copy-start.2
  91.5 12.5 %all-to-all-start.1 = ((bf16[512,5,2,128]{3,2,1,0:T(2,128)(2,1)}), bf16[512,5,2,128]{3,2,1,0:T(2,128)(2,1)S(1)}, u32[]{:S(2)}, u32[]{:S(2)}) async-start(bf16[512,5,2,128]{3,2,1,0:T(2,128)(2,1)} %get-tuple-element.8), calls=%async_computation.1 | async-start | bytes 2621440 | tf_op jit(solution)/shard_map/all_to_all | solution.py:413
  104.0 0.0 copy-done.2
  104.0 4.5 %inverse_table.1.refs_1_ = bf16[2688,1280]{1,0:T(8,128)(2,1)S(1)} custom-call(s32[1,1]{1,0:T(1,128)S(6)} %copy.9.pair_ids, s32[1,1,2]{2,1,0:T(1,128)S(1)} %copy-done.2, s32[640]{0:T(1024)S(1)} %copy-done.1), custom_call_target="tpu_custom_call" | custom-call | flops 26583040 | bytes 6645760 | tf_op jit(solution)/shard_map/inverse_table/pallas_call | solution.py:335
  108.5 0.0 copy-start
  108.6 2.8 %copy-done = bf16[2688,1280]{1,0:T(8,128)(2,1)} copy-done((bf16[2688,1280]{1,0:T(8,128)(2,1)}, bf16[2688,1280]{1,0:T(8,128)(2,1)S(1)}, u32[]{:S(2)}) %copy-start) | copy-done | bytes 6881304
  111.4 32.4 %all-to-all-done.1 = bf16[512,5,2,128]{3,2,1,0:T(2,128)(2,1)S(1)} async-done(((bf16[512,5,2,128]{3,2,1,0:T(2,128)(2,1)}), bf16[512,5,2,128]{3,2,1,0:T(2,128)(2,1)S(1)}, u32[]{:S(2)}, u32[]{:S(2)}) %all-to-all-start.1) | async-done | bytes 1310752 | tf_op jit(solution)/shard_map/all_to_all | solution.py:413
  143.8 6.3 %inverse_dft.1 = bf16[2596,256]{1,0:T(8,128)(2,1)} custom-call(s32[1,1]{1,0:T(1,128)S(6)} %copy.9.pair_ids, bf16[8,640,128]{2,1,0:T(8,128)(2,1)S(1)} %bitcast.12, bf16[2688,1280]{1,0:T(8,128)(2,1)} %copy-done), custom_call_target="tpu_custom_call" | custom-call | flops 1701314560 | bytes 7974912 | tf_op jit(solution)/shard_map/inverse_dft/pallas_call | solution.py:390
  (2 shorter events, 0.0 us)
Async XLA Ops:
  7.2 74.6 %all-gather.3.cloned.1.call-start = ((), (), s32[]{:S(2)}) async-start(), calls=%async_computation.2 | async-start | bytes 7464960 | tf_op jit(solution)/shard_map/all_gather | solution.py:423
  19.8 22.2 %copy-start.3 = (f32[640]{0:T(1024)S(1)}, f32[640]{0:T(1024)}, u32[]{:S(2)}) copy-start(f32[640]{0:T(1024)} %param.13) | copy-start | bytes 7684
  19.8 61.9 %copy-start.1 = (s32[640]{0:T(1024)S(1)}, s32[640]{0:T(1024)}, u32[]{:S(2)}) copy-start(s32[640]{0:T(1024)} %wavenumbers.5) | copy-start | bytes 7684
  19.8 61.9 %all-to-all-start = ((bf16[512,5,2,128]{3,2,1,0:T(2,128)(2,1)}), bf16[512,5,2,128]{3,2,1,0:T(2,128)(2,1)S(1)}, u32[]{:S(2)}, u32[]{:S(2)}) async-start(bf16[512,5,2,128]{3,2,1,0:T(2,128)(2,1)} %bitcast.15), calls=%async_computation | async-start | bytes 2621440 | tf_op jit(solution)/shard_map/all_to_all | solution.py:413
  91.5 12.5 %copy-start.2 = (s32[1,1,2]{2,1,0:T(1,128)S(1)}, s32[1,1,2]{2,1,0:T(1,128)}, u32[]{:S(2)}) copy-start(s32[1,1,2]{2,1,0:T(1,128)} %trims.2) | copy-start | bytes 28
  91.5 52.2 %all-to-all-start.1 = ((bf16[512,5,2,128]{3,2,1,0:T(2,128)(2,1)}), bf16[512,5,2,128]{3,2,1,0:T(2,128)(2,1)S(1)}, u32[]{:S(2)}, u32[]{:S(2)}) async-start(bf16[512,5,2,128]{3,2,1,0:T(2,128)(2,1)} %get-tuple-element.8), calls=%async_computation.1 | async-start | bytes 2621440 | tf_op jit(solution)/shard_map/all_to_all | solution.py:413
  108.5 2.9 %copy-start = (bf16[2688,1280]{1,0:T(8,128)(2,1)}, bf16[2688,1280]{1,0:T(8,128)(2,1)S(1)}, u32[]{:S(2)}) copy-start(bf16[2688,1280]{1,0:T(8,128)(2,1)S(1)} %inverse_table.1.refs_1_) | copy-start | bytes 20643844
Sparse Core Ops, SparseCore 0:
  10.2 66.5 all-gather.2

commit v9 on v8

--- a/solution.py
+++ b/solution.py
@@ -202,7 +202,7 @@
         return jnp.concatenate([legendre[group, 0] for group in range(start, start + count)], axis=1)
 
     rows = (groups * each, LANES)
-    sums = jnp.dot(matrix(0, groups), values.reshape(*rows)[...], preferred_element_type=jnp.float32).T
+    sums = jnp.dot(matrix(0, groups), values[0], preferred_element_type=jnp.float32).T
     fields = sums.shape[0] // 2
     pair = band[0] + start + pl.program_id(0)
     first_wave = wavenumbers[2 * pair]
@@ -349,8 +349,7 @@
 
 def legendre_call(highest, start, band, wavenumbers, values, gathered, damping, spectrum):
     groups, local_pairs, degrees, each = gathered.shape
-    cycles = groups * each
-    count = values.shape[1]
+    count, cycles, _ = values.shape
     pair_block = pl.BlockSpec((cycles // 2, 1, 2, LANES), lambda q: (0, q, 0, 0))
     fields = LANES // 2
     previous = [] if spectrum is None else [spectrum]
@@ -360,7 +359,7 @@
         in_specs=[
             SMEM,
             SMEM,
-            pair_block,
+            pl.BlockSpec((1, cycles, LANES), lambda q: (q, 0, 0)),
             pl.BlockSpec((groups, 1, degrees, each), lambda q: (0, q + start, 0, 0)),
             pl.BlockSpec(damping.shape, lambda q: (0, 0)),
         ]
@@ -371,7 +370,7 @@
         ],
         out_shape=[
             jax.ShapeDtypeStruct((local_pairs, fields, degrees), jnp.bfloat16),
-            jax.ShapeDtypeStruct(values.shape, jnp.bfloat16),
+            jax.ShapeDtypeStruct((cycles // 2, count, 2, LANES), jnp.bfloat16),
         ],
         input_output_aliases={5: 0} if previous else {},
         compiler_params=parameters("arbitrary", limit=LARGE_VMEM_BYTES),
@@ -436,8 +435,9 @@
     spectrum = None
     returned = []
     for (start, end), message in zip(CHUNKS, arrived):
+        values = message.transpose(1, 0, 2, 3).reshape(end - start, groups * local_cycles, LANES)
         spectrum, rebuilt = legendre_call(
-            highest, start, band, wavenumbers, message, gathered, padded, spectrum
+            highest, start, band, wavenumbers, values, gathered, padded, spectrum
         )
         message = exchange(rebuilt)
         returned.append(message.reshape(groups, bands * (end - start) * 2, LANES))

time: 157 us -> 157 us (level)
  transfers between devices with their start and end apart: 3 -> 3, of which waited for: 2 -> 2; matrix products, arithmetic and copies ran while one was open for 0% -> 1% of each run, Pallas kernels for 10% -> 10%
where the time goes in v9:
time: 157 us; the launch traced here: 156 us
  waiting for transfers between devices  73.1 us (47%)
  starting transfers between devices  34 us (22%)
  Pallas kernels  30.6 us (19%)
  between operations  14.8 us (9%)
  local copies, waits for them, and re-layouts  3.77 us (2%)
    all_to_all x2, waiting for transfers between devices, exchange(): lax.all_to_all(message, ('fld', 'band'), split_axis=0, concat_axis=0, til...  72.4 us
    all_to_all x2, starting transfers between devices, exchange(): lax.all_to_all(message, ('fld', 'band'), split_axis=0, concat_axis=0, til...  33.9 us
    pallas_call x1, Pallas kernels, forward_call(): pl.pallas_call(functools.partial(forward_kernel, highest, chunk, stride),...  11 us
    pallas_call x1, Pallas kernels, legendre_call(): pl.pallas_call(functools.partial(legendre_kernel, start, highest), grid=(...  9.08 us
    pallas_call x1, Pallas kernels, inverse_call(): pl.pallas_call(functools.partial(inverse_kernel, len(values)), grid=(bloc...  6.3 us
    pallas_call x1, Pallas kernels, table_call(): pl.pallas_call(functools.partial(table_kernel, length, highest, stride),...  4.18 us
  transfers between devices with their start and end apart: 3, of which 2 were waited for; matrix products, arithmetic and copies ran while one was open for 1% of the time, Pallas kernels for 10%

profile of v9, /device:TPU:1, one launch (start us, length us, event | category | flops | bytes accessed | tf_op | source)
XLA Modules:
  0.0 156.2 jit_solution(13941089370998179924)
XLA Ops:
  7.2 0.0 all-gather.3.cloned.1.call-start
  7.2 0.7 all-gather.3.cloned.1.call-update
  8.5 11.0 %forward_dft.1 = bf16[8,640,128]{2,1,0:T(8,128)(2,1)} custom-call(s32[1,1]{1,0:T(1,128)S(6)} %copy.11.pair_ids, s32[1,1,2]{2,1,0:T(1,128)} %trims.2, f32[1,1,2]{2,1,0:T(1,128)} %weights.1, s32[640]{0:T(1024)} %wavenumbers.5, bf16[2596,256]{1,0:T(8,128)(2,1)} %bitcast.21), custom_call_target="tpu_custom_call" | custom-call | flops 1701314560 | bytes 1329152 | tf_op jit(solution)/shard_map/forward_dft/pallas_call | solution.py:309
  19.6 0.0 copy-start.3
  19.6 22.3 %all-to-all-start = ((bf16[512,5,2,128]{3,2,1,0:T(2,128)(2,1)}), bf16[512,5,2,128]{3,2,1,0:T(2,128)(2,1)S(1)}, u32[]{:S(2)}, u32[]{:S(2)}) async-start(bf16[512,5,2,128]{3,2,1,0:T(2,128)(2,1)} %bitcast.19), calls=%async_computation | async-start | bytes 2621440 | tf_op jit(solution)/shard_map/all_to_all | solution.py:412
  41.9 0.0 copy-done.3
  42.0 39.7 %all-to-all-done = bf16[512,5,2,128]{3,2,1,0:T(2,128)(2,1)S(1)} async-done(((bf16[512,5,2,128]{3,2,1,0:T(2,128)(2,1)}), bf16[512,5,2,128]{3,2,1,0:T(2,128)(2,1)S(1)}, u32[]{:S(2)}, u32[]{:S(2)}) %all-to-all-start) | async-done | bytes 1310752 | tf_op jit(solution)/shard_map/all_to_all | solution.py:412
  81.7 0.0 copy-start.1
  81.7 0.9 copy.10
  82.6 0.0 all-gather.3.cloned.1.call-done
  82.6 0.0 copy-done.1
  82.6 9.1 %legendre_both_ways.1 = (bf16[5,64,641]{2,1,0:T(8,128)(2,1)}, bf16[512,5,2,128]{3,2,1,0:T(2,128)(2,1)}) custom-call(s32[1]{0:T(128)} %bitcast.band, s32[640]{0:T(1024)S(1)} %copy-done.1, bf16[5,1024,128]{2,1,0:T(8,128)(2,1)S(1)} %bitcast.15, bf16[8,5,641,128]{3,2,1,0:T(8,128)(2,1)} %bitcast.16, f32[8,768]{1,0:T(8,128)S(1)} %broadcast_in_dim.2.damping), custom_call_target="tpu_custom_call" | custom-call | flops 1680343040 | bytes 6563840 | tf_op jit(solution)/shard_map/legendre_both_ways/pallas_call | solution.py:356
  91.7 0.0 copy-start.2
  91.7 11.6 %all-to-all-start.1 = ((bf16[512,5,2,128]{3,2,1,0:T(2,128)(2,1)}), bf16[512,5,2,128]{3,2,1,0:T(2,128)(2,1)S(1)}, u32[]{:S(2)}, u32[]{:S(2)}) async-start(bf16[512,5,2,128]{3,2,1,0:T(2,128)(2,1)} %get-tuple-element.8), calls=%async_computation.1 | async-start | bytes 2621440 | tf_op jit(solution)/shard_map/all_to_all | solution.py:412
  103.3 0.0 copy-done.2
  103.3 4.2 %inverse_table.1.refs_1_ = bf16[2688,1280]{1,0:T(8,128)(2,1)S(1)} custom-call(s32[1,1]{1,0:T(1,128)S(6)} %copy.11.pair_ids, s32[1,1,2]{2,1,0:T(1,128)S(1)} %copy-done.2, s32[640]{0:T(1024)S(1)} %copy-done.1), custom_call_target="tpu_custom_call" | custom-call | flops 26583040 | bytes 6645760 | tf_op jit(solution)/shard_map/inverse_table/pallas_call | solution.py:335
  107.5 0.0 copy-start
  107.5 2.8 %copy-done = bf16[2688,1280]{1,0:T(8,128)(2,1)} copy-done((bf16[2688,1280]{1,0:T(8,128)(2,1)}, bf16[2688,1280]{1,0:T(8,128)(2,1)S(1)}, u32[]{:S(2)}) %copy-start) | copy-done | bytes 6881304
  110.4 32.7 %all-to-all-done.1 = bf16[512,5,2,128]{3,2,1,0:T(2,128)(2,1)S(1)} async-done(((bf16[512,5,2,128]{3,2,1,0:T(2,128)(2,1)}), bf16[512,5,2,128]{3,2,1,0:T(2,128)(2,1)S(1)}, u32[]{:S(2)}, u32[]{:S(2)}) %all-to-all-start.1) | async-done | bytes 1310752 | tf_op jit(solution)/shard_map/all_to_all | solution.py:412
  143.0 6.3 %inverse_dft.1 = bf16[2596,256]{1,0:T(8,128)(2,1)} custom-call(s32[1,1]{1,0:T(1,128)S(6)} %copy.11.pair_ids, bf16[8,640,128]{2,1,0:T(8,128)(2,1)S(1)} %bitcast.14, bf16[2688,1280]{1,0:T(8,128)(2,1)} %copy-done), custom_call_target="tpu_custom_call" | custom-call | flops 1701314560 | bytes 7974912 | tf_op jit(solution)/shard_map/inverse_dft/pallas_call | solution.py:389
  (2 shorter events, 0.0 us)
Async XLA Ops:
  7.2 75.4 %all-gather.3.cloned.1.call-start = ((), (), s32[]{:S(2)}) async-start(), calls=%async_computation.2 | async-start | bytes 7464960 | tf_op jit(solution)/shard_map/all_gather | solution.py:422
  19.6 22.4 %copy-start.3 = (f32[640]{0:T(1024)S(1)}, f32[640]{0:T(1024)}, u32[]{:S(2)}) copy-start(f32[640]{0:T(1024)} %param.13) | copy-start | bytes 7684
  19.6 62.1 %all-to-all-start = ((bf16[512,5,2,128]{3,2,1,0:T(2,128)(2,1)}), bf16[512,5,2,128]{3,2,1,0:T(2,128)(2,1)S(1)}, u32[]{:S(2)}, u32[]{:S(2)}) async-start(bf16[512,5,2,128]{3,2,1,0:T(2,128)(2,1)} %bitcast.19), calls=%async_computation | async-start | bytes 2621440 | tf_op jit(solution)/shard_map/all_to_all | solution.py:412
  81.7 0.9 copy-start.1
  91.7 11.6 %copy-start.2 = (s32[1,1,2]{2,1,0:T(1,128)S(1)}, s32[1,1,2]{2,1,0:T(1,128)}, u32[]{:S(2)}) copy-start(s32[1,1,2]{2,1,0:T(1,128)} %trims.2) | copy-start | bytes 28
  91.7 51.3 %all-to-all-start.1 = ((bf16[512,5,2,128]{3,2,1,0:T(2,128)(2,1)}), bf16[512,5,2,128]{3,2,1,0:T(2,128)(2,1)S(1)}, u32[]{:S(2)}, u32[]{:S(2)}) async-start(bf16[512,5,2,128]{3,2,1,0:T(2,128)(2,1)} %get-tuple-element.8), calls=%async_computation.1 | async-start | bytes 2621440 | tf_op jit(solution)/shard_map/all_to_all | solution.py:412
  107.5 2.9 %copy-start = (bf16[2688,1280]{1,0:T(8,128)(2,1)}, bf16[2688,1280]{1,0:T(8,128)(2,1)S(1)}, u32[]{:S(2)}) copy-start(bf16[2688,1280]{1,0:T(8,128)(2,1)S(1)} %inverse_table.1.refs_1_) | copy-start | bytes 20643844
Sparse Core Ops, SparseCore 0:
  10.2 66.5 all-gather.2

commit v10 on v9

--- a/solution.py
+++ b/solution.py
@@ -229,7 +229,7 @@
 
 def inverse_kernel(chunks, pair_ids, *refs):
     values = refs[:chunks]
-    table_hbm, restored, table, rows, factors, sems = refs[chunks:]
+    table_hbm, restored, table, messages, rows, factors, sems, message_sems = refs[chunks:]
     block = pl.program_id(0)
     first = 20 + 4 * pair_ids[0, 0]
     share = LANES // 4
@@ -240,15 +240,23 @@
 
     @pl.when(block == 0)
     def _():
-        for one in range(sems.shape[0]):
-            arriving(one).start()
         base = 0
         for chunk in values:
             groups, height, _ = chunk.shape
             quarter = height // 2
+            copies = [
+                pltpu.make_async_copy(chunk.at[group], messages.at[group], message_sems.at[group])
+                for group in range(groups)
+            ]
+            for copy in copies:
+                copy.start()
+            if base == 0:
+                for one in range(sems.shape[0]):
+                    arriving(one).start()
             for side in range(groups // 4):
                 for near in range(4):
-                    rows[near, :height] = chunk[4 * side + near].astype(jnp.float32)
+                    copies[4 * side + near].wait()
+                    rows[near, :height] = messages[4 * side + near].astype(jnp.float32)
                 for cycle in range(2):
                     turned = [
                         jnp.concatenate(
@@ -390,15 +398,17 @@
         functools.partial(inverse_kernel, len(values)),
         grid=(blocks,),
         in_specs=[SMEM]
-        + [pl.BlockSpec(one.shape, lambda i: (0, 0, 0)) for one in values]
+        + [pl.BlockSpec(memory_space=pl.ANY)] * len(values)
         + [pl.BlockSpec(memory_space=pl.ANY)],
         out_specs=pl.BlockSpec((INVERSE_BLOCK, fields), lambda i: (i, 0)),
         out_shape=jax.ShapeDtypeStruct((length, fields), jnp.bfloat16),
         scratch_shapes=[
             pltpu.VMEM((blocks * INVERSE_BLOCK, total), jnp.bfloat16),
+            pltpu.VMEM(values[0].shape, jnp.bfloat16),
             pltpu.VMEM((4, max(one.shape[1] for one in values), LANES), jnp.float32),
             pltpu.VMEM((2, total, fields), jnp.bfloat16),
             pltpu.SemaphoreType.DMA((blocks,)),
+            pltpu.SemaphoreType.DMA((values[0].shape[0],)),
         ],
         compiler_params=parameters("arbitrary", limit=LARGE_VMEM_BYTES),
         cost_estimate=pl.CostEstimate(

time: 157 us -> 157 us (level)
  no operation moved by 1% of the time
where the time goes in v10:
time: 157 us
  waiting for transfers between devices  73 us (46%)
  starting transfers between devices  33.9 us (22%)
  Pallas kernels  31.4 us (20%)
  between operations  14.8 us (9%)
  local copies, waits for them, and re-layouts  3.77 us (2%)
    all_to_all x2, waiting for transfers between devices, exchange(): lax.all_to_all(message, ('fld', 'band'), split_axis=0, concat_axis=0, til...  72.3 us
    all_to_all x2, starting transfers between devices, exchange(): lax.all_to_all(message, ('fld', 'band'), split_axis=0, concat_axis=0, til...  33.8 us
    pallas_call x1, Pallas kernels, forward_call(): pl.pallas_call(functools.partial(forward_kernel, highest, chunk, stride),...  11.1 us
    pallas_call x1, Pallas kernels, legendre_call(): pl.pallas_call(functools.partial(legendre_kernel, start, highest), grid=(...  9.08 us
    pallas_call x1, Pallas kernels, inverse_call(): pl.pallas_call(functools.partial(inverse_kernel, len(values)), grid=(bloc...  6.96 us
    pallas_call x1, Pallas kernels, table_call(): pl.pallas_call(functools.partial(table_kernel, length, highest, stride),...  4.3 us
  transfers between devices with their start and end apart: 3, of which 2 were waited for; matrix products, arithmetic and copies ran while one was open for 1% of the time, Pallas kernels for 10%

profile of v10, /device:TPU:1, one launch (start us, length us, event | category | flops | bytes accessed | tf_op | source)
XLA Modules:
  0.0 156.9 jit_solution(14816646108561185967)
XLA Ops:
  7.2 0.0 all-gather.3.cloned.1.call-start
  7.2 0.7 all-gather.3.cloned.1.call-update
  8.5 11.1 %forward_dft.1 = bf16[8,640,128]{2,1,0:T(8,128)(2,1)} custom-call(s32[1,1]{1,0:T(1,128)S(6)} %copy.11.pair_ids, s32[1,1,2]{2,1,0:T(1,128)} %trims.2, f32[1,1,2]{2,1,0:T(1,128)} %weights.1, s32[640]{0:T(1024)} %wavenumbers.5, bf16[2596,256]{1,0:T(8,128)(2,1)} %bitcast.21), custom_call_target="tpu_custom_call" | custom-call | flops 1701314560 | bytes 1329152 | tf_op jit(solution)/shard_map/forward_dft/pallas_call | solution.py:317
  19.7 0.0 copy-start.3
  19.7 22.3 %all-to-all-start = ((bf16[512,5,2,128]{3,2,1,0:T(2,128)(2,1)}), bf16[512,5,2,128]{3,2,1,0:T(2,128)(2,1)S(1)}, u32[]{:S(2)}, u32[]{:S(2)}) async-start(bf16[512,5,2,128]{3,2,1,0:T(2,128)(2,1)} %bitcast.19), calls=%async_computation | async-start | bytes 2621440 | tf_op jit(solution)/shard_map/all_to_all | solution.py:422
  42.0 0.0 copy-done.3
  42.0 39.7 %all-to-all-done = bf16[512,5,2,128]{3,2,1,0:T(2,128)(2,1)S(1)} async-done(((bf16[512,5,2,128]{3,2,1,0:T(2,128)(2,1)}), bf16[512,5,2,128]{3,2,1,0:T(2,128)(2,1)S(1)}, u32[]{:S(2)}, u32[]{:S(2)}) %all-to-all-start) | async-done | bytes 1310752 | tf_op jit(solution)/shard_map/all_to_all | solution.py:422
  81.7 0.0 copy-start.1
  81.7 0.9 copy.10
  82.6 0.0 all-gather.3.cloned.1.call-done
  82.6 0.0 copy-done.1
  82.6 9.1 %legendre_both_ways.1 = (bf16[5,64,641]{2,1,0:T(8,128)(2,1)}, bf16[512,5,2,128]{3,2,1,0:T(2,128)(2,1)}) custom-call(s32[1]{0:T(128)} %bitcast.band, s32[640]{0:T(1024)S(1)} %copy-done.1, bf16[5,1024,128]{2,1,0:T(8,128)(2,1)S(1)} %bitcast.15, bf16[8,5,641,128]{3,2,1,0:T(8,128)(2,1)} %bitcast.16, f32[8,768]{1,0:T(8,128)S(1)} %broadcast_in_dim.2.damping), custom_call_target="tpu_custom_call" | custom-call | flops 1680343040 | bytes 6563840 | tf_op jit(solution)/shard_map/legendre_both_ways/pallas_call | solution.py:364
  91.7 0.0 copy-start.2
  91.7 11.6 %all-to-all-start.1 = ((bf16[512,5,2,128]{3,2,1,0:T(2,128)(2,1)}), bf16[512,5,2,128]{3,2,1,0:T(2,128)(2,1)S(1)}, u32[]{:S(2)}, u32[]{:S(2)}) async-start(bf16[512,5,2,128]{3,2,1,0:T(2,128)(2,1)} %get-tuple-element.8), calls=%async_computation.1 | async-start | bytes 2621440 | tf_op jit(solution)/shard_map/all_to_all | solution.py:422
  103.3 0.0 copy-done.2
  103.3 4.3 %inverse_table.1.refs_1_ = bf16[2688,1280]{1,0:T(8,128)(2,1)S(1)} custom-call(s32[1,1]{1,0:T(1,128)S(6)} %copy.11.pair_ids, s32[1,1,2]{2,1,0:T(1,128)S(1)} %copy-done.2, s32[640]{0:T(1024)S(1)} %copy-done.1), custom_call_target="tpu_custom_call" | custom-call | flops 26583040 | bytes 6645760 | tf_op jit(solution)/shard_map/inverse_table/pallas_call | solution.py:343
  107.6 0.0 copy-start
  107.6 2.8 %copy-done = bf16[2688,1280]{1,0:T(8,128)(2,1)} copy-done((bf16[2688,1280]{1,0:T(8,128)(2,1)}, bf16[2688,1280]{1,0:T(8,128)(2,1)S(1)}, u32[]{:S(2)}) %copy-start) | copy-done | bytes 6881304
  110.5 32.6 %all-to-all-done.1 = bf16[512,5,2,128]{3,2,1,0:T(2,128)(2,1)S(1)} async-done(((bf16[512,5,2,128]{3,2,1,0:T(2,128)(2,1)}), bf16[512,5,2,128]{3,2,1,0:T(2,128)(2,1)S(1)}, u32[]{:S(2)}, u32[]{:S(2)}) %all-to-all-start.1) | async-done | bytes 1310752 | tf_op jit(solution)/shard_map/all_to_all | solution.py:422
  143.0 7.0 %inverse_dft.1 = bf16[2596,256]{1,0:T(8,128)(2,1)} custom-call(s32[1,1]{1,0:T(1,128)S(6)} %copy.11.pair_ids, bf16[8,640,128]{2,1,0:T(8,128)(2,1)S(1)} %bitcast.14, bf16[2688,1280]{1,0:T(8,128)(2,1)} %copy-done), custom_call_target="tpu_custom_call" | custom-call | flops 1701314560 | bytes 7974912 | tf_op jit(solution)/shard_map/inverse_dft/pallas_call | solution.py:397
  (2 shorter events, 0.0 us)
Async XLA Ops:
  7.2 75.5 %all-gather.3.cloned.1.call-start = ((), (), s32[]{:S(2)}) async-start(), calls=%async_computation.2 | async-start | bytes 7464960 | tf_op jit(solution)/shard_map/all_gather | solution.py:432
  19.7 22.3 %copy-start.3 = (f32[640]{0:T(1024)S(1)}, f32[640]{0:T(1024)}, u32[]{:S(2)}) copy-start(f32[640]{0:T(1024)} %param.13) | copy-start | bytes 7684
  19.7 62.0 %all-to-all-start = ((bf16[512,5,2,128]{3,2,1,0:T(2,128)(2,1)}), bf16[512,5,2,128]{3,2,1,0:T(2,128)(2,1)S(1)}, u32[]{:S(2)}, u32[]{:S(2)}) async-start(bf16[512,5,2,128]{3,2,1,0:T(2,128)(2,1)} %bitcast.19), calls=%async_computation | async-start | bytes 2621440 | tf_op jit(solution)/shard_map/all_to_all | solution.py:422
  81.7 0.9 copy-start.1
  91.7 11.6 %copy-start.2 = (s32[1,1,2]{2,1,0:T(1,128)S(1)}, s32[1,1,2]{2,1,0:T(1,128)}, u32[]{:S(2)}) copy-start(s32[1,1,2]{2,1,0:T(1,128)} %trims.2) | copy-start | bytes 28
  91.7 51.3 %all-to-all-start.1 = ((bf16[512,5,2,128]{3,2,1,0:T(2,128)(2,1)}), bf16[512,5,2,128]{3,2,1,0:T(2,128)(2,1)S(1)}, u32[]{:S(2)}, u32[]{:S(2)}) async-start(bf16[512,5,2,128]{3,2,1,0:T(2,128)(2,1)} %get-tuple-element.8), calls=%async_computation.1 | async-start | bytes 2621440 | tf_op jit(solution)/shard_map/all_to_all | solution.py:422
  107.6 2.9 %copy-start = (bf16[2688,1280]{1,0:T(8,128)(2,1)}, bf16[2688,1280]{1,0:T(8,128)(2,1)S(1)}, u32[]{:S(2)}) copy-start(bf16[2688,1280]{1,0:T(8,128)(2,1)S(1)} %inverse_table.1.refs_1_) | copy-start | bytes 20643844
Sparse Core Ops, SparseCore 0:
  10.2 66.5 all-gather.2
